TPU v7x, 256 devices: a whole 4x4x8 slice. The times are simulated.
256 devices in a mesh: cam: 4 (over y_hi, core), frame: 64 (over y_lo, z, x).
Axes of the slice: x: 4, y: 4 (y_hi: 2, y_lo: 2; y = y_hi * 2 + y_lo), z: 8, core: 2. Of those that a mesh axis runs over, the one named last changes fastest.
Arguments:
- tokens: bfloat16 [8, 64, 256, 1152], P('cam', 'frame'), may hold values from -6 to 6
- counts: int32 [8, 64], P('cam', 'frame'), may hold values from 1 to 4, as said below
- neighbours: int32 [8, 2], P('cam'), may hold values from 0 to 7, as said below
- side_keys: bfloat16 [2, 576], replicated, may hold values from -5 to 5
- cross_qkv: bfloat16 [1152, 1728], replicated, may hold values from -2 to 2
- cross_out: bfloat16 [576, 1152], replicated, may hold values from -0.25 to 0.25
- time_qkv: bfloat16 [1152, 1728], replicated, may hold values from -2 to 2
- time_out: bfloat16 [576, 1152], replicated, may hold values from -0.25 to 0.25
Outputs:
- block_output: bfloat16 [8, 64, 256, 1152], P('cam', 'frame')
Inputs may be any that keep to these rules, and one draw needn't show every extreme that they name: `counts`: in every camera some frame is full, with 4 rows. Row c holds camera c's cycle neighbours (c - 1) mod 8 and (c + 1) mod 8, in either order.
All inputs are finite; a program needn't handle non-finite values.
Results may differ from a plain program's by a relative error of at most 0.017.
The roundings to bfloat16 on the way count: a program that leaves them out, or rounds other values in their place, can miss the bound.
Values may be sent and summed in bfloat16 or wider, within the bound.
No kernel may reach another device: no remote copies, remote signals or barrier semaphores. Data moves between devices by JAX's collectives and lax.ppermute only.
A program may use at most 128 MiB of HBM per device.

v0:
```python
import jax
import jax.numpy as jnp
from jax import lax
from jax.sharding import PartitionSpec as P

HEADS = 8


epsilon = 1e-06
row_tokens = 64


def passed_along(x, axis, by):
    peers = lax.axis_size(axis)
    return lax.ppermute(x, axis, [(i, (i + by) % peers) for i in range(peers)])


def normalize(values):
    values = values.astype(jnp.float32)
    mean = jnp.mean(values, axis=-1, keepdims=True)
    centred = values - mean
    variance = jnp.mean(centred * centred, axis=-1, keepdims=True)
    return (centred * lax.rsqrt(variance + epsilon)).astype(jnp.bfloat16)


def project(normed, weight):
    flat = normed.reshape(-1, normed.shape[-1])
    result = jnp.dot(flat, weight, preferred_element_type=jnp.float32)
    return result.reshape(normed.shape[:-1] + (weight.shape[1],))


def softmax_rows(scores, allowed):
    masked = jnp.where(allowed, scores, -1e30)
    highest = jnp.max(masked, axis=-1, keepdims=True)
    expo = jnp.exp(masked - highest)
    return (expo / jnp.sum(expo, axis=-1, keepdims=True)).astype(jnp.bfloat16)


def temporal_tail(projected, arrived, time_out):
    cams_here, frames, places, _ = projected.shape
    inner = time_out.shape[0]
    head_size = inner // HEADS
    query_heads = projected[..., :inner].reshape(cams_here, frames, places, HEADS, head_size)
    key_heads = projected[..., inner : 2 * inner].reshape(
        cams_here, frames, places, HEADS, head_size
    )
    value_heads = projected[..., 2 * inner :].reshape(cams_here, frames, places, HEADS, head_size)
    scores = jnp.einsum(
        "cfphd,cgphd->cphfg", query_heads, key_heads, preferred_element_type=jnp.float32
    ) * head_size ** (-0.5)
    allowed = (jnp.transpose(arrived, (0, 2, 1)) > 0.5)[:, :, None, None, :]
    allowed = allowed | jnp.eye(frames, dtype=jnp.bool_)[None, None, None]
    probs = softmax_rows(scores, allowed)
    attended = jnp.einsum(
        "cphfg,cgphd->cfphd", probs, value_heads, preferred_element_type=jnp.float32
    )
    attended = attended.astype(jnp.bfloat16).reshape(cams_here, frames, places, inner)
    returned = lax.all_to_all(attended, "frame", split_axis=1, concat_axis=2, tiled=True)
    return project(returned, time_out)


def shards(tokens, counts, neighbours, side_keys, cross_qkv, cross_out, time_qkv, time_out):
    cam_here, frames_here, token_count, width = tokens.shape
    inner = cross_out.shape[0]
    head_size = inner // HEADS
    position = lax.broadcasted_iota(jnp.int32, (cam_here, frames_here, token_count), 2)
    valid = (position < row_tokens * counts[:, :, None]).astype(jnp.bfloat16)
    projected = project(normalize(tokens), cross_qkv).astype(jnp.bfloat16)
    query = projected[..., :inner]
    keys = projected[..., inner : 2 * inner]
    values = projected[..., 2 * inner :]
    left_keys, left_values, left_valid = passed_along((keys[-1], values[-1], valid[-1]), "cam", 1)
    right_keys, right_values, right_valid = passed_along((keys[0], values[0], valid[0]), "cam", -1)
    lower_keys = jnp.concatenate([left_keys[None], keys[:-1]], axis=0)
    lower_values = jnp.concatenate([left_values[None], values[:-1]], axis=0)
    lower_valid = jnp.concatenate([left_valid[None], valid[:-1]], axis=0)
    upper_keys = jnp.concatenate([keys[1:], right_keys[None]], axis=0)
    upper_values = jnp.concatenate([values[1:], right_values[None]], axis=0)
    upper_valid = jnp.concatenate([valid[1:], right_valid[None]], axis=0)
    cameras = cam_here * lax.axis_size("cam")
    cam_ids = cam_here * lax.axis_index("cam") + jnp.arange(cam_here, dtype=jnp.int32)
    first_lower = neighbours[:, 0] == (cam_ids - 1) % cameras
    side_lower = jnp.where(first_lower[:, None], side_keys[0][None], side_keys[1][None]).astype(
        jnp.float32
    )
    side_upper = jnp.where(first_lower[:, None], side_keys[1][None], side_keys[0][None]).astype(
        jnp.float32
    )
    lower_keys = (lower_keys.astype(jnp.float32) + side_lower[:, None, None, :]).astype(
        jnp.bfloat16
    )
    upper_keys = (upper_keys.astype(jnp.float32) + side_upper[:, None, None, :]).astype(
        jnp.bfloat16
    )
    all_keys = jnp.concatenate([keys, lower_keys, upper_keys], axis=2)
    all_values = jnp.concatenate([values, lower_values, upper_values], axis=2)
    all_valid = jnp.concatenate([valid, lower_valid, upper_valid], axis=2)
    items = cam_here * frames_here
    query_heads = query.reshape(items, token_count, HEADS, head_size)
    key_heads = all_keys.reshape(items, 3 * token_count, HEADS, head_size)
    value_heads = all_values.reshape(items, 3 * token_count, HEADS, head_size)
    scores = jnp.einsum(
        "bqhd,bkhd->bhqk", query_heads, key_heads, preferred_element_type=jnp.float32
    ) * head_size ** (-0.5)
    allowed = (all_valid.reshape(items, 3 * token_count) > 0.5)[:, None, None, :]
    probs = softmax_rows(scores, allowed)
    attended = jnp.einsum("bhqk,bkhd->bqhd", probs, value_heads, preferred_element_type=jnp.float32)
    attended = attended.astype(jnp.bfloat16).reshape(cam_here, frames_here, token_count, inner)
    mixed = (project(attended, cross_out) + tokens.astype(jnp.float32)).astype(jnp.bfloat16)
    normed = normalize(mixed)
    time_proj = project(normed, time_qkv).astype(jnp.bfloat16)
    temporal = temporal_tail(
        lax.all_to_all(time_proj, "frame", split_axis=2, concat_axis=1, tiled=True),
        lax.all_to_all(valid, "frame", split_axis=2, concat_axis=1, tiled=True),
        time_out,
    )
    return (temporal + mixed.astype(jnp.float32)).astype(jnp.bfloat16)


def solution(mesh):
    return jax.shard_map(
        shards,
        mesh=mesh,
        in_specs=(
            P("cam", "frame", None, None),
            P("cam", "frame"),
            P("cam", None),
            P(),
            P(),
            P(),
            P(),
            P(),
        ),
        out_specs=P("cam", "frame", None, None),
        check_vma=False,
    )
```

profile of v0, /device:TPU:22, one launch (start us, length us, event | category | flops | bytes accessed | tf_op | source)
XLA Modules:
  0.0 170.5 jit_solution(15354001180407707164)
XLA Ops:
  0.0 1.6 convert_reduce_fusion.1
  1.7 1.7 %fusion.29 = f32[2,256]{1,0:T(2,128)S(1)} fusion(bf16[2,1,256,1152]{3,2,1,0:T(8,128)(2,1)} %param.8, f32[2,256]{1,0:T(2,128)S(1)} %broadcast_multiply_fusion.1), kind=kLoop, calls=%fused_computation.34 | loop fusion | flops 2358784 | bytes 1183744 | tf_op jit(solution)/shard_map/reduce_sum | solution.py:22
  3.4 4.8 %fusion.11 = bf16[2,256,1728]{1,2,0:T(8,128)(2,1)S(1)} fusion(bf16[1152,1728]{0,1:T(8,128)(2,1)} %param.12, bf16[2,1,256,1152]{3,2,1,0:T(8,128)(2,1)S(1)} %copy-done.1, f32[2,256]{1,0:T(2,128)S(1)} %add_rsqrt_fusion.1, f32[2,256]{1,0:T(2,128)S(1)} %broadcast_multiply_fusion.1), kind=kOutput, calls=%fused_computation.22 | convolution fusion | flops 2041675776 | bytes 6934528 | tf_op jit(solution)/shard_map/dot_general | solution.py:28
  8.2 1.3 slice_bitcast_fusion.5
  9.6 0.7 slice_bitcast_fusion.6
  10.3 0.5 collective-permute-start
  10.8 2.7 %collective-permute-start.5 = (bf16[1,256,576]{1,2,0:T(8,128)(2,1)}, bf16[1,256,576]{1,2,0:T(8,128)(2,1)}, u32[]{:S(2)}, u32[]{:S(2)}) collective-permute-start(bf16[1,256,576]{1,2,0:T(8,128)(2,1)} %get-tuple-element.13), channel_id=1, source_target_pairs={{0,192},{64,0},{128,64},{192,128},{1,193},{65,1},{129,65},{193,129... | collective-permute-start | bytes 884744 | tf_op jit(solution)/shard_map/ppermute | solution.py:15
  13.6 0.1 compare_convert_fusion
  13.6 0.6 slice_bitcast_fusion.3
  14.2 0.5 collective-permute-start.2
  14.8 0.8 copy.79
  15.6 13.3 %all-to-all-start.1 = ((bf16[2,1,256]{0,1,2:T(2,128)(2,1)}), bf16[2,1,256]{0,1,2:T(2,128)(2,1)S(1)}, u32[]{:S(2)}, u32[]{:S(2)}) async-start(bf16[2,1,256]{0,1,2:T(2,128)(2,1)} %copy.79), calls=%async_computation.1 | async-start | bytes 262144 | tf_op jit(solution)/shard_map/all_to_all | solution.py:114
  28.9 1.1 fusion.79
  30.1 0.1 broadcast_in_dim.102
  30.2 0.1 broadcast_in_dim.100
  30.3 0.9 compare_reduce_fusion
  31.2 0.1 select_convert_fusion.1
  31.3 0.9 slice.72
  32.1 1.3 collective-permute-start.4
  33.5 1.3 add_convert_fusion
  34.8 5.4 %collective-permute-done.4 = bf16[1,256,576]{1,2,0:T(8,128)(2,1)S(1)} collective-permute-done((bf16[1,256,576]{1,2,0:T(8,128)(2,1)}, bf16[1,256,576]{1,2,0:T(8,128)(2,1)S(1)}, u32[]{:S(2)}, u32[]{:S(2)}) %collective-permute-start.4) | collective-permute-done | bytes 294944 | tf_op jit(solution)/shard_map/ppermute | solution.py:15
  40.2 0.2 add_convert_fusion.1
  40.4 1.8 %fusion.32 = f32[2,8,256,768]{3,2,1,0:T(8,128)S(1)} fusion(bf16[2,256,8,72]{1,3,2,0:T(8,128)(2,1)S(1)} %bitcast.115, bf16[2,256,8,72]{1,3,2,0:T(8,128)(2,1)S(1)} %add_convert_fusion, bf16[2,256,8,72]{1,3,2,0:T(8,128)(2,1)S(1)} %add_convert_fusion.1, bf16[2,256,8,72]{1,3,2,0:T(8,128)(2,1)S(1)} %bitcast.114), kind=kOutput, calls=%fused_computation.41 | convolution fusion | flops 458293248 | bytes 14942208 | tf_op jit(solution)/shard_map/bqhd,bkhd->bhqk/dot_general | solution.py:102
  42.3 7.0 %fusion.80 = (f32[2,8,256]{2,1,0:T(8,128)S(1)}, f32[2,8,256,768]{3,2,1,0:T(8,128)}) fusion(f32[2,8,256,768]{3,2,1,0:T(8,128)S(1)} %fusion.32, pred[2,768]{1,0:T(4,128)(4,1)S(1)} %bitcast.122), kind=kOutput, calls=%fused_computation.104 | output fusion | flops 18875136 | bytes 25183744 | tf_op jit(solution)/shard_map/sub | solution.py:35
  49.3 1.2 maximum_maximum_fusion
  50.5 6.8 %fusion.41 = bf16[2,8,72,256]{3,2,1,0:T(8,128)(2,1)S(1)} fusion(bf16[2,768,8,72]{1,3,2,0:T(8,128)(2,1)S(1)} %bitcast.116, f32[2,8,256,768]{3,2,1,0:T(8,128)} %get-tuple-element.27, f32[2,8,256]{2,1,0:T(8,128)S(1)} %get-tuple-element.26), kind=kOutput, calls=%fused_computation.51 | convolution fusion | flops 459571200 | bytes 14958592 | tf_op jit(solution)/shard_map/bhqk,bkhd->bqhd/dot_general | solution.py:107
  57.4 1.4 convert_reduce_fusion
  58.8 0.4 fusion.27
  59.2 0.5 copy-done.8
  59.8 2.8 %fusion.24 = bf16[2,1,256,1728]{2,3,0,1:T(8,128)(2,1)S(1)} fusion(bf16[1152,1728]{0,1:T(8,128)(2,1)S(1)} %copy-done.12, bf16[2,1,256,1152]{3,2,0,1:T(8,128)(2,1)S(1)} %get-tuple-element.29, f32[2,256]{1,0:T(2,128)S(1)} %add_rsqrt_fusion, f32[2,256]{1,0:T(2,128)S(1)} %broadcast_multiply_fusion), kind=kOutput, calls=%fused_computation.31 | convolution fusion | flops 2041675776 | bytes 6934528 | tf_op jit(solution)/shard_map/dot_general | solution.py:28
  62.6 3.7 %copy.77 = bf16[2,1,256,1728]{3,0,1,2:T(2,128)(2,1)} copy(bf16[2,1,256,1728]{2,3,0,1:T(8,128)(2,1)S(1)} %fusion.24) | data formatting | bytes 3538944 | tf_op jit(solution)/shard_map/convert_element_type | solution.py:111
  66.2 11.1 %all-to-all-start = ((bf16[2,1,256,1728]{3,0,1,2:T(2,128)(2,1)}), bf16[2,1,256,1728]{3,0,1,2:T(2,128)(2,1)S(1)}, u32[]{:S(2)}, u32[]{:S(2)}) async-start(bf16[2,1,256,1728]{3,0,1,2:T(2,128)(2,1)} %copy.77), calls=%async_computation | async-start | bytes 3670016 | tf_op jit(solution)/shard_map/all_to_all | solution.py:113
  77.4 0.1 copy.80
  77.5 0.1 gt.30
  77.6 0.1 copy.81
  77.7 0.2 broadcast_or_fusion
  77.9 43.9 %all-to-all-done = bf16[2,1,256,1728]{3,0,1,2:T(2,128)(2,1)S(1)} async-done(((bf16[2,1,256,1728]{3,0,1,2:T(2,128)(2,1)}), bf16[2,1,256,1728]{3,0,1,2:T(2,128)(2,1)S(1)}, u32[]{:S(2)}, u32[]{:S(2)}) %all-to-all-start) | async-done | bytes 1769504 | tf_op jit(solution)/shard_map/all_to_all | solution.py:113
  121.8 2.8 %fusion.78 = (bf16[2,64,4,576]{3,0,2,1:T(2,128)(2,1)}, bf16[2,64,4,576]{3,0,2,1:T(2,128)(2,1)}, bf16[2,64,4,576]{3,0,2,1:T(2,128)(2,1)}) fusion(bf16[2,64,4,1728]{3,0,2,1:T(2,128)(2,1)S(1)} %bitcast.109), kind=kLoop, calls=%fused_computation.102 | loop fusion | bytes 3538944 | tf_op jit(solution)/shard_map/slice | solution.py:47
  124.7 2.8 %reshape.345 = bf16[2,64,4,8,72]{4,3,0,2,1:T(8,128)(2,1)S(1)} reshape(bf16[2,64,4,576]{3,0,2,1:T(2,128)(2,1)} %get-tuple-element.8) | data formatting | bytes 1179648 | tf_op jit(solution)/shard_map/reshape | solution.py:44
  127.5 3.5 %reshape.344 = bf16[2,64,4,8,72]{4,3,0,2,1:T(8,128)(2,1)} reshape(bf16[2,64,4,576]{3,0,2,1:T(2,128)(2,1)} %get-tuple-element.9) | data formatting | bytes 1179648 | tf_op jit(solution)/shard_map/reshape | solution.py:43
  131.0 2.3 %reshape.343 = bf16[2,64,4,8,72]{4,3,0,2,1:T(8,128)(2,1)} reshape(bf16[2,64,4,576]{3,0,2,1:T(2,128)(2,1)S(1)} %copy-done.3) | data formatting | bytes 1179648 | tf_op jit(solution)/shard_map/reshape | solution.py:47
  133.2 4.5 %fusion.81 = (f32[2,4,8,64]{3,2,1,0:T(8,128)S(1)}, f32[2,4,8,64,64]{3,4,2,1,0:T(8,128)}) fusion(pred[2,4,64,64]{2,3,1,0:T(8,128)(4,1)S(1)} %broadcast_or_fusion, bf16[2,64,4,8,72]{4,3,0,2,1:T(8,128)(2,1)S(1)} %reshape.345, bf16[2,64,4,8,72]{4,3,0,2,1:T(8,128)(2,1)} %reshape.344), kind=kOutput, calls=%fused_computation.105 | convolution fusion | flops 38797376 | bytes 2277376 | tf_op jit(solution)/shard_map/sub | solution.py:35
  137.7 3.2 %fusion.38 = bf16[2,64,4,8,72]{4,1,3,2,0:T(8,128)(2,1)S(1)} fusion(f32[2,4,8,64,64]{3,4,2,1,0:T(8,128)} %get-tuple-element.31, bf16[2,64,4,8,72]{4,3,0,2,1:T(8,128)(2,1)} %reshape.343, f32[2,4,8,64]{3,2,1,0:T(8,128)S(1)} %get-tuple-element.30), kind=kOutput, calls=%fused_computation.48 | convolution fusion | flops 38567936 | bytes 2244608 | tf_op jit(solution)/shard_map/cphfg,cgphd->cfphd/dot_general | solution.py:54
  140.9 0.7 copy.100
  141.6 1.2 reshape.346
  142.8 25.0 %all_to_all.30 = bf16[2,64,4,576]{3,2,0,1:T(4,128)(2,1)S(1)} all-to-all(bf16[2,64,4,576]{3,2,0,1:T(4,128)(2,1)S(1)} %reshape.346), channel_id=1, replica_groups=mesh['cam'=4,'frame'=64] {'frame'}, dimensions={1} | all-to-all | bytes 1179648 | tf_op jit(solution)/shard_map/all_to_all | solution.py:58
  167.8 0.5 copy.90
  168.3 2.2 %fusion.23 = bf16[2,1,256,1152]{3,2,1,0:T(8,128)(2,1)} fusion(bf16[2,1,256,1152]{3,2,0,1:T(8,128)(2,1)S(1)} %copy-done.9, bf16[576,1152]{1,0:T(8,128)(2,1)S(1)} %copy-done.13, bf16[2,256,576]{2,0,1:T(2,128)(2,1)S(1)} %bitcast.119), kind=kOutput, calls=%fused_computation.30 | convolution fusion | flops 681246720 | bytes 4276224 | tf_op jit(solution)/shard_map/dot_general | solution.py:28
  (47 shorter events, 0.2 us)
Async XLA Ops:
  0.0 57.3 %copy-start = (bf16[576,1152]{1,0:T(8,128)(2,1)S(1)}, bf16[576,1152]{1,0:T(8,128)(2,1)}, u32[]{:S(2)}) copy-start(bf16[576,1152]{1,0:T(8,128)(2,1)} %param.13) | copy-start | bytes 3981316
  0.0 3.4 %copy-start.1 = (bf16[2,1,256,1152]{3,2,1,0:T(8,128)(2,1)S(1)}, bf16[2,1,256,1152]{3,2,1,0:T(8,128)(2,1)}, u32[]{:S(2)}) copy-start(bf16[2,1,256,1152]{3,2,1,0:T(8,128)(2,1)} %param.8) | copy-start | bytes 3538948
  8.2 5.3 %copy-start.14 = (s32[2,1]{0,1:T(1,128)S(1)}, s32[2,1]{0,1:T(1,128)}, u32[]{:S(2)}) copy-start(s32[2,1]{0,1:T(1,128)} %param.9) | copy-start | bytes 28
  9.6 20.5 %copy-start.11 = (bf16[2,576]{1,0:T(2,128)(2,1)S(1)}, bf16[2,576]{1,0:T(2,128)(2,1)}, u32[]{:S(2)}) copy-start(bf16[2,576]{1,0:T(2,128)(2,1)} %param.11) | copy-start | bytes 6916
  9.6 39.7 %collective-permute-start.1 = (bf16[1,256,576]{1,2,0:T(8,128)(2,1)}, bf16[1,256,576]{1,2,0:T(8,128)(2,1)}, u32[]{:S(2)}, u32[]{:S(2)}) collective-permute-start(bf16[1,256,576]{1,2,0:T(8,128)(2,1)} %get-tuple-element.14), channel_id=1, source_target_pairs={{0,192},{64,0},{128,64},{192,128},{1,193},{65,1},{129,65},{193,129... | collective-permute-start | bytes 884744 | tf_op jit(solution)/shard_map/ppermute | solution.py:15
  10.3 39.0 %collective-permute-start = (bf16[1,256,576]{1,2,0:T(8,128)(2,1)}, bf16[1,256,576]{1,2,0:T(8,128)(2,1)}, u32[]{:S(2)}, u32[]{:S(2)}) collective-permute-start(bf16[1,256,576]{1,2,0:T(8,128)(2,1)} %get-tuple-element.18), channel_id=1, source_target_pairs={{0,64},{64,128},{128,192},{192,0},{1,65},{65,129},{129,193},{193,1... | collective-permute-start | bytes 884744 | tf_op jit(solution)/shard_map/ppermute | solution.py:15
  10.8 22.7 %collective-permute-start.5 = (bf16[1,256,576]{1,2,0:T(8,128)(2,1)}, bf16[1,256,576]{1,2,0:T(8,128)(2,1)}, u32[]{:S(2)}, u32[]{:S(2)}) collective-permute-start(bf16[1,256,576]{1,2,0:T(8,128)(2,1)} %get-tuple-element.13), channel_id=1, source_target_pairs={{0,192},{64,0},{128,64},{192,128},{1,193},{65,1},{129,65},{193,129... | collective-permute-start | bytes 884744 | tf_op jit(solution)/shard_map/ppermute | solution.py:15
  14.2 17.9 %collective-permute-start.3 = (bf16[1,256]{1,0:T(2,128)(2,1)}, bf16[1,256]{1,0:T(2,128)(2,1)S(1)}, u32[]{:S(2)}, u32[]{:S(2)}) collective-permute-start(bf16[1,256]{1,0:T(2,128)(2,1)} %get-tuple-element.23), channel_id=1, source_target_pairs={{0,192},{64,0},{128,64},{192,128},{1,193},{65,1},{129,65},{193,129... | collective-permute-start | bytes 1544 | tf_op jit(solution)/shard_map/ppermute | solution.py:15
  14.2 19.2 %collective-permute-start.2 = (bf16[1,256]{1,0:T(2,128)(2,1)}, bf16[1,256]{1,0:T(2,128)(2,1)S(1)}, u32[]{:S(2)}, u32[]{:S(2)}) collective-permute-start(bf16[1,256]{1,0:T(2,128)(2,1)} %get-tuple-element.22), channel_id=1, source_target_pairs={{0,64},{64,128},{128,192},{192,0},{1,65},{65,129},{129,193},{193,1... | collective-permute-start | bytes 1544 | tf_op jit(solution)/shard_map/ppermute | solution.py:15
  15.6 50.7 %all-to-all-start.1 = ((bf16[2,1,256]{0,1,2:T(2,128)(2,1)}), bf16[2,1,256]{0,1,2:T(2,128)(2,1)S(1)}, u32[]{:S(2)}, u32[]{:S(2)}) async-start(bf16[2,1,256]{0,1,2:T(2,128)(2,1)} %copy.79), calls=%async_computation.1 | async-start | bytes 262144 | tf_op jit(solution)/shard_map/all_to_all | solution.py:114
  30.2 9.9 %copy-start.10 = (bf16[1,1,256,576]{2,3,0,1:T(8,128)(2,1)S(1)}, bf16[1,1,256,576]{2,3,0,1:T(8,128)(2,1)}, u32[]{:S(2)}) copy-start(bf16[1,1,256,576]{2,3,0,1:T(8,128)(2,1)} %get-tuple-element.16) | copy-start | bytes 884740
  30.3 10.2 %copy-start.4 = (bf16[2,1,256,576]{2,3,0,1:T(8,128)(2,1)S(1)}, bf16[2,1,256,576]{2,3,0,1:T(8,128)(2,1)}, u32[]{:S(2)}) copy-start(bf16[2,1,256,576]{2,3,0,1:T(8,128)(2,1)} %get-tuple-element.10) | copy-start | bytes 1769476
  30.3 10.2 %copy-start.5 = (bf16[2,1,256,576]{2,3,0,1:T(8,128)(2,1)S(1)}, bf16[2,1,256,576]{2,3,0,1:T(8,128)(2,1)}, u32[]{:S(2)}) copy-start(bf16[2,1,256,576]{2,3,0,1:T(8,128)(2,1)} %get-tuple-element.11) | copy-start | bytes 1769476
  32.1 8.1 %collective-permute-start.4 = (bf16[1,256,576]{1,2,0:T(8,128)(2,1)}, bf16[1,256,576]{1,2,0:T(8,128)(2,1)S(1)}, u32[]{:S(2)}, u32[]{:S(2)}) collective-permute-start(bf16[1,256,576]{1,2,0:T(8,128)(2,1)} %get-tuple-element.12), channel_id=1, source_target_pairs={{0,64},{64,128},{128,192},{192,0},{1,65},{65,129},{129,193},{193,1... | collective-permute-start | bytes 884744 | tf_op jit(solution)/shard_map/ppermute | solution.py:15
  42.3 7.0 %copy-start.6 = (bf16[2,1,256,576]{2,3,1,0:T(8,128)(2,1)S(1)}, bf16[2,1,256,576]{2,3,1,0:T(8,128)(2,1)}, u32[]{:S(2)}) copy-start(bf16[2,1,256,576]{2,3,1,0:T(8,128)(2,1)} %slice.72) | copy-start | bytes 1769476
  42.3 7.0 %copy-start.7 = (bf16[1,1,256,576]{2,3,1,0:T(8,128)(2,1)S(1)}, bf16[1,1,256,576]{2,3,1,0:T(8,128)(2,1)}, u32[]{:S(2)}) copy-start(bf16[1,1,256,576]{2,3,1,0:T(8,128)(2,1)} %get-tuple-element.15) | copy-start | bytes 884740
  50.5 6.8 %copy-start.2 = (bf16[2,1,256,1152]{3,2,1,0:T(8,128)(2,1)S(1)}, bf16[2,1,256,1152]{3,2,1,0:T(8,128)(2,1)}, u32[]{:S(2)}) copy-start(bf16[2,1,256,1152]{3,2,1,0:T(8,128)(2,1)} %param.8) | copy-start | bytes 3538948
  57.3 2.4 %copy-start.12 = (bf16[1152,1728]{0,1:T(8,128)(2,1)S(1)}, bf16[1152,1728]{0,1:T(8,128)(2,1)}, u32[]{:S(2)}) copy-start(bf16[1152,1728]{0,1:T(8,128)(2,1)} %param.14) | copy-start | bytes 11943940
  58.8 1.0 copy-start.8
  66.2 55.6 %all-to-all-start = ((bf16[2,1,256,1728]{3,0,1,2:T(2,128)(2,1)}), bf16[2,1,256,1728]{3,0,1,2:T(2,128)(2,1)S(1)}, u32[]{:S(2)}, u32[]{:S(2)}) async-start(bf16[2,1,256,1728]{3,0,1,2:T(2,128)(2,1)} %copy.77), calls=%async_computation | async-start | bytes 3670016 | tf_op jit(solution)/shard_map/all_to_all | solution.py:113
  124.7 6.3 %copy-start.3 = (bf16[2,64,4,576]{3,0,2,1:T(2,128)(2,1)S(1)}, bf16[2,64,4,576]{3,0,2,1:T(2,128)(2,1)}, u32[]{:S(2)}) copy-start(bf16[2,64,4,576]{3,0,2,1:T(2,128)(2,1)} %get-tuple-element.7) | copy-start | bytes 1769476
  142.8 25.5 %copy-start.9 = (bf16[2,1,256,1152]{3,2,0,1:T(8,128)(2,1)S(1)}, bf16[2,1,256,1152]{3,2,0,1:T(8,128)(2,1)}, u32[]{:S(2)}) copy-start(bf16[2,1,256,1152]{3,2,0,1:T(8,128)(2,1)} %copy-done.8) | copy-start | bytes 3538948
  142.8 25.5 %copy-start.13 = (bf16[576,1152]{1,0:T(8,128)(2,1)S(1)}, bf16[576,1152]{1,0:T(8,128)(2,1)}, u32[]{:S(2)}) copy-start(bf16[576,1152]{1,0:T(8,128)(2,1)} %param.15) | copy-start | bytes 3981316
where the time goes:
time: 171 us
  waiting for transfers between devices  49.3 us (29%)
  starting transfers between devices  29.6 us (17%)
  matrix products  27.6 us (16%)
  blocking collectives  25 us (15%)
  local copies, waits for them, and re-layouts  24.1 us (14%)
  other arithmetic  14.8 us (9%)
    all_to_all x1, waiting for transfers between devices, shards(): lax.all_to_all(time_proj, 'frame', split_axis=2, concat_axis=1, tiled=True)  43.9 us
    all_to_all x1, blocking collectives, temporal_tail(): lax.all_to_all(attended, 'frame', split_axis=1, concat_axis=2, tiled=True)  25 us
    all_to_all x1, starting transfers between devices, shards(): lax.all_to_all(valid, 'frame', split_axis=2, concat_axis=1, tiled=True)  13.3 us
    dot_general x4, matrix products, project(): result = jnp.dot(flat, weight, preferred_element_type=jnp.float32)  11.2 us
    all_to_all x1, starting transfers between devices, shards(): lax.all_to_all(time_proj, 'frame', split_axis=2, concat_axis=1, tiled=True)  11.1 us
    sub x1, other arithmetic, softmax_rows(): expo = jnp.exp(masked - highest)  7 us
    dot_general x1, matrix products, shards(): jnp.einsum('bhqk,bkhd->bqhd', probs, value_heads, preferred_element_type=...  6.82 us
    ppermute x6, waiting for transfers between devices, passed_along(): return lax.ppermute(x, axis, [(i, (i + by) % peers) for i in range(peers)])  5.4 us
  transfers between devices with their start and end apart: 8, of which 2 were waited for; matrix products, arithmetic and copies ran while one was open for 19% of the time, Pallas kernels for 0%

commit v1 on v0

v1 whole, which is shorter than its diff:
```python
import functools
import math

import jax
import jax.numpy as jnp
from jax import lax
from jax.experimental import pallas as pl
from jax.experimental.pallas import tpu as pltpu
from jax.sharding import PartitionSpec as P

HEADS = 8
HEAD = 72
INNER = HEADS * HEAD
EPS = 1e-06
ROW_TOKENS = 64
BIG = 1e30
COEF = HEAD ** (-0.5) * math.log2(math.e)
LANES = 128
MIB = 1 << 20


def passed_along(x, axis, by):
    peers = lax.axis_size(axis)
    return lax.ppermute(x, axis, [(i, (i + by) % peers) for i in range(peers)])


def dot_nt(a, b):
    return lax.dot_general(a, b, (((1,), (1,)), ((), ())), preferred_element_type=jnp.float32)


def dot_nn(a, b):
    return lax.dot_general(a, b, (((1,), (0,)), ((), ())), preferred_element_type=jnp.float32)


def normalize(values):
    values = values.astype(jnp.float32)
    mean = jnp.mean(values, axis=-1, keepdims=True)
    centred = values - mean
    variance = jnp.mean(centred * centred, axis=-1, keepdims=True)
    return (centred * lax.rsqrt(variance + EPS)).astype(jnp.bfloat16)


def lane_ids(rows):
    return lax.broadcasted_iota(jnp.int32, (rows, LANES), 1)


def row_ids(rows):
    return lax.broadcasted_iota(jnp.int32, (rows, LANES), 0)


def invalid_bias(rows, count):
    return jnp.where(row_ids(rows) < ROW_TOKENS * count, 0.0, -BIG).astype(jnp.bfloat16)


def query_window(x, head):
    window = x[:, head * HEAD : head * HEAD + LANES]
    return jnp.where(lane_ids(x.shape[0]) == HEAD, jnp.ones_like(window), window)


def key_window(x, start, bias):
    window = x[:, start : start + LANES]
    lane = lane_ids(x.shape[0])
    return jnp.where(lane < HEAD, window, jnp.where(lane == HEAD, bias, jnp.zeros_like(window)))


def value_window(x, start):
    window = x[:, start : start + LANES]
    return jnp.where(lane_ids(x.shape[0]) == HEAD, jnp.ones_like(window), window)


def join_heads(pieces):
    return jnp.concatenate([piece[:, :HEAD] for piece in pieces], axis=1)


def side_row(side_ref, neighbours_ref, cam, lower, cameras, cam_here):
    camera = lax.axis_index("cam") * cam_here + cam
    first_lower = neighbours_ref[cam, 0] == lax.rem(camera + cameras - 1, cameras)
    pick_first = first_lower if lower else jnp.logical_not(first_lower)
    return jnp.where(pick_first, side_ref[0:1, :], side_ref[1:2, :])


def local_kernel(cameras, counts_ref, neighbours_ref, tokens_ref, weight_ref, side_ref, query_ref, part_ref, qkv_ref):
    rows = tokens_ref.shape[0] // 2
    normed = normalize(tokens_ref[...])
    width = weight_ref.shape[0]
    qkv_ref[:, :width] = dot_nt(normed, weight_ref[...]).astype(jnp.bfloat16)
    qkv_ref[:, width:] = jnp.zeros((2 * rows, qkv_ref.shape[1] - width), jnp.bfloat16)
    query_ref[...] = qkv_ref[:, : query_ref.shape[1]]
    biases = [invalid_bias(rows, counts_ref[c, 0]) for c in range(2)]
    for c in range(2):
        own, other = pl.ds(c * rows, rows), pl.ds((1 - c) * rows, rows)
        side = side_row(side_ref, neighbours_ref, c, c == 1, cameras, 2)
        q_all = qkv_ref[own, :640]
        k_own = qkv_ref[own, 512:1280]
        k_other = qkv_ref[other, 512:1280]
        k_other = (k_other.astype(jnp.float32) + side).astype(jnp.bfloat16)
        v_own, v_other = qkv_ref[own, 1152:], qkv_ref[other, 1152:]
        for h in range(HEADS):
            q = query_window(q_all, h)
            start = INNER - 512 + h * HEAD
            k = jnp.concatenate(
                [key_window(k_own, start, biases[c]), key_window(k_other, start, biases[1 - c])], axis=0
            )
            v = jnp.concatenate([value_window(v_own, h * HEAD), value_window(v_other, h * HEAD)], axis=0)
            scores = dot_nt(q, k)
            highest = jnp.max(scores, axis=1, keepdims=True)
            expo = jnp.exp2((scores - highest) * COEF).astype(jnp.bfloat16)
            summed = dot_nn(expo, v)
            part_ref[c, h] = jnp.where(lane_ids(rows) == HEAD + 1, highest, summed)


def merge_kernel(
    cameras, counts_ref, far_counts_ref, neighbours_ref, tokens_ref, lower_ref, upper_ref, weight_ref, side_ref, query_ref,
    part_ref, out_weight_ref, mixed_ref, payload_ref, kv_ref,
):
    rows = tokens_ref.shape[0] // 2
    kv_weight = weight_ref[INNER:, :]
    for c, far_ref in enumerate((lower_ref, upper_ref)):
        here = pl.ds(c * rows, rows)
        kv_ref[here, : 2 * INNER] = dot_nt(normalize(far_ref[...]), kv_weight).astype(jnp.bfloat16)
        kv_ref[here, 2 * INNER :] = jnp.zeros((rows, kv_ref.shape[1] - 2 * INNER), jnp.bfloat16)
    for c in range(2):
        here = pl.ds(c * rows, rows)
        side = side_row(side_ref, neighbours_ref, c, c == 0, cameras, 2)
        bias = invalid_bias(rows, far_counts_ref[c, 0])
        q_all = query_ref[here, :]
        k_all = (kv_ref[here, : 640].astype(jnp.float32) + side).astype(jnp.bfloat16)
        v_all = kv_ref[here, 512:]
        pieces = []
        for h in range(HEADS):
            q = query_window(q_all, h)
            k = key_window(k_all, h * HEAD, bias)
            v = value_window(v_all, INNER - 512 + h * HEAD)
            scores = dot_nt(q, k)
            part = part_ref[c, h]
            before = part[:, HEAD + 1 : HEAD + 2]
            highest = jnp.maximum(jnp.max(scores, axis=1, keepdims=True), before)
            expo = jnp.exp2((scores - highest) * COEF).astype(jnp.bfloat16)
            summed = part * jnp.exp2((before - highest) * COEF) + dot_nn(expo, v)
            pieces.append(summed / summed[:, HEAD : HEAD + 1])
        attended = join_heads(pieces).astype(jnp.bfloat16)
        mixed = dot_nn(attended, out_weight_ref[...]) + tokens_ref[here, :].astype(jnp.float32)
        mixed = mixed.astype(jnp.bfloat16)
        mixed_ref[here, :] = mixed
        width = mixed.shape[1]
        payload_ref[here, :width] = normalize(mixed)
        valid = row_ids(rows) < ROW_TOKENS * counts_ref[c, 0]
        payload_ref[here, width:] = jnp.where(valid, 1.0, 0.0).astype(jnp.bfloat16)


def time_kernel(frames, payload_ref, weight_ref, out_ref, qkv_ref):
    rows = payload_ref.shape[0]
    places = rows // frames
    width = weight_ref.shape[0]
    model = weight_ref.shape[1]
    qkv_ref[:, :width] = dot_nt(payload_ref[:, :model], weight_ref[...]).astype(jnp.bfloat16)
    qkv_ref[:, width:] = jnp.zeros((rows, qkv_ref.shape[1] - width), jnp.bfloat16)
    lane = lane_ids(rows)
    frame = row_ids(rows) // places
    place = row_ids(rows) % places
    invalid = payload_ref[:, model:].astype(jnp.float32) < 0.5
    query_mask = jnp.where(
        lane < frames,
        jnp.where(lane == frame, 1.0, 0.0),
        jnp.where(jnp.logical_and(lane < frames + places, lane - frames != place), -BIG, 0.0),
    ).astype(jnp.bfloat16)
    key_mask = jnp.where(
        lane < frames,
        jnp.where(jnp.logical_and(invalid, lane != frame), -BIG, 0.0),
        jnp.where(lane - frames == place, 1.0, 0.0),
    ).astype(jnp.bfloat16)
    zero = jnp.zeros((rows, LANES), jnp.bfloat16)
    q_all, k_all, v_all = qkv_ref[:, :640], qkv_ref[:, 512:1280], qkv_ref[:, 1152:]
    block = 256
    ks, vs = [], []
    pieces = [[] for _ in range(rows // block)]
    for h in range(HEADS):
        k = jnp.concatenate([key_window(k_all, INNER - 512 + h * HEAD, zero), key_mask], axis=1)
        v = value_window(v_all, h * HEAD)
        q = jnp.concatenate([q_all[:, h * HEAD : h * HEAD + LANES], query_mask], axis=1)
        for b in range(rows // block):
            scores = dot_nt(q[b * block : (b + 1) * block], k)
            highest = jnp.max(scores, axis=1, keepdims=True)
            expo = jnp.exp2((scores - highest) * COEF).astype(jnp.bfloat16)
            summed = dot_nn(expo, v)
            pieces[b].append(summed / summed[:, HEAD : HEAD + 1])
    for b in range(rows // block):
        out_ref[b * block : (b + 1) * block, :] = join_heads(pieces[b]).astype(jnp.bfloat16)


def final_kernel(attended_ref, weight_ref, mixed_ref, out_ref):
    result = dot_nn(attended_ref[...], weight_ref[...]) + mixed_ref[...].astype(jnp.float32)
    out_ref[...] = result.astype(jnp.bfloat16)


SMEM = pl.BlockSpec(memory_space=pltpu.SMEM)
VMEM = pl.BlockSpec(memory_space=pltpu.VMEM)


def kernel_call(body, ins, outs, scratch, mib, flops, nbytes):
    return pl.pallas_call(
        body,
        out_shape=outs,
        in_specs=ins,
        out_specs=[VMEM] * len(outs),
        scratch_shapes=scratch,
        compiler_params=pltpu.CompilerParams(vmem_limit_bytes=mib * MIB),
        cost_estimate=pl.CostEstimate(flops=flops, bytes_accessed=nbytes, transcendentals=0),
    )


def shards(tokens, counts, neighbours, side_keys, cross_qkv, cross_out, time_qkv, time_out):
    cam_here, frames_here, token_count, model = tokens.shape
    cameras = cam_here * lax.axis_size("cam")
    frames = lax.axis_size("frame")
    rows = cam_here * token_count
    bf16 = jnp.bfloat16
    spread = functools.partial(jax.ShapeDtypeStruct, dtype=bf16)

    lower_count = passed_along(counts[-1:], "cam", 1)
    upper_count = passed_along(counts[:1], "cam", -1)
    lower = passed_along(tokens[-1, 0], "cam", 1)
    upper = passed_along(tokens[0, 0], "cam", -1)
    far_counts = jnp.concatenate([lower_count, upper_count], axis=0)

    flat = tokens.reshape(rows, model)
    cross_t, time_t = cross_qkv.T, time_qkv.T
    side_local = jnp.pad(side_keys.astype(jnp.float32), ((0, 0), (INNER - 512, 128)))
    side_far = jnp.pad(side_keys.astype(jnp.float32), ((0, 0), (0, 64)))

    query, part = kernel_call(
        functools.partial(local_kernel, cameras),
        [SMEM, SMEM, VMEM, VMEM, VMEM],
        [spread((rows, 640)), jax.ShapeDtypeStruct((2, HEADS, token_count, LANES), jnp.float32)],
        [pltpu.VMEM((rows, 1792), bf16)],
        32,
        6_000_000_000,
        20_000_000,
    )(counts, neighbours, flat, cross_t, side_local)

    mixed, payload = kernel_call(
        functools.partial(merge_kernel, cameras),
        [SMEM, SMEM, SMEM] + [VMEM] * 8,
        [spread((rows, model)), spread((rows, model + LANES))],
        [pltpu.VMEM((rows, 1280), bf16)],
        32,
        4_000_000_000,
        12_000_000,
    )(counts, far_counts, neighbours, flat, lower, upper, cross_t, side_far, query, part, cross_out)

    chunk = rows // frames
    arrived = lax.all_to_all(
        payload.reshape(frames, chunk, model + LANES), "frame", split_axis=0, concat_axis=0, tiled=True
    )
    (attended,) = kernel_call(
        functools.partial(time_kernel, frames),
        [VMEM] * 2,
        [spread((rows, INNER))],
        [pltpu.VMEM((rows, 1792), bf16)],
        32,
        6_000_000_000,
        10_000_000,
    )(arrived.reshape(rows, model + LANES), time_t)
    returned = lax.all_to_all(
        attended.reshape(frames, chunk, INNER), "frame", split_axis=0, concat_axis=0, tiled=True
    )
    (out,) = kernel_call(
        final_kernel,
        [VMEM] * 3,
        [spread((rows, model))],
        [],
        32,
        700_000_000,
        4_000_000,
    )(returned.reshape(rows, INNER), time_out, mixed)
    return out.reshape(tokens.shape)


def solution(mesh):
    return jax.shard_map(
        shards,
        mesh=mesh,
        in_specs=(
            P("cam", "frame", None, None),
            P("cam", "frame"),
            P("cam", None),
            P(),
            P(),
            P(),
            P(),
            P(),
        ),
        out_specs=P("cam", "frame", None, None),
        check_vma=False,
    )
```

time: 171 us -> 119 us (0.70)
  waiting for transfers between devices: 49.3 us -> 0.67 us
  blocking collectives: 25 us -> 72.8 us
  Pallas kernels: 0 us -> 33.3 us
  matrix products: 27.6 us -> 0 us
  starting transfers between devices: 29.6 us -> 3.83 us
  local copies, waits for them, and re-layouts: 24.1 us -> 5.03 us
  other arithmetic: 14.8 us -> 1.19 us
    all_to_all x1 -> x2, blocking collectives: 25 us -> 72.8 us  [the longest x1 47.6 us: shards(): lax.all_to_all(payload.reshape(frames, chunk, model + LANES), 'frame', sp...]
    all_to_all x2 -> x0, waiting for transfers between devices: 43.9 us -> none  [the longest x1 43.9 us: shards(): lax.all_to_all(time_proj, 'frame', split_axis=2, concat_axis=1, tiled=True)]
    pallas_call x0 -> x4, Pallas kernels: none -> 33.3 us  [the longest x1 13 us: shards(): kernel_call(functools.partial(merge_kernel, cameras), [SMEM, SMEM, SMEM]...]
    all_to_all x2 -> x0, starting transfers between devices: 24.4 us -> none  [the longest x1 13.3 us: shards(): lax.all_to_all(valid, 'frame', split_axis=2, concat_axis=1, tiled=True)]
    dot_general x7 -> x0, matrix products: 23.1 us -> none  [the longest x4 11.2 us: project(): result = jnp.dot(flat, weight, preferred_element_type=jnp.float32)]
    reshape x5 -> x0, local copies, waits for them, and re-layouts: 10.4 us -> none  [the longest x1 3.5 us: temporal_tail(): projected[..., :inner].reshape(cams_here, frames, places, HEADS, head_size)]
    sub x1 -> x0, other arithmetic: 7 us -> none  [softmax_rows(): expo = jnp.exp(masked - highest)]
    ppermute x6 -> x4, waiting for transfers between devices: 5.4 us -> 0.67 us  [passed_along(): return lax.ppermute(x, axis, [(i, (i + by) % peers) for i in range(peers)])]
  transfers between devices with their start and end apart: 8 -> 4, of which waited for: 2 -> 1; matrix products, arithmetic and copies ran while one was open for 19% -> 2% of each run, Pallas kernels for 0% -> 8%
where the time goes in v1:
time: 119 us; the launch traced here: 117 us
  blocking collectives  72.8 us (61%)
  Pallas kernels  33.3 us (28%)
  local copies, waits for them, and re-layouts  5.03 us (4%)
  starting transfers between devices  3.83 us (3%)
  other arithmetic  1.19 us (1%)
    all_to_all x1, blocking collectives, shards(): lax.all_to_all(payload.reshape(frames, chunk, model + LANES), 'frame', sp...  47.6 us
    all_to_all x1, blocking collectives, shards(): lax.all_to_all(attended.reshape(frames, chunk, INNER), 'frame', split_axi...  25.1 us
    pallas_call x1, Pallas kernels, shards(): kernel_call(functools.partial(merge_kernel, cameras), [SMEM, SMEM, SMEM]...  13 us
    pallas_call x1, Pallas kernels, shards(): kernel_call(functools.partial(local_kernel, cameras), [SMEM, SMEM, VMEM,...  9.85 us
    pallas_call x1, Pallas kernels, shards(): kernel_call(functools.partial(time_kernel, frames), [VMEM] * 2, [spread((...  8.33 us
    ppermute x4, starting transfers between devices, passed_along(): return lax.ppermute(x, axis, [(i, (i + by) % peers) for i in range(peers)])  3.83 us
  transfers between devices with their start and end apart: 4, of which 1 were waited for; matrix products, arithmetic and copies ran while one was open for 2% of the time, Pallas kernels for 8%

profile of v1, /device:TPU:22, one launch (start us, length us, event | category | flops | bytes accessed | tf_op | source)
XLA Modules:
  0.0 116.9 jit_solution(14040996113639147752)
XLA Ops:
  0.0 0.0 copy-start.7
  0.0 0.0 copy-start.1
  0.0 0.0 copy-start.6
  0.0 0.0 copy-start.5
  0.0 1.4 %fusion = (s32[1,1]{0,1:T(1,128)}, s32[1,1]{0,1:T(1,128)}) fusion(s32[2,1]{0,1:T(1,128)} %param.9), kind=kLoop, calls=%fused_computation.3 | loop fusion | bytes 16 | tf_op jit(solution)/shard_map/slice | solution.py:220
  1.4 0.0 collective-permute-start
  1.4 3.2 %collective-permute-start.1 = (s32[1,1]{1,0:T(1,128)}, s32[1,1]{1,0:T(1,128)}, u32[]{:S(2)}, u32[]{:S(2)}) collective-permute-start(s32[1,1]{1,0:T(1,128)} %bitcast.1), channel_id=1, source_target_pairs={{0,192},{64,0},{128,64},{192,128},{1,193},{65,1},{129,65},{193,129... | collective-permute-start | bytes 20 | tf_op jit(solution)/shard_map/ppermute | solution.py:24
  4.6 1.3 %slice_bitcast_fusion = (bf16[256,1152]{1,0:T(8,128)(2,1)S(1)}, bf16[256,1152]{1,0:T(8,128)(2,1)S(1)}) fusion(bf16[2,1,256,1152]{3,2,1,0:T(8,128)(2,1)} %param.8), kind=kLoop, calls=%fused_computation | loop fusion | bytes 2359296 | tf_op jit(solution)/shard_map/squeeze | solution.py:223
  6.0 0.1 collective-permute-start.3
  6.1 0.5 collective-permute-start.2
  6.6 0.0 copy-done.7
  6.6 0.1 copy.12.counts_ref
  6.7 0.0 copy-done.6
  6.7 0.1 pad.9.side_ref
  6.7 0.0 copy-done.1
  6.7 0.0 copy-done.5
  6.8 0.0 copy-start.2
  6.8 2.1 %copy-done.2 = bf16[1152,1728]{0,1:T(8,128)(2,1)S(1)} copy-done((bf16[1152,1728]{0,1:T(8,128)(2,1)S(1)}, bf16[1152,1728]{0,1:T(8,128)(2,1)}, u32[]{:S(2)}) %copy-start.2) | copy-done | bytes 3981336
  8.9 0.0 copy-start.4
  8.9 9.8 %shard_map.82 = (bf16[512,640]{1,0:T(8,128)(2,1)S(1)}, f32[2,8,256,128]{3,2,1,0:T(8,128)S(1)}) custom-call(s32[2,1]{1,0:T(2,128)S(1)} %copy.12.counts_ref, s32[2,2]{1,0:T(2,128)S(1)} %copy-done.5, bf16[512,1152]{1,0:T(8,128)(2,1)S(1)} %bitcast.19, bf16[1728,1152]{1,0:T(8,128)(2,1)S(1)} %bitcast.22, f32[2,768]{1,0:T(2,128)S(1)} %pad.9.side_ref), custom_call_target="tpu_custom_call" | custom-call | flops 6000000000 | bytes 20000000 | tf_op jit(solution)/shard_map/pallas_call | solution.py:231
  18.7 0.0 collective-permute-done
  18.7 0.0 collective-permute-done.1
  18.8 1.2 %pad_add_fusion.far_counts_ref = s32[2,1]{1,0:T(2,128)S(1)} fusion(s32[1,1]{1,0:T(1,128)} %collective-permute-done.1, s32[1,1]{1,0:T(1,128)} %collective-permute-done), kind=kLoop, calls=%fused_computation.2 | loop fusion | flops 2 | bytes 16 | tf_op jit(solution)/shard_map/concatenate | solution.py:224
  19.9 0.0 collective-permute-done.3.upper_ref
  20.0 0.7 collective-permute-done.2.lower_ref
  20.6 0.0 copy-done.4
  20.6 0.0 copy-start.3
  20.6 13.0 %shard_map.83 = (bf16[512,1152]{1,0:T(8,128)(2,1)S(1)}, bf16[512,1280]{1,0:T(8,128)(2,1)S(1)}) custom-call(s32[2,1]{1,0:T(2,128)S(1)} %copy.12.counts_ref, s32[2,1]{1,0:T(2,128)S(1)} %pad_add_fusion.far_counts_ref, s32[2,2]{1,0:T(2,128)S(1)} %copy-done.5, bf16[512,1152]{1,0:T(8,128)(2,1)S(1)} %bitcast.20, ...), custom_call_target="tpu_custom_call" | custom-call | flops 4000000000 | bytes 12000000 | tf_op jit(solution)/shard_map/pallas_call | solution.py:241
  33.6 47.6 %all_to_all.10 = bf16[64,8,1280]{2,1,0:T(8,128)(2,1)S(1)} all-to-all(bf16[64,8,1280]{2,1,0:T(8,128)(2,1)S(1)} %bitcast.17), channel_id=1, replica_groups=mesh['cam'=4,'frame'=64] {'frame'}, dimensions={0} | all-to-all | bytes 2621440 | tf_op jit(solution)/shard_map/all_to_all | solution.py:252
  81.3 0.0 copy-done.3
  81.3 0.0 copy-start
  81.3 8.3 %shard_map.84 = bf16[512,576]{1,0:T(8,128)(2,1)S(1)} custom-call(bf16[512,1280]{1,0:T(8,128)(2,1)S(1)} %bitcast.18, bf16[1728,1152]{1,0:T(8,128)(2,1)S(1)} %bitcast.24), custom_call_target="tpu_custom_call" | custom-call | flops 6000000000 | bytes 10000000 | tf_op jit(solution)/shard_map/pallas_call | solution.py:255
  89.6 25.1 %all_to_all.11 = bf16[64,8,576]{2,1,0:T(8,128)(2,1)S(1)} all-to-all(bf16[64,8,576]{2,1,0:T(8,128)(2,1)S(1)} %bitcast.21), channel_id=1, replica_groups=mesh['cam'=4,'frame'=64] {'frame'}, dimensions={0} | all-to-all | bytes 1179648 | tf_op jit(solution)/shard_map/all_to_all | solution.py:264
  114.8 0.0 copy-done
  114.8 2.2 %shard_map.85 = bf16[512,1152]{1,0:T(8,128)(2,1)} custom-call(bf16[512,576]{1,0:T(8,128)(2,1)S(1)} %bitcast.16, bf16[576,1152]{1,0:T(8,128)(2,1)S(1)} %copy-done, bf16[512,1152]{1,0:T(8,128)(2,1)S(1)} %get-tuple-element.12.mixed_ref), custom_call_target="tpu_custom_call" | custom-call | flops 700000000 | bytes 4000000 | tf_op jit(solution)/shard_map/pallas_call | solution.py:267
  (1 shorter events, 0.0 us)
Async XLA Ops:
  0.0 6.6 %copy-start.7 = (s32[2,1]{0,1:T(1,128)S(1)}, s32[2,1]{0,1:T(1,128)}, u32[]{:S(2)}) copy-start(s32[2,1]{0,1:T(1,128)} %param.9) | copy-start | bytes 28
  0.0 6.7 %copy-start.1 = (bf16[2,1,256,1152]{3,2,1,0:T(8,128)(2,1)S(1)}, bf16[2,1,256,1152]{3,2,1,0:T(8,128)(2,1)}, u32[]{:S(2)}) copy-start(bf16[2,1,256,1152]{3,2,1,0:T(8,128)(2,1)} %param.8) | copy-start | bytes 3538948
  0.0 6.7 %copy-start.6 = (bf16[2,576]{1,0:T(2,128)(2,1)S(1)}, bf16[2,576]{1,0:T(2,128)(2,1)}, u32[]{:S(2)}) copy-start(bf16[2,576]{1,0:T(2,128)(2,1)} %param.11) | copy-start | bytes 6916
  0.0 6.7 %copy-start.5 = (s32[2,2]{1,0:T(2,128)S(1)}, s32[2,2]{1,0:T(2,128)}, u32[]{:S(2)}) copy-start(s32[2,2]{1,0:T(2,128)} %neighbours_ref.3) | copy-start | bytes 52
  1.4 17.4 %collective-permute-start = (s32[1,1]{1,0:T(1,128)}, s32[1,1]{1,0:T(1,128)}, u32[]{:S(2)}, u32[]{:S(2)}) collective-permute-start(s32[1,1]{1,0:T(1,128)} %bitcast), channel_id=1, source_target_pairs={{0,64},{64,128},{128,192},{192,0},{1,65},{65,129},{129,193},{193,1... | collective-permute-start | bytes 20 | tf_op jit(solution)/shard_map/ppermute | solution.py:24
  1.4 17.4 %collective-permute-start.1 = (s32[1,1]{1,0:T(1,128)}, s32[1,1]{1,0:T(1,128)}, u32[]{:S(2)}, u32[]{:S(2)}) collective-permute-start(s32[1,1]{1,0:T(1,128)} %bitcast.1), channel_id=1, source_target_pairs={{0,192},{64,0},{128,64},{192,128},{1,193},{65,1},{129,65},{193,129... | collective-permute-start | bytes 20 | tf_op jit(solution)/shard_map/ppermute | solution.py:24
  6.0 14.0 %collective-permute-start.3 = (bf16[256,1152]{1,0:T(8,128)(2,1)S(1)}, bf16[256,1152]{1,0:T(8,128)(2,1)S(1)}, u32[]{:S(2)}, u32[]{:S(2)}) collective-permute-start(bf16[256,1152]{1,0:T(8,128)(2,1)S(1)} %get-tuple-element.13), channel_id=1, source_target_pairs={{0,192},{64,0},{128,64},{192,128},{1,193},{65,1},{129,65},{193,129... | collective-permute-start | bytes 1769480 | tf_op jit(solution)/shard_map/ppermute | solution.py:24
  6.1 14.6 %collective-permute-start.2 = (bf16[256,1152]{1,0:T(8,128)(2,1)S(1)}, bf16[256,1152]{1,0:T(8,128)(2,1)S(1)}, u32[]{:S(2)}, u32[]{:S(2)}) collective-permute-start(bf16[256,1152]{1,0:T(8,128)(2,1)S(1)} %get-tuple-element.14), channel_id=1, source_target_pairs={{0,64},{64,128},{128,192},{192,0},{1,65},{65,129},{129,193},{193,1... | collective-permute-start | bytes 1769480 | tf_op jit(solution)/shard_map/ppermute | solution.py:24
  6.8 2.1 %copy-start.2 = (bf16[1152,1728]{0,1:T(8,128)(2,1)S(1)}, bf16[1152,1728]{0,1:T(8,128)(2,1)}, u32[]{:S(2)}) copy-start(bf16[1152,1728]{0,1:T(8,128)(2,1)} %param.12) | copy-start | bytes 11943940
  8.9 11.7 %copy-start.4 = (bf16[576,1152]{1,0:T(8,128)(2,1)S(1)}, bf16[576,1152]{1,0:T(8,128)(2,1)}, u32[]{:S(2)}) copy-start(bf16[576,1152]{1,0:T(8,128)(2,1)} %out_weight_ref.1) | copy-start | bytes 3981316
  20.6 60.6 %copy-start.3 = (bf16[1152,1728]{0,1:T(8,128)(2,1)S(1)}, bf16[1152,1728]{0,1:T(8,128)(2,1)}, u32[]{:S(2)}) copy-start(bf16[1152,1728]{0,1:T(8,128)(2,1)} %param.14) | copy-start | bytes 11943940
  81.3 33.5 %copy-start = (bf16[576,1152]{1,0:T(8,128)(2,1)S(1)}, bf16[576,1152]{1,0:T(8,128)(2,1)}, u32[]{:S(2)}) copy-start(bf16[576,1152]{1,0:T(8,128)(2,1)} %weight_ref.1) | copy-start | bytes 3981316

commit v2 on v1

v2 whole, which is shorter than its diff:
```python
import functools
import math

import jax
import jax.numpy as jnp
from jax import lax
from jax.experimental import pallas as pl
from jax.experimental.pallas import tpu as pltpu
from jax.sharding import PartitionSpec as P

HEADS = 8
HEAD = 72
INNER = HEADS * HEAD
EPS = 1e-06
ROW_TOKENS = 64
BIG = 1e30
COEF = HEAD ** (-0.5) * math.log2(math.e)
LANES = 128
KEY_LANES = 640
MIB = 1 << 20


def passed_along(x, axis, by):
    peers = lax.axis_size(axis)
    return lax.ppermute(x, axis, [(i, (i + by) % peers) for i in range(peers)])


def dot_nt(a, b):
    return lax.dot_general(a, b, (((1,), (1,)), ((), ())), preferred_element_type=jnp.float32)


def dot_nn(a, b):
    return lax.dot_general(a, b, (((1,), (0,)), ((), ())), preferred_element_type=jnp.float32)


def normalize(values):
    values = values.astype(jnp.float32)
    mean = jnp.mean(values, axis=-1, keepdims=True)
    centred = values - mean
    variance = jnp.mean(centred * centred, axis=-1, keepdims=True)
    return (centred * lax.rsqrt(variance + EPS)).astype(jnp.bfloat16)


def keys_bias(rows, count):
    position = lax.broadcasted_iota(jnp.int32, (rows, LANES), 0)
    return jnp.where(position < ROW_TOKENS * count, 0.0, -BIG).astype(jnp.bfloat16)


def key_window(keys, head, bias):
    window = keys[:, head * HEAD : head * HEAD + LANES]
    lane = lax.broadcasted_iota(jnp.int32, window.shape, 1)
    window = jnp.where(lane < HEAD, window, jnp.zeros_like(window))
    return window if bias is None else jnp.where(lane == HEAD, bias, window)


def one_then_zeros(rows, columns):
    return jnp.where(lax.broadcasted_iota(jnp.int32, (rows, columns), 0) == 0, 1.0, 0.0)


def head_rows(x, head):
    return x[head * HEAD : (head + 1) * HEAD, :]


def rounded(x):
    return x.astype(jnp.bfloat16).astype(jnp.float32)


def padded_keys(keys):
    fill = jnp.zeros((keys.shape[0], KEY_LANES - keys.shape[1]), jnp.float32)
    return jnp.concatenate([keys, fill], axis=1).astype(jnp.bfloat16)


def with_side(keys, side):
    return (keys.astype(jnp.float32) + side).astype(jnp.bfloat16)


def side_row(side_ref, neighbours_ref, cam, lower, cameras, cam_here):
    camera = lax.axis_index("cam") * cam_here + cam
    first_lower = neighbours_ref[cam, 0] == lax.rem(camera + cameras - 1, cameras)
    pick_first = first_lower if lower else jnp.logical_not(first_lower)
    return jnp.where(pick_first, side_ref[0:1, :], side_ref[1:2, :])


def staggered(items, score, rest, ahead):
    scores = [score(item) for item in items[:ahead]]
    for i, item in enumerate(items):
        if i + ahead < len(items):
            scores.append(score(items[i + ahead]))
        rest(item, scores[i])
        scores[i] = None


def norm_kernel(tokens_ref, first_ref, second_ref):
    rows = first_ref.shape[0]
    first_ref[...] = normalize(tokens_ref[:rows, :])
    second_ref[...] = normalize(tokens_ref[rows:, :])


def local_kernel(
    cameras, counts_ref, neighbours_ref, first_ref, second_ref, weight_ref, side_ref, query_ref, part_ref, value_ref
):
    rows = first_ref.shape[0]
    normed = jnp.concatenate([first_ref[...], second_ref[...]], axis=0)
    keys = padded_keys(dot_nt(normed, weight_ref[INNER : 2 * INNER, :]))
    query_ref[...] = rounded(dot_nt(weight_ref[:INNER, :], normed))
    value_ref[...] = rounded(dot_nt(weight_ref[2 * INNER :, :], normed))
    biases = [keys_bias(rows, counts_ref[c, 0]) for c in range(2)]
    one_rows = one_then_zeros(LANES - HEAD, rows)
    value_ones = one_then_zeros(8, 2 * rows)
    kept = []
    for c in range(2):
        own, other = slice(c * rows, (c + 1) * rows), slice((1 - c) * rows, (2 - c) * rows)
        side = side_row(side_ref, neighbours_ref, c, c == 1, cameras, 2)
        kept.append(
            (
                own,
                other,
                jnp.concatenate([keys[own], with_side(keys[other], side)], axis=0),
                jnp.concatenate([biases[c], biases[1 - c]], axis=0),
            )
        )

    def score(item):
        c, h = item
        own, _, k_all, bias = kept[c]
        q = jnp.concatenate([head_rows(query_ref[:, own], h), one_rows], axis=0).astype(jnp.bfloat16)
        return dot_nn(key_window(k_all, h, bias), q)

    def rest(item, scores):
        c, h = item
        own, other, _, _ = kept[c]
        highest = jnp.max(scores, axis=0, keepdims=True)
        expo = jnp.exp2((scores - highest) * COEF).astype(jnp.bfloat16)
        v = jnp.concatenate([head_rows(value_ref[:, own], h), head_rows(value_ref[:, other], h)], axis=1)
        summed = dot_nn(jnp.concatenate([v, value_ones], axis=0).astype(jnp.bfloat16), expo)
        row = lax.broadcasted_iota(jnp.int32, summed.shape, 0)
        part_ref[c, h] = jnp.where(row == HEAD + 1, highest, summed)

    staggered([(c, h) for c in range(2) for h in range(HEADS)], score, rest, 3)


def merge_kernel(
    cameras, counts_ref, lower_counts_ref, upper_counts_ref, neighbours_ref, tokens_ref, lower_ref, upper_ref, weight_ref,
    side_ref, query_ref, part_ref, out_weight_ref, mixed_ref, payload_ref, value_ref,
):
    rows = lower_ref.shape[0]
    far = jnp.concatenate([lower_ref[...], upper_ref[...]], axis=0)
    keys = padded_keys(dot_nt(far, weight_ref[INNER : 2 * INNER, :]))
    value_ref[...] = rounded(dot_nt(weight_ref[2 * INNER :, :], far))
    one_rows = one_then_zeros(LANES - HEAD, rows)
    value_ones = one_then_zeros(8, rows)
    far_counts = (lower_counts_ref[1, 0], upper_counts_ref[0, 0])
    kept = []
    for c in range(2):
        here = slice(c * rows, (c + 1) * rows)
        side = side_row(side_ref, neighbours_ref, c, c == 0, cameras, 2)
        kept.append((here, with_side(keys[here], side), keys_bias(rows, far_counts[c])))
    pieces = [[], []]

    def score(item):
        c, h = item
        here, k_all, bias = kept[c]
        q = jnp.concatenate([head_rows(query_ref[:, here], h), one_rows], axis=0).astype(jnp.bfloat16)
        return dot_nn(key_window(k_all, h, bias), q)

    def rest(item, scores):
        c, h = item
        here = kept[c][0]
        part = part_ref[c, h]
        before = part[HEAD + 1 : HEAD + 2, :]
        highest = jnp.maximum(jnp.max(scores, axis=0, keepdims=True), before)
        expo = jnp.exp2((scores - highest) * COEF).astype(jnp.bfloat16)
        v = jnp.concatenate([head_rows(value_ref[:, here], h), value_ones], axis=0).astype(jnp.bfloat16)
        summed = part * jnp.exp2((before - highest) * COEF) + dot_nn(v, expo)
        pieces[c].append(summed[:HEAD] * (1.0 / summed[HEAD : HEAD + 1]))

    staggered([(c, h) for c in range(2) for h in range(HEADS)], score, rest, 3)
    for c in range(2):
        here = slice(c * rows, (c + 1) * rows)
        attended = jnp.concatenate(pieces[c], axis=0).T.astype(jnp.bfloat16)
        mixed = dot_nn(attended, out_weight_ref[...]) + tokens_ref[here, :].astype(jnp.float32)
        mixed = mixed.astype(jnp.bfloat16)
        mixed_ref[here, :] = mixed
        width = mixed.shape[1]
        payload_ref[here, :width] = normalize(mixed)
        position = lax.broadcasted_iota(jnp.int32, (rows, LANES), 0)
        valid = position < ROW_TOKENS * counts_ref[c, 0]
        payload_ref[here, width:] = jnp.where(valid, 1.0, 0.0).astype(jnp.bfloat16)


def time_kernel(frames, payload_ref, weight_ref, out_ref, query_ref, value_ref):
    rows = payload_ref.shape[0]
    places = rows // frames
    model = weight_ref.shape[1]
    normed = payload_ref[:, :model]
    keys = padded_keys(dot_nt(normed, weight_ref[INNER : 2 * INNER, :]))
    query_ref[...] = rounded(dot_nt(weight_ref[:INNER, :], normed))
    value_ref[...] = rounded(dot_nt(weight_ref[2 * INNER :, :], normed))
    lane = lax.broadcasted_iota(jnp.int32, (rows, LANES), 1)
    key = lax.broadcasted_iota(jnp.int32, (rows, LANES), 0)
    invalid = payload_ref[:, model:].astype(jnp.float32) < 0.5
    key_mask = jnp.where(
        lane < frames,
        jnp.where(jnp.logical_and(invalid, lane != key // places), -BIG, 0.0),
        jnp.where(lane - frames == key % places, 1.0, 0.0),
    ).astype(jnp.bfloat16)
    entry = lax.broadcasted_iota(jnp.int32, (LANES, rows), 0)
    query = lax.broadcasted_iota(jnp.int32, (LANES, rows), 1)
    query_mask = jnp.where(
        entry < frames,
        jnp.where(entry == query // places, 1.0, 0.0),
        jnp.where(jnp.logical_and(entry < frames + places, entry - frames != query % places), -BIG, 0.0),
    ).astype(jnp.bfloat16)
    zero_rows = jnp.zeros((LANES - HEAD, rows), jnp.float32)
    value_ones = one_then_zeros(8, rows)
    block = 256
    blocks = rows // block
    pieces = [[] for _ in range(blocks)]

    def score(item):
        h, b = item
        here = slice(b * block, (b + 1) * block)
        q = jnp.concatenate([head_rows(query_ref[:, here], h), zero_rows[:, here]], axis=0).astype(jnp.bfloat16)
        return dot_nn(
            jnp.concatenate([key_window(keys, h, None), key_mask], axis=1),
            jnp.concatenate([q, query_mask[:, here]], axis=0),
        )

    def rest(item, scores):
        h, b = item
        highest = jnp.max(scores, axis=0, keepdims=True)
        expo = jnp.exp2((scores - highest) * COEF).astype(jnp.bfloat16)
        v = jnp.concatenate([head_rows(value_ref[...], h), value_ones], axis=0).astype(jnp.bfloat16)
        summed = dot_nn(v, expo)
        pieces[b].append(summed[:HEAD] * (1.0 / summed[HEAD : HEAD + 1]))

    staggered([(h, b) for h in range(HEADS) for b in range(blocks)], score, rest, 3)
    for b in range(blocks):
        out_ref[b * block : (b + 1) * block, :] = jnp.concatenate(pieces[b], axis=0).T.astype(jnp.bfloat16)


def final_kernel(attended_ref, weight_ref, mixed_ref, out_ref):
    result = dot_nn(attended_ref[...], weight_ref[...]) + mixed_ref[...].astype(jnp.float32)
    out_ref[...] = result.astype(jnp.bfloat16)


SMEM = pl.BlockSpec(memory_space=pltpu.SMEM)
VMEM = pl.BlockSpec(memory_space=pltpu.VMEM)


def kernel_call(body, ins, outs, scratch, mib, flops, nbytes):
    return pl.pallas_call(
        body,
        out_shape=outs,
        in_specs=ins,
        out_specs=[VMEM] * len(outs),
        scratch_shapes=scratch,
        compiler_params=pltpu.CompilerParams(vmem_limit_bytes=mib * MIB),
        cost_estimate=pl.CostEstimate(flops=flops, bytes_accessed=nbytes, transcendentals=0),
    )


def shards(tokens, counts, neighbours, side_keys, cross_qkv, cross_out, time_qkv, time_out):
    cam_here, frames_here, token_count, model = tokens.shape
    cameras = cam_here * lax.axis_size("cam")
    frames = lax.axis_size("frame")
    rows = cam_here * token_count
    bf16 = jnp.bfloat16
    spread = functools.partial(jax.ShapeDtypeStruct, dtype=bf16)

    flat = tokens.reshape(rows, model)
    cross_t, time_t = cross_qkv.T, time_qkv.T
    side = jnp.pad(side_keys.astype(jnp.float32), ((0, 0), (0, KEY_LANES - INNER)))

    first, second = kernel_call(
        norm_kernel, [VMEM], [spread((token_count, model))] * 2, [], 16, 5_000_000, 2_400_000
    )(flat)
    lower = passed_along(second, "cam", 1)
    upper = passed_along(first, "cam", -1)
    lower_counts = passed_along(counts, "cam", 1)
    upper_counts = passed_along(counts, "cam", -1)

    query, part = kernel_call(
        functools.partial(local_kernel, cameras),
        [SMEM, SMEM, VMEM, VMEM, VMEM, VMEM],
        [
            jax.ShapeDtypeStruct((INNER, rows), jnp.float32),
            jax.ShapeDtypeStruct((2, HEADS, HEAD + 8, token_count), jnp.float32),
        ],
        [pltpu.VMEM((INNER, rows), jnp.float32)],
        32,
        6_000_000_000,
        20_000_000,
    )(counts, neighbours, first, second, cross_t, side)

    mixed, payload = kernel_call(
        functools.partial(merge_kernel, cameras),
        [SMEM] * 4 + [VMEM] * 8,
        [spread((rows, model)), spread((rows, model + LANES))],
        [pltpu.VMEM((INNER, rows), jnp.float32)],
        32,
        4_000_000_000,
        12_000_000,
    )(counts, lower_counts, upper_counts, neighbours, flat, lower, upper, cross_t, side, query, part, cross_out)

    chunk = rows // frames
    arrived = lax.all_to_all(
        payload.reshape(frames, chunk, model + LANES), "frame", split_axis=0, concat_axis=0, tiled=True
    )
    (attended,) = kernel_call(
        functools.partial(time_kernel, frames),
        [VMEM] * 2,
        [spread((rows, INNER))],
        [pltpu.VMEM((INNER, rows), jnp.float32)] * 2,
        32,
        6_000_000_000,
        10_000_000,
    )(arrived.reshape(rows, model + LANES), time_t)
    returned = lax.all_to_all(
        attended.reshape(frames, chunk, INNER), "frame", split_axis=0, concat_axis=0, tiled=True
    )
    (out,) = kernel_call(
        final_kernel,
        [VMEM] * 3,
        [spread((rows, model))],
        [],
        32,
        700_000_000,
        4_000_000,
    )(returned.reshape(rows, INNER), time_out, mixed)
    return out.reshape(tokens.shape)


def solution(mesh):
    return jax.shard_map(
        shards,
        mesh=mesh,
        in_specs=(
            P("cam", "frame", None, None),
            P("cam", "frame"),
            P("cam", None),
            P(),
            P(),
            P(),
            P(),
            P(),
        ),
        out_specs=P("cam", "frame", None, None),
        check_vma=False,
    )
```

time: 119 us -> 108 us (0.908)
  Pallas kernels: 33.3 us -> 18.9 us
  waiting for transfers between devices: 0.67 us -> 3.33 us
  blocking collectives: 72.8 us -> 74.5 us
    pallas_call x1 -> x2, Pallas kernels: 13 us -> 6.05 us  [the longest x1 5.36 us: shards(): kernel_call(functools.partial(merge_kernel, cameras), [SMEM] * 4 + [VMEM]...]
    pallas_call x1, Pallas kernels: 9.85 us -> 5.5 us  [shards(): kernel_call(functools.partial(local_kernel, cameras), [SMEM, SMEM, VMEM,...]
    pallas_call x1, Pallas kernels: 8.33 us -> 5.19 us  [shards(): kernel_call(functools.partial(time_kernel, frames), [VMEM] * 2, [spread((...]
    ppermute x4, waiting for transfers between devices: 0.67 us -> 3.33 us  [passed_along(): return lax.ppermute(x, axis, [(i, (i + by) % peers) for i in range(peers)])]
    unnamed x17 -> x15, local copies, waits for them, and re-layouts: 2.25 us -> 4.83 us
    all_to_all x1, blocking collectives: 25.1 us -> 27.4 us  [shards(): lax.all_to_all(attended.reshape(frames, chunk, INNER), 'frame', split_axi...]
    slice x1 -> x0, local copies, waits for them, and re-layouts: 1.37 us -> none  [shards(): lower_count = passed_along(counts[-1:], 'cam', 1)]
    squeeze x1 -> x0, local copies, waits for them, and re-layouts: 1.33 us -> none  [shards(): upper = passed_along(tokens[0, 0], 'cam', -1)]
  transfers between devices with their start and end apart: 4 -> 4, of which waited for: 1 -> 2; matrix products, arithmetic and copies ran while one was open for 2% -> 1% of each run, Pallas kernels for 8% -> 6%
where the time goes in v2:
time: 108 us; the launch traced here: 106 us
  blocking collectives  74.5 us (69%)
  Pallas kernels  18.9 us (17%)
  local copies, waits for them, and re-layouts  4.83 us (4%)
  starting transfers between devices  3.84 us (4%)
  waiting for transfers between devices  3.33 us (3%)
    all_to_all x1, blocking collectives, shards(): lax.all_to_all(payload.reshape(frames, chunk, model + LANES), 'frame', sp...  47 us
    all_to_all x1, blocking collectives, shards(): lax.all_to_all(attended.reshape(frames, chunk, INNER), 'frame', split_axi...  27.4 us
    pallas_call x1, Pallas kernels, shards(): kernel_call(functools.partial(local_kernel, cameras), [SMEM, SMEM, VMEM,...  5.5 us
    pallas_call x1, Pallas kernels, shards(): kernel_call(functools.partial(merge_kernel, cameras), [SMEM] * 4 + [VMEM]...  5.36 us
    pallas_call x1, Pallas kernels, shards(): kernel_call(functools.partial(time_kernel, frames), [VMEM] * 2, [spread((...  5.19 us
    unnamed x15, local copies, waits for them, and re-layouts  4.83 us
    ppermute x4, starting transfers between devices, passed_along(): return lax.ppermute(x, axis, [(i, (i + by) % peers) for i in range(peers)])  3.84 us
    ppermute x4, waiting for transfers between devices, passed_along(): return lax.ppermute(x, axis, [(i, (i + by) % peers) for i in range(peers)])  3.33 us
  transfers between devices with their start and end apart: 4, of which 2 were waited for; matrix products, arithmetic and copies ran while one was open for 1% of the time, Pallas kernels for 6%

profile of v2, /device:TPU:22, one launch (start us, length us, event | category | flops | bytes accessed | tf_op | source)
XLA Modules:
  0.0 106.1 jit_solution(7711313222960780830)
XLA Ops:
  0.0 0.7 copy.12.counts_ref
  0.7 0.0 collective-permute-start.1
  0.7 0.5 collective-permute-start
  1.3 0.0 copy-start.1
  1.3 1.3 %copy-done.1 = bf16[2,1,256,1152]{3,2,1,0:T(8,128)(2,1)S(1)} copy-done((bf16[2,1,256,1152]{3,2,1,0:T(8,128)(2,1)S(1)}, bf16[2,1,256,1152]{3,2,1,0:T(8,128)(2,1)}, u32[]{:S(2)}) %copy-start.1) | copy-done | bytes 1179672
  2.5 0.7 shard_map.82
  3.2 2.7 %collective-permute-start.2 = (bf16[256,1152]{1,0:T(8,128)(2,1)S(1)}, bf16[256,1152]{1,0:T(8,128)(2,1)S(1)}, u32[]{:S(2)}, u32[]{:S(2)}) collective-permute-start(bf16[256,1152]{1,0:T(8,128)(2,1)S(1)} %get-tuple-element.11.second_ref), channel_id=1, source_target_pairs={{0,64},{64,128},{128,192},{192,0},{1,65},{65,129},{129,193},{193,1... | collective-permute-start | bytes 1769480 | tf_op jit(solution)/shard_map/ppermute | solution.py:25
  5.9 0.7 collective-permute-start.3
  6.5 0.7 pad_convert_fusion.side_ref
  7.2 0.0 copy-start.3
  7.2 2.1 %copy-done.3 = bf16[1152,1728]{0,1:T(8,128)(2,1)S(1)} copy-done((bf16[1152,1728]{0,1:T(8,128)(2,1)S(1)}, bf16[1152,1728]{0,1:T(8,128)(2,1)}, u32[]{:S(2)}) %copy-start.3) | copy-done | bytes 3981336
  9.4 0.0 copy-start.6
  9.4 0.7 copy-done.6
  10.0 0.0 copy-start.2
  10.0 0.0 copy-start.5
  10.0 5.5 %shard_map.83 = (f32[576,512]{1,0:T(8,128)S(1)}, f32[2,8,80,256]{3,2,1,0:T(8,128)S(1)}) custom-call(s32[2,1]{1,0:T(2,128)S(1)} %copy.12.counts_ref, s32[2,2]{1,0:T(2,128)S(1)} %copy-done.6, bf16[256,1152]{1,0:T(8,128)(2,1)S(1)} %get-tuple-element.12.first_ref, bf16[256,1152]{1,0:T(8,128)(2,1)S(1)} %get-tuple-element.11.second_ref, ...), custom_call_target="tpu_custom_call" | custom-call | flops 6000000000 | bytes 20000000 | tf_op jit(solution)/shard_map/pallas_call | solution.py:283
  15.6 0.0 collective-permute-done.1.upper_counts_ref
  15.6 0.0 collective-permute-done.lower_counts_ref
  15.6 1.8 %collective-permute-done.2.lower_ref = bf16[256,1152]{1,0:T(8,128)(2,1)S(1)} collective-permute-done((bf16[256,1152]{1,0:T(8,128)(2,1)S(1)}, bf16[256,1152]{1,0:T(8,128)(2,1)S(1)}, u32[]{:S(2)}, u32[]{:S(2)}) %collective-permute-start.2) | collective-permute-done | bytes 589856 | tf_op jit(solution)/shard_map/ppermute | solution.py:25
  17.3 1.6 %collective-permute-done.3.upper_ref = bf16[256,1152]{1,0:T(8,128)(2,1)S(1)} collective-permute-done((bf16[256,1152]{1,0:T(8,128)(2,1)S(1)}, bf16[256,1152]{1,0:T(8,128)(2,1)S(1)}, u32[]{:S(2)}, u32[]{:S(2)}) %collective-permute-start.3) | collective-permute-done | bytes 589856 | tf_op jit(solution)/shard_map/ppermute | solution.py:25
  18.9 0.0 copy-done.2
  18.9 0.0 copy-done.5
  18.9 0.0 copy-start.4
  18.9 5.4 %shard_map.84 = (bf16[512,1152]{1,0:T(8,128)(2,1)S(1)}, bf16[512,1280]{1,0:T(8,128)(2,1)S(1)}) custom-call(s32[2,1]{1,0:T(2,128)S(1)} %copy.12.counts_ref, s32[2,1]{1,0:T(2,128)S(1)} %collective-permute-done.lower_counts_ref, s32[2,1]{1,0:T(2,128)S(1)} %collective-permute-done.1.upper_counts_ref, s32[2,2]{1,0:T(2,128)S(1)} %copy-done.6, ...), custom_call_target="tpu_custom_call" | custom-call | flops 4000000000 | bytes 12000000 | tf_op jit(solution)/shard_map/pallas_call | solution.py:296
  24.3 47.0 %all_to_all.10 = bf16[64,8,1280]{2,1,0:T(8,128)(2,1)S(1)} all-to-all(bf16[64,8,1280]{2,1,0:T(8,128)(2,1)S(1)} %bitcast.11), channel_id=1, replica_groups=mesh['cam'=4,'frame'=64] {'frame'}, dimensions={0} | all-to-all | bytes 2621440 | tf_op jit(solution)/shard_map/all_to_all | solution.py:307
  71.3 0.0 copy-done.4
  71.3 0.0 copy-start
  71.3 5.2 %shard_map.85 = bf16[512,576]{1,0:T(8,128)(2,1)S(1)} custom-call(bf16[512,1280]{1,0:T(8,128)(2,1)S(1)} %bitcast.12, bf16[1728,1152]{1,0:T(8,128)(2,1)S(1)} %bitcast.18), custom_call_target="tpu_custom_call" | custom-call | flops 6000000000 | bytes 10000000 | tf_op jit(solution)/shard_map/pallas_call | solution.py:310
  76.5 27.4 %all_to_all.11 = bf16[64,8,576]{2,1,0:T(8,128)(2,1)S(1)} all-to-all(bf16[64,8,576]{2,1,0:T(8,128)(2,1)S(1)} %bitcast.15), channel_id=1, replica_groups=mesh['cam'=4,'frame'=64] {'frame'}, dimensions={0} | all-to-all | bytes 1179648 | tf_op jit(solution)/shard_map/all_to_all | solution.py:319
  103.9 0.0 copy-done
  103.9 2.2 %shard_map.86 = bf16[512,1152]{1,0:T(8,128)(2,1)} custom-call(bf16[512,576]{1,0:T(8,128)(2,1)S(1)} %bitcast.10, bf16[576,1152]{1,0:T(8,128)(2,1)S(1)} %copy-done, bf16[512,1152]{1,0:T(8,128)(2,1)S(1)} %get-tuple-element.16.mixed_ref), custom_call_target="tpu_custom_call" | custom-call | flops 700000000 | bytes 4000000 | tf_op jit(solution)/shard_map/pallas_call | solution.py:322
Async XLA Ops:
  0.7 14.8 %collective-permute-start.1 = (s32[2,1]{1,0:T(2,128)S(1)}, s32[2,1]{1,0:T(2,128)S(1)}, u32[]{:S(2)}, u32[]{:S(2)}) collective-permute-start(s32[2,1]{1,0:T(2,128)S(1)} %copy.12.counts_ref), channel_id=1, source_target_pairs={{0,192},{64,0},{128,64},{192,128},{1,193},{65,1},{129,65},{193,129... | collective-permute-start | bytes 32 | tf_op jit(solution)/shard_map/ppermute | solution.py:25
  0.7 14.8 %collective-permute-start = (s32[2,1]{1,0:T(2,128)S(1)}, s32[2,1]{1,0:T(2,128)S(1)}, u32[]{:S(2)}, u32[]{:S(2)}) collective-permute-start(s32[2,1]{1,0:T(2,128)S(1)} %copy.12.counts_ref), channel_id=1, source_target_pairs={{0,64},{64,128},{128,192},{192,0},{1,65},{65,129},{129,193},{193,1... | collective-permute-start | bytes 32 | tf_op jit(solution)/shard_map/ppermute | solution.py:25
  1.3 1.3 %copy-start.1 = (bf16[2,1,256,1152]{3,2,1,0:T(8,128)(2,1)S(1)}, bf16[2,1,256,1152]{3,2,1,0:T(8,128)(2,1)}, u32[]{:S(2)}) copy-start(bf16[2,1,256,1152]{3,2,1,0:T(8,128)(2,1)} %param.8) | copy-start | bytes 3538948
  3.2 14.1 %collective-permute-start.2 = (bf16[256,1152]{1,0:T(8,128)(2,1)S(1)}, bf16[256,1152]{1,0:T(8,128)(2,1)S(1)}, u32[]{:S(2)}, u32[]{:S(2)}) collective-permute-start(bf16[256,1152]{1,0:T(8,128)(2,1)S(1)} %get-tuple-element.11.second_ref), channel_id=1, source_target_pairs={{0,64},{64,128},{128,192},{192,0},{1,65},{65,129},{129,193},{193,1... | collective-permute-start | bytes 1769480 | tf_op jit(solution)/shard_map/ppermute | solution.py:25
  5.9 13.0 %collective-permute-start.3 = (bf16[256,1152]{1,0:T(8,128)(2,1)S(1)}, bf16[256,1152]{1,0:T(8,128)(2,1)S(1)}, u32[]{:S(2)}, u32[]{:S(2)}) collective-permute-start(bf16[256,1152]{1,0:T(8,128)(2,1)S(1)} %get-tuple-element.12.first_ref), channel_id=1, source_target_pairs={{0,192},{64,0},{128,64},{192,128},{1,193},{65,1},{129,65},{193,129... | collective-permute-start | bytes 1769480 | tf_op jit(solution)/shard_map/ppermute | solution.py:25
  7.2 2.1 %copy-start.3 = (bf16[1152,1728]{0,1:T(8,128)(2,1)S(1)}, bf16[1152,1728]{0,1:T(8,128)(2,1)}, u32[]{:S(2)}) copy-start(bf16[1152,1728]{0,1:T(8,128)(2,1)} %param.12) | copy-start | bytes 11943940
  9.4 0.7 copy-start.6
  10.0 8.9 %copy-start.2 = (bf16[2,1,256,1152]{3,2,1,0:T(8,128)(2,1)S(1)}, bf16[2,1,256,1152]{3,2,1,0:T(8,128)(2,1)}, u32[]{:S(2)}) copy-start(bf16[2,1,256,1152]{3,2,1,0:T(8,128)(2,1)} %param.8) | copy-start | bytes 3538948
  10.0 8.9 %copy-start.5 = (bf16[576,1152]{1,0:T(8,128)(2,1)S(1)}, bf16[576,1152]{1,0:T(8,128)(2,1)}, u32[]{:S(2)}) copy-start(bf16[576,1152]{1,0:T(8,128)(2,1)} %out_weight_ref.1) | copy-start | bytes 3981316
  18.9 52.4 %copy-start.4 = (bf16[1152,1728]{0,1:T(8,128)(2,1)S(1)}, bf16[1152,1728]{0,1:T(8,128)(2,1)}, u32[]{:S(2)}) copy-start(bf16[1152,1728]{0,1:T(8,128)(2,1)} %param.14) | copy-start | bytes 11943940
  71.3 32.6 %copy-start = (bf16[576,1152]{1,0:T(8,128)(2,1)S(1)}, bf16[576,1152]{1,0:T(8,128)(2,1)}, u32[]{:S(2)}) copy-start(bf16[576,1152]{1,0:T(8,128)(2,1)} %weight_ref.1) | copy-start | bytes 3981316

commit v3 on v2

--- a/solution.py
+++ b/solution.py
@@ -20,9 +20,26 @@
 MIB = 1 << 20
 
 
-def passed_along(x, axis, by):
-    peers = lax.axis_size(axis)
-    return lax.ppermute(x, axis, [(i, (i + by) % peers) for i in range(peers)])
+def to_owners(x):
+    return lax.all_to_all(x, "frame", split_axis=0, concat_axis=0, tiled=True)
+
+
+def cam_is_odd():
+    return lax.rem(lax.axis_index("cam"), 2)
+
+
+def exchange_pairs(peers):
+    inside, early, late = [], [], []
+    for i in range(0, peers, 2):
+        inside += [(i, i + 1), (i + 1, i)]
+        last = (i + peers - 1) % peers
+        (late if (i // 2) % 2 else early).extend([(last, i), (i, last)])
+    return inside, early, late
+
+
+def is_early():
+    peers = lax.axis_size("cam")
+    return lax.rem(lax.rem(lax.axis_index("cam") + 1, peers) // 2, 2) == 0
 
 
 def dot_nt(a, b):
@@ -42,7 +59,7 @@
 
 
 def keys_bias(rows, count):
-    position = lax.broadcasted_iota(jnp.int32, (rows, LANES), 0)
+    position = lax.broadcasted_iota(jnp.int32, (rows, LANES), 0).astype(jnp.float32)
     return jnp.where(position < ROW_TOKENS * count, 0.0, -BIG).astype(jnp.bfloat16)
 
 
@@ -74,11 +91,11 @@
     return (keys.astype(jnp.float32) + side).astype(jnp.bfloat16)
 
 
-def side_row(side_ref, neighbours_ref, cam, lower, cameras, cam_here):
+def side_row(side, neighbours_ref, cam, lower, cameras, cam_here):
     camera = lax.axis_index("cam") * cam_here + cam
     first_lower = neighbours_ref[cam, 0] == lax.rem(camera + cameras - 1, cameras)
     pick_first = first_lower if lower else jnp.logical_not(first_lower)
-    return jnp.where(pick_first, side_ref[0:1, :], side_ref[1:2, :])
+    return jnp.where(pick_first, side[0:1, :], side[1:2, :])
 
 
 def staggered(items, score, rest, ahead):
@@ -90,27 +107,41 @@
         scores[i] = None
 
 
-def norm_kernel(tokens_ref, first_ref, second_ref):
-    rows = first_ref.shape[0]
-    first_ref[...] = normalize(tokens_ref[:rows, :])
-    second_ref[...] = normalize(tokens_ref[rows:, :])
+def norm_kernel(counts_ref, tokens_ref, across_ref, inside_ref, normed_ref):
+    rows = normed_ref.shape[0] // 2
+    odd = cam_is_odd()
+    for cam, out_ref in ((odd, across_ref), (1 - odd, inside_ref)):
+        here = pl.ds(pl.multiple_of(cam * rows, rows), rows)
+        normed = normalize(tokens_ref[here, :])
+        out_ref[:rows, :] = normed
+        count = counts_ref[0, cam].astype(jnp.float32)
+        out_ref[rows:, :] = jnp.full((out_ref.shape[0] - rows, out_ref.shape[1]), count, jnp.float32).astype(jnp.bfloat16)
+        normed_ref[here, :] = normed
 
 
 def local_kernel(
-    cameras, counts_ref, neighbours_ref, first_ref, second_ref, weight_ref, side_ref, query_ref, part_ref, value_ref
+    cameras, counts_ref, neighbours_ref, normed_ref, weight_ref, side_ref, query_ref, part_ref, info_ref, value_ref
 ):
-    rows = first_ref.shape[0]
-    normed = jnp.concatenate([first_ref[...], second_ref[...]], axis=0)
+    rows = normed_ref.shape[0] // 2
+    normed = normed_ref[...]
     keys = padded_keys(dot_nt(normed, weight_ref[INNER : 2 * INNER, :]))
     query_ref[...] = rounded(dot_nt(weight_ref[:INNER, :], normed))
     value_ref[...] = rounded(dot_nt(weight_ref[2 * INNER :, :], normed))
-    biases = [keys_bias(rows, counts_ref[c, 0]) for c in range(2)]
+    sides = jnp.concatenate(
+        [side_ref[...].astype(jnp.float32), jnp.zeros((2, KEY_LANES - INNER), jnp.float32)], axis=1
+    )
+    counts = [counts_ref[0, c].astype(jnp.float32) for c in range(2)]
+    for c in range(2):
+        info_ref[c : c + 1, :] = side_row(sides, neighbours_ref, c, c == 0, cameras, 2)
+        info_ref[2 + c : 3 + c, :] = jnp.full((1, KEY_LANES), counts[c], jnp.float32)
+    info_ref[4:, :] = jnp.zeros((info_ref.shape[0] - 4, KEY_LANES), jnp.float32)
+    biases = [keys_bias(rows, counts[c]) for c in range(2)]
     one_rows = one_then_zeros(LANES - HEAD, rows)
     value_ones = one_then_zeros(8, 2 * rows)
     kept = []
     for c in range(2):
         own, other = slice(c * rows, (c + 1) * rows), slice((1 - c) * rows, (2 - c) * rows)
-        side = side_row(side_ref, neighbours_ref, c, c == 1, cameras, 2)
+        side = side_row(sides, neighbours_ref, c, c == 1, cameras, 2)
         kept.append(
             (
                 own,
@@ -140,21 +171,28 @@
 
 
 def merge_kernel(
-    cameras, counts_ref, lower_counts_ref, upper_counts_ref, neighbours_ref, tokens_ref, lower_ref, upper_ref, weight_ref,
-    side_ref, query_ref, part_ref, out_weight_ref, mixed_ref, payload_ref, value_ref,
+    early_ref, late_ref, inside_ref, weight_ref, info_ref, query_ref, part_ref, tokens_ref, out_weight_ref, mixed_ref,
+    payload_ref, far_ref, value_ref,
 ):
-    rows = lower_ref.shape[0]
-    far = jnp.concatenate([lower_ref[...], upper_ref[...]], axis=0)
+    rows = tokens_ref.shape[0] // 2
+    model = tokens_ref.shape[1]
+    odd, early = cam_is_odd(), is_early()
+    far_ref[pl.ds(pl.multiple_of(odd * rows, rows), rows), :] = jnp.where(early, early_ref[:rows, :], late_ref[:rows, :])
+    far_ref[pl.ds(pl.multiple_of((1 - odd) * rows, rows), rows), :] = inside_ref[:rows, :]
+    across_count = jnp.where(early, early_ref[rows : rows + 16, :LANES], late_ref[rows : rows + 16, :LANES])
+    inside_count = inside_ref[rows : rows + 16, :LANES]
+    even = odd == 0
+    far_counts = (jnp.where(even, across_count, inside_count), jnp.where(even, inside_count, across_count))
+    far = far_ref[...]
     keys = padded_keys(dot_nt(far, weight_ref[INNER : 2 * INNER, :]))
     value_ref[...] = rounded(dot_nt(weight_ref[2 * INNER :, :], far))
     one_rows = one_then_zeros(LANES - HEAD, rows)
     value_ones = one_then_zeros(8, rows)
-    far_counts = (lower_counts_ref[1, 0], upper_counts_ref[0, 0])
     kept = []
     for c in range(2):
         here = slice(c * rows, (c + 1) * rows)
-        side = side_row(side_ref, neighbours_ref, c, c == 0, cameras, 2)
-        kept.append((here, with_side(keys[here], side), keys_bias(rows, far_counts[c])))
+        bias = keys_bias(rows, far_counts[c].astype(jnp.float32)[:1, :])
+        kept.append((here, with_side(keys[here], info_ref[c : c + 1, :]), bias))
     pieces = [[], []]
 
     def score(item):
@@ -183,8 +221,8 @@
         mixed_ref[here, :] = mixed
         width = mixed.shape[1]
         payload_ref[here, :width] = normalize(mixed)
-        position = lax.broadcasted_iota(jnp.int32, (rows, LANES), 0)
-        valid = position < ROW_TOKENS * counts_ref[c, 0]
+        position = lax.broadcasted_iota(jnp.int32, (rows, LANES), 0).astype(jnp.float32)
+        valid = position < ROW_TOKENS * info_ref[2 + c : 3 + c, :LANES]
         payload_ref[here, width:] = jnp.where(valid, 1.0, 0.0).astype(jnp.bfloat16)
 
 
@@ -269,44 +307,51 @@
     spread = functools.partial(jax.ShapeDtypeStruct, dtype=bf16)
 
     flat = tokens.reshape(rows, model)
+    own_counts = counts.reshape(1, cam_here)
     cross_t, time_t = cross_qkv.T, time_qkv.T
-    side = jnp.pad(side_keys.astype(jnp.float32), ((0, 0), (0, KEY_LANES - INNER)))
-
-    first, second = kernel_call(
-        norm_kernel, [VMEM], [spread((token_count, model))] * 2, [], 16, 5_000_000, 2_400_000
-    )(flat)
-    lower = passed_along(second, "cam", 1)
-    upper = passed_along(first, "cam", -1)
-    lower_counts = passed_along(counts, "cam", 1)
-    upper_counts = passed_along(counts, "cam", -1)
-
-    query, part = kernel_call(
+    inside_pairs, early_pairs, late_pairs = exchange_pairs(lax.axis_size("cam"))
+    sent = token_count + 16
+
+    across, inside, normed = kernel_call(
+        norm_kernel,
+        [SMEM, VMEM],
+        [spread((sent, model))] * 2 + [spread((rows, model))],
+        [],
+        16,
+        6_000_000_000,
+        2_400_000,
+    )(own_counts, flat)
+    early_far = lax.ppermute(across, "cam", early_pairs)
+    inside_far = lax.ppermute(inside, "cam", inside_pairs)
+
+    query, part, info = kernel_call(
         functools.partial(local_kernel, cameras),
-        [SMEM, SMEM, VMEM, VMEM, VMEM, VMEM],
+        [SMEM, SMEM, VMEM, VMEM, VMEM],
         [
             jax.ShapeDtypeStruct((INNER, rows), jnp.float32),
             jax.ShapeDtypeStruct((2, HEADS, HEAD + 8, token_count), jnp.float32),
+            jax.ShapeDtypeStruct((8, KEY_LANES), jnp.float32),
         ],
         [pltpu.VMEM((INNER, rows), jnp.float32)],
         32,
         6_000_000_000,
         20_000_000,
-    )(counts, neighbours, first, second, cross_t, side)
+    )(own_counts, neighbours, normed, cross_t, side_keys)
+    across, query = lax.optimization_barrier((across, query))
+    late_far = lax.ppermute(across, "cam", late_pairs)
 
     mixed, payload = kernel_call(
-        functools.partial(merge_kernel, cameras),
-        [SMEM] * 4 + [VMEM] * 8,
+        merge_kernel,
+        [VMEM] * 9,
         [spread((rows, model)), spread((rows, model + LANES))],
-        [pltpu.VMEM((INNER, rows), jnp.float32)],
+        [pltpu.VMEM((rows, model), bf16), pltpu.VMEM((INNER, rows), jnp.float32)],
         32,
         4_000_000_000,
         12_000_000,
-    )(counts, lower_counts, upper_counts, neighbours, flat, lower, upper, cross_t, side, query, part, cross_out)
+    )(early_far, late_far, inside_far, cross_t, info, query, part, flat, cross_out)
 
     chunk = rows // frames
-    arrived = lax.all_to_all(
-        payload.reshape(frames, chunk, model + LANES), "frame", split_axis=0, concat_axis=0, tiled=True
-    )
+    arrived = to_owners(payload.reshape(frames, chunk, model + LANES))
     (attended,) = kernel_call(
         functools.partial(time_kernel, frames),
         [VMEM] * 2,
@@ -316,9 +361,7 @@
         6_000_000_000,
         10_000_000,
     )(arrived.reshape(rows, model + LANES), time_t)
-    returned = lax.all_to_all(
-        attended.reshape(frames, chunk, INNER), "frame", split_axis=0, concat_axis=0, tiled=True
-    )
+    returned = to_owners(attended.reshape(frames, chunk, INNER))
     (out,) = kernel_call(
         final_kernel,
         [VMEM] * 3,

time: 108 us -> 101 us (0.935)
  the two profiles are of different devices: /device:TPU:22 before, /device:TPU:1 now
where the time goes in v3:
time: 101 us
  blocking collectives  62.9 us (62%)
  Pallas kernels  18.8 us (19%)
  waiting for transfers between devices  10.1 us (10%)
  starting transfers between devices  7.01 us (7%)
  local copies, waits for them, and re-layouts  1.96 us (2%)
    all_to_all x2, blocking collectives, to_owners(): return lax.all_to_all(x, 'frame', split_axis=0, concat_axis=0, tiled=True)  62.9 us
    ppermute x1, waiting for transfers between devices, shards(): late_far = lax.ppermute(across, 'cam', late_pairs)  10.1 us
    pallas_call x1, Pallas kernels, shards(): kernel_call(functools.partial(local_kernel, cameras), [SMEM, SMEM, VMEM,...  5.47 us
    pallas_call x1, Pallas kernels, shards(): kernel_call(functools.partial(time_kernel, frames), [VMEM] * 2, [spread((...  5.19 us
    pallas_call x1, Pallas kernels, shards(): kernel_call(merge_kernel, [VMEM] * 9, [spread((rows, model)), spread((row...  4.72 us
    ppermute x1, starting transfers between devices, shards(): inside_far = lax.ppermute(inside, 'cam', inside_pairs)  3.33 us
    ppermute x1, starting transfers between devices, shards(): late_far = lax.ppermute(across, 'cam', late_pairs)  2.99 us
    pallas_call x1, Pallas kernels, shards(): kernel_call(final_kernel, [VMEM] * 3, [spread((rows, model))], [], 32, 70...  2.17 us
  transfers between devices with their start and end apart: 3, of which 1 were waited for; matrix products, arithmetic and copies ran while one was open for 0% of the time, Pallas kernels for 5%

profile of v3, /device:TPU:1, one launch (start us, length us, event | category | flops | bytes accessed | tf_op | source)
XLA Modules:
  0.0 100.9 jit_solution(14300059510316997907)
XLA Ops:
  0.0 0.0 copy-start.4
  0.0 1.3 %copy-done.4 = bf16[2,1,256,1152]{3,2,1,0:T(8,128)(2,1)S(1)} copy-done((bf16[2,1,256,1152]{3,2,1,0:T(8,128)(2,1)S(1)}, bf16[2,1,256,1152]{3,2,1,0:T(8,128)(2,1)}, u32[]{:S(2)}) %copy-start.4) | copy-done | bytes 1179672
  1.3 0.0 copy-start.8
  1.3 0.7 copy-done.8
  1.9 0.0 copy-start.1
  1.9 0.0 copy-start.6
  1.9 0.0 copy-start.7
  1.9 0.0 copy-start.9
  1.9 1.3 %shard_map.82 = (bf16[272,1152]{1,0:T(8,128)(2,1)S(1)}, bf16[272,1152]{1,0:T(8,128)(2,1)S(1)}, bf16[512,1152]{1,0:T(8,128)(2,1)S(1)}) custom-call(s32[1,2]{1,0:T(1,128)S(1)} %bitcast.20, bf16[512,1152]{1,0:T(8,128)(2,1)S(1)} %bitcast.18), custom_call_target="tpu_custom_call" | custom-call | flops 6000000000 | bytes 2400000 | tf_op jit(solution)/shard_map/pallas_call | solution.py:315
  3.2 3.3 %collective-permute-start.2 = (bf16[272,1152]{1,0:T(8,128)(2,1)S(1)}, bf16[272,1152]{1,0:T(8,128)(2,1)S(1)}, u32[]{:S(2)}, u32[]{:S(2)}) collective-permute-start(bf16[272,1152]{1,0:T(8,128)(2,1)S(1)} %get-tuple-element.19), channel_id=1, source_target_pairs={{0,64},{64,0},{128,192},{192,128},{1,65},{65,1},{129,193},{193,129... | collective-permute-start | bytes 1880072 | tf_op jit(solution)/shard_map/ppermute | solution.py:325
  6.5 0.7 collective-permute-start
  7.2 0.0 copy-done.1
  7.3 0.0 copy-done.6
  7.3 0.0 copy-done.7
  7.3 0.0 copy-done.9
  7.3 0.0 copy-start.3
  7.3 0.0 copy-start.5
  7.3 5.5 %shard_map.83 = (f32[576,512]{1,0:T(8,128)S(1)}, f32[2,8,80,256]{3,2,1,0:T(8,128)S(1)}, f32[8,640]{1,0:T(8,128)S(1)}) custom-call(s32[1,2]{1,0:T(1,128)S(1)} %bitcast.21, s32[2,2]{1,0:T(2,128)S(1)} %copy-done.7, bf16[512,1152]{1,0:T(8,128)(2,1)S(1)} %get-tuple-element.16.normed_ref, bf16[1728,1152]{1,0:T(8,128)(2,1)S(1)} %bitcast.15, ...), custom_call_target="tpu_custom_call" | custom-call | flops 6000000000 | bytes 20000000 | tf_op jit(solution)/shard_map/pallas_call | solution.py:327
  12.8 3.0 %collective-permute-start.1 = (bf16[272,1152]{1,0:T(8,128)(2,1)S(1)}, bf16[272,1152]{1,0:T(8,128)(2,1)S(1)}, u32[]{:S(2)}, u32[]{:S(2)}) collective-permute-start(bf16[272,1152]{1,0:T(8,128)(2,1)S(1)} %get-tuple-element.18), channel_id=1, source_target_pairs={{64,128},{128,64},{65,129},{129,65},{66,130},{130,66},{67,131},{13... | collective-permute-start | bytes 1880072 | tf_op jit(solution)/shard_map/ppermute | solution.py:341
  15.8 0.0 collective-permute-done.2.inside_ref
  15.8 0.0 collective-permute-done.early_ref
  15.8 10.1 %collective-permute-done.1.late_ref = bf16[272,1152]{1,0:T(8,128)(2,1)S(1)} collective-permute-done((bf16[272,1152]{1,0:T(8,128)(2,1)S(1)}, bf16[272,1152]{1,0:T(8,128)(2,1)S(1)}, u32[]{:S(2)}, u32[]{:S(2)}) %collective-permute-start.1) | collective-permute-done | bytes 626720 | tf_op jit(solution)/shard_map/ppermute | solution.py:341
  25.9 0.0 copy-done.3
  25.9 0.0 copy-done.5
  25.9 0.0 copy-start.2
  25.9 4.7 %shard_map.84 = (bf16[512,1152]{1,0:T(8,128)(2,1)S(1)}, bf16[512,1280]{1,0:T(8,128)(2,1)S(1)}) custom-call(bf16[272,1152]{1,0:T(8,128)(2,1)S(1)} %collective-permute-done.early_ref, bf16[272,1152]{1,0:T(8,128)(2,1)S(1)} %collective-permute-done.1.late_ref, bf16[272,1152]{1,0:T(8,128)(2,1)S(1)} %collective-permute-done.2.inside_ref, ...), custom_call_target="tpu_custom_call" | custom-call | flops 4000000000 | bytes 12000000 | tf_op jit(solution)/shard_map/pallas_call | solution.py:343
  30.6 39.7 %all_to_all.10 = bf16[64,8,1280]{2,1,0:T(8,128)(2,1)S(1)} all-to-all(bf16[64,8,1280]{2,1,0:T(8,128)(2,1)S(1)} %bitcast.12), channel_id=1, replica_groups=mesh['cam'=4,'frame'=64] {'frame'}, dimensions={0} | all-to-all | bytes 2621440 | tf_op jit(solution)/shard_map/all_to_all | solution.py:24
  70.3 0.0 copy-done.2
  70.3 0.0 copy-start
  70.3 5.2 %shard_map.85 = bf16[512,576]{1,0:T(8,128)(2,1)S(1)} custom-call(bf16[512,1280]{1,0:T(8,128)(2,1)S(1)} %bitcast.13, bf16[1728,1152]{1,0:T(8,128)(2,1)S(1)} %bitcast.17), custom_call_target="tpu_custom_call" | custom-call | flops 6000000000 | bytes 10000000 | tf_op jit(solution)/shard_map/pallas_call | solution.py:355
  75.5 23.2 %all_to_all.11 = bf16[64,8,576]{2,1,0:T(8,128)(2,1)S(1)} all-to-all(bf16[64,8,576]{2,1,0:T(8,128)(2,1)S(1)} %bitcast.14), channel_id=1, replica_groups=mesh['cam'=4,'frame'=64] {'frame'}, dimensions={0} | all-to-all | bytes 1179648 | tf_op jit(solution)/shard_map/all_to_all | solution.py:24
  98.7 0.0 copy-done
  98.7 2.2 %shard_map.86 = bf16[512,1152]{1,0:T(8,128)(2,1)} custom-call(bf16[512,576]{1,0:T(8,128)(2,1)S(1)} %bitcast.11, bf16[576,1152]{1,0:T(8,128)(2,1)S(1)} %copy-done, bf16[512,1152]{1,0:T(8,128)(2,1)S(1)} %get-tuple-element.24.mixed_ref), custom_call_target="tpu_custom_call" | custom-call | flops 700000000 | bytes 4000000 | tf_op jit(solution)/shard_map/pallas_call | solution.py:365
Async XLA Ops:
  0.0 1.3 %copy-start.4 = (bf16[2,1,256,1152]{3,2,1,0:T(8,128)(2,1)S(1)}, bf16[2,1,256,1152]{3,2,1,0:T(8,128)(2,1)}, u32[]{:S(2)}) copy-start(bf16[2,1,256,1152]{3,2,1,0:T(8,128)(2,1)} %param.8) | copy-start | bytes 3538948
  1.3 0.7 copy-start.8
  1.9 5.3 %copy-start.1 = (bf16[1152,1728]{0,1:T(8,128)(2,1)S(1)}, bf16[1152,1728]{0,1:T(8,128)(2,1)}, u32[]{:S(2)}) copy-start(bf16[1152,1728]{0,1:T(8,128)(2,1)} %param.12) | copy-start | bytes 11943940
  1.9 5.3 %copy-start.6 = (bf16[2,576]{1,0:T(2,128)(2,1)S(1)}, bf16[2,576]{1,0:T(2,128)(2,1)}, u32[]{:S(2)}) copy-start(bf16[2,576]{1,0:T(2,128)(2,1)} %side_ref.1) | copy-start | bytes 6916
  1.9 5.3 %copy-start.7 = (s32[2,2]{1,0:T(2,128)S(1)}, s32[2,2]{1,0:T(2,128)}, u32[]{:S(2)}) copy-start(s32[2,2]{1,0:T(2,128)} %neighbours_ref.1) | copy-start | bytes 52
  1.9 5.3 %copy-start.9 = (s32[2,1]{0,1:T(1,128)S(1)}, s32[2,1]{0,1:T(1,128)}, u32[]{:S(2)}) copy-start(s32[2,1]{0,1:T(1,128)} %param.9) | copy-start | bytes 28
  3.2 12.6 %collective-permute-start.2 = (bf16[272,1152]{1,0:T(8,128)(2,1)S(1)}, bf16[272,1152]{1,0:T(8,128)(2,1)S(1)}, u32[]{:S(2)}, u32[]{:S(2)}) collective-permute-start(bf16[272,1152]{1,0:T(8,128)(2,1)S(1)} %get-tuple-element.19), channel_id=1, source_target_pairs={{0,64},{64,0},{128,192},{192,128},{1,65},{65,1},{129,193},{193,129... | collective-permute-start | bytes 1880072 | tf_op jit(solution)/shard_map/ppermute | solution.py:325
  6.5 9.3 %collective-permute-start = (bf16[272,1152]{1,0:T(8,128)(2,1)S(1)}, bf16[272,1152]{1,0:T(8,128)(2,1)S(1)}, u32[]{:S(2)}, u32[]{:S(2)}) collective-permute-start(bf16[272,1152]{1,0:T(8,128)(2,1)S(1)} %get-tuple-element.18), channel_id=1, source_target_pairs={{192,0},{0,192},{193,1},{1,193},{194,2},{2,194},{195,3},{3,195},{1... | collective-permute-start | bytes 1880072 | tf_op jit(solution)/shard_map/ppermute | solution.py:324
  7.3 18.6 %copy-start.3 = (bf16[576,1152]{1,0:T(8,128)(2,1)S(1)}, bf16[576,1152]{1,0:T(8,128)(2,1)}, u32[]{:S(2)}) copy-start(bf16[576,1152]{1,0:T(8,128)(2,1)} %out_weight_ref.1) | copy-start | bytes 3981316
  7.3 18.6 %copy-start.5 = (bf16[2,1,256,1152]{3,2,1,0:T(8,128)(2,1)S(1)}, bf16[2,1,256,1152]{3,2,1,0:T(8,128)(2,1)}, u32[]{:S(2)}) copy-start(bf16[2,1,256,1152]{3,2,1,0:T(8,128)(2,1)} %param.8) | copy-start | bytes 3538948
  12.8 13.1 %collective-permute-start.1 = (bf16[272,1152]{1,0:T(8,128)(2,1)S(1)}, bf16[272,1152]{1,0:T(8,128)(2,1)S(1)}, u32[]{:S(2)}, u32[]{:S(2)}) collective-permute-start(bf16[272,1152]{1,0:T(8,128)(2,1)S(1)} %get-tuple-element.18), channel_id=1, source_target_pairs={{64,128},{128,64},{65,129},{129,65},{66,130},{130,66},{67,131},{13... | collective-permute-start | bytes 1880072 | tf_op jit(solution)/shard_map/ppermute | solution.py:341
  25.9 44.4 %copy-start.2 = (bf16[1152,1728]{0,1:T(8,128)(2,1)S(1)}, bf16[1152,1728]{0,1:T(8,128)(2,1)}, u32[]{:S(2)}) copy-start(bf16[1152,1728]{0,1:T(8,128)(2,1)} %param.14) | copy-start | bytes 11943940
  70.3 28.4 %copy-start = (bf16[576,1152]{1,0:T(8,128)(2,1)S(1)}, bf16[576,1152]{1,0:T(8,128)(2,1)}, u32[]{:S(2)}) copy-start(bf16[576,1152]{1,0:T(8,128)(2,1)} %weight_ref.1) | copy-start | bytes 3981316

commit v4 on v3

v4 whole, which is shorter than its diff:
```python
import functools
import math

import jax
import jax.numpy as jnp
from jax import lax
from jax.experimental import pallas as pl
from jax.experimental.pallas import tpu as pltpu
from jax.sharding import PartitionSpec as P

HEADS = 8
HEAD = 72
INNER = HEADS * HEAD
EPS = 1e-06
ROW_TOKENS = 64
BIG = 1e30
COEF = HEAD ** (-0.5) * math.log2(math.e)
LANES = 128
KEY_LANES = 640
MIB = 1 << 20


def to_owners(x):
    return lax.all_to_all(x, "frame", split_axis=0, concat_axis=0, tiled=True)


def cam_is_odd():
    return lax.rem(lax.axis_index("cam"), 2)


def exchange_pairs(peers):
    inside, early, late = [], [], []
    for i in range(0, peers, 2):
        inside += [(i, i + 1), (i + 1, i)]
        last = (i + peers - 1) % peers
        (late if (i // 2) % 2 else early).extend([(last, i), (i, last)])
    return inside, early, late


def is_early():
    peers = lax.axis_size("cam")
    return lax.rem(lax.rem(lax.axis_index("cam") + 1, peers) // 2, 2) == 0


def dot_nt(a, b):
    return lax.dot_general(a, b, (((1,), (1,)), ((), ())), preferred_element_type=jnp.float32)


def dot_nn(a, b):
    return lax.dot_general(a, b, (((1,), (0,)), ((), ())), preferred_element_type=jnp.float32)


def normalize(values):
    values = values.astype(jnp.float32)
    mean = jnp.mean(values, axis=-1, keepdims=True)
    centred = values - mean
    variance = jnp.mean(centred * centred, axis=-1, keepdims=True)
    return (centred * lax.rsqrt(variance + EPS)).astype(jnp.bfloat16)


def keys_bias(rows, count):
    position = lax.broadcasted_iota(jnp.int32, (rows, LANES), 0).astype(jnp.float32)
    return jnp.where(position < ROW_TOKENS * count, 0.0, -BIG).astype(jnp.bfloat16)


def key_window(keys, head, bias):
    window = keys[:, head * HEAD : head * HEAD + LANES]
    lane = lax.broadcasted_iota(jnp.int32, window.shape, 1)
    window = jnp.where(lane < HEAD, window, jnp.zeros_like(window))
    return window if bias is None else jnp.where(lane == HEAD, bias, window)


def one_then_zeros(rows, columns):
    return jnp.where(lax.broadcasted_iota(jnp.int32, (rows, columns), 0) == 0, 1.0, 0.0)


def head_rows(x, head):
    return x[head * HEAD : (head + 1) * HEAD, :]


def rounded(x):
    return x.astype(jnp.bfloat16).astype(jnp.float32)


def padded_keys(keys):
    fill = jnp.zeros((keys.shape[0], KEY_LANES - keys.shape[1]), jnp.float32)
    return jnp.concatenate([keys, fill], axis=1).astype(jnp.bfloat16)


def with_side(keys, side):
    return (keys.astype(jnp.float32) + side).astype(jnp.bfloat16)


def side_row(side, neighbours_ref, cam, lower, cameras, cam_here):
    camera = lax.axis_index("cam") * cam_here + cam
    first_lower = neighbours_ref[cam, 0] == lax.rem(camera + cameras - 1, cameras)
    return jnp.where(first_lower == lower, side[0:1, :], side[1:2, :])


def staggered(items, score, rest, ahead):
    scores = [score(item) for item in items[:ahead]]
    for i, item in enumerate(items):
        if i + ahead < len(items):
            scores.append(score(items[i + ahead]))
        rest(item, scores[i])
        scores[i] = None


def camera_rows(cam, rows):
    return pl.ds(pl.multiple_of(cam * rows, rows), rows)


def norm_kernel(counts_ref, tokens_ref, outer_ref, inner_ref):
    rows = tokens_ref.shape[0] // 2
    odd = cam_is_odd()
    for cam, out_ref in ((odd, outer_ref), (1 - odd, inner_ref)):
        out_ref[:rows, :] = normalize(tokens_ref[camera_rows(cam, rows), :])
        count = counts_ref[0, cam].astype(jnp.float32)
        out_ref[rows:, :] = jnp.full((out_ref.shape[0] - rows, out_ref.shape[1]), count, jnp.float32).astype(jnp.bfloat16)


def write_finished(i, pieces, tokens, out_weight_ref, info_ref, mixed_ref, payload_ref):
    attended = jnp.concatenate(pieces, axis=0).T.astype(jnp.bfloat16)
    mixed = (dot_nn(attended, out_weight_ref[...]) + tokens.astype(jnp.float32)).astype(jnp.bfloat16)
    rows, width = mixed.shape
    mixed_ref[...] = mixed
    payload_ref[:rows, :width] = normalize(mixed)
    position = lax.broadcasted_iota(jnp.int32, (rows, LANES), 0).astype(jnp.float32)
    valid = position < ROW_TOKENS * info_ref[2 + i : 3 + i, :LANES]
    payload_ref[:rows, width:] = jnp.where(valid, 1.0, 0.0).astype(jnp.bfloat16)


def local_kernel(
    cameras, counts_ref, neighbours_ref, outer_ref, inner_ref, far_ref, weight_ref, side_ref, tokens_ref, out_weight_ref,
    query_ref, part_ref, info_ref, mixed_ref, payload_ref, value_ref,
):
    rows = mixed_ref.shape[0]
    odd = cam_is_odd()
    cams = (odd, 1 - odd)
    normed = jnp.concatenate([outer_ref[:rows, :], inner_ref[:rows, :], far_ref[:rows, :]], axis=0)
    keys = padded_keys(dot_nt(normed, weight_ref[INNER : 2 * INNER, :]))
    query_ref[...] = rounded(dot_nt(weight_ref[:INNER, :], normed[: 2 * rows]))
    value_ref[...] = rounded(dot_nt(weight_ref[2 * INNER :, :], normed))
    sides = jnp.concatenate(
        [side_ref[...].astype(jnp.float32), jnp.zeros((2, KEY_LANES - INNER), jnp.float32)], axis=1
    )
    far_sides = [side_row(sides, neighbours_ref, cam, cam == 0, cameras, 2) for cam in cams]
    near_sides = [side_row(sides, neighbours_ref, cam, cam == 1, cameras, 2) for cam in cams]
    counts = [counts_ref[0, cam].astype(jnp.float32) for cam in cams]
    info_ref[0:1, :] = far_sides[0]
    info_ref[1:2, :] = far_sides[1]
    for i in range(2):
        info_ref[2 + i : 3 + i, :] = jnp.full((1, KEY_LANES), counts[i], jnp.float32)
    info_ref[4:, :] = jnp.zeros((info_ref.shape[0] - 4, KEY_LANES), jnp.float32)
    biases = [keys_bias(rows, count) for count in counts]
    far_bias = keys_bias(rows, far_ref[rows : rows + 16, :LANES].astype(jnp.float32)[:1])
    one_rows = one_then_zeros(LANES - HEAD, rows)
    value_ones = one_then_zeros(8, 3 * rows)
    outer, inner, far = (slice(i * rows, (i + 1) * rows) for i in range(3))
    kept = (
        (
            outer,
            (outer, inner),
            jnp.concatenate([keys[outer], with_side(keys[inner], near_sides[0])], axis=0),
            jnp.concatenate([biases[0], biases[1]], axis=0),
        ),
        (
            inner,
            (inner, outer, far),
            jnp.concatenate(
                [keys[inner], with_side(keys[outer], near_sides[1]), with_side(keys[far], far_sides[1])], axis=0
            ),
            jnp.concatenate([biases[1], biases[0], far_bias], axis=0),
        ),
    )
    pieces = []

    def score(item):
        i, h = item
        own, _, k_all, bias = kept[i]
        q = jnp.concatenate([head_rows(query_ref[:, own], h), one_rows], axis=0).astype(jnp.bfloat16)
        return dot_nn(key_window(k_all, h, bias), q)

    def rest(item, scores):
        i, h = item
        blocks = kept[i][1]
        highest = jnp.max(scores, axis=0, keepdims=True)
        expo = jnp.exp2((scores - highest) * COEF).astype(jnp.bfloat16)
        v = jnp.concatenate([head_rows(value_ref[:, block], h) for block in blocks], axis=1)
        v = jnp.concatenate([v, value_ones[:, : v.shape[1]]], axis=0).astype(jnp.bfloat16)
        summed = dot_nn(v, expo)
        if i == 0:
            row = lax.broadcasted_iota(jnp.int32, summed.shape, 0)
            part_ref[h] = jnp.where(row == HEAD + 1, highest, summed)
        else:
            pieces.append(summed[:HEAD] * (1.0 / summed[HEAD : HEAD + 1]))

    staggered([(i, h) for i in (1, 0) for h in range(HEADS)], score, rest, 3)
    tokens = tokens_ref[camera_rows(1 - odd, rows), :]
    write_finished(1, pieces, tokens, out_weight_ref, info_ref, mixed_ref, payload_ref)


def outer_kernel(
    early_ref, late_ref, weight_ref, info_ref, query_ref, part_ref, tokens_ref, out_weight_ref, inner_ref, mixed_ref,
    payload_ref, value_ref,
):
    rows = mixed_ref.shape[0]
    early = is_early()
    far = jnp.where(early, early_ref[:rows, :], late_ref[:rows, :])
    far_count = jnp.where(early, early_ref[rows : rows + 16, :LANES], late_ref[rows : rows + 16, :LANES])
    keys = padded_keys(dot_nt(far, weight_ref[INNER : 2 * INNER, :]))
    keys = with_side(keys, info_ref[0:1, :])
    value_ref[...] = rounded(dot_nt(weight_ref[2 * INNER :, :], far))
    payload_ref[rows:, :] = inner_ref[...]
    bias = keys_bias(rows, far_count.astype(jnp.float32)[:1])
    one_rows = one_then_zeros(LANES - HEAD, rows)
    value_ones = one_then_zeros(8, rows)
    pieces = []

    def score(h):
        q = jnp.concatenate([head_rows(query_ref[:, :rows], h), one_rows], axis=0).astype(jnp.bfloat16)
        return dot_nn(key_window(keys, h, bias), q)

    def rest(h, scores):
        part = part_ref[h]
        before = part[HEAD + 1 : HEAD + 2, :]
        highest = jnp.maximum(jnp.max(scores, axis=0, keepdims=True), before)
        expo = jnp.exp2((scores - highest) * COEF).astype(jnp.bfloat16)
        v = jnp.concatenate([head_rows(value_ref[...], h), value_ones], axis=0).astype(jnp.bfloat16)
        summed = part * jnp.exp2((before - highest) * COEF) + dot_nn(v, expo)
        pieces.append(summed[:HEAD] * (1.0 / summed[HEAD : HEAD + 1]))

    staggered(list(range(HEADS)), score, rest, 3)
    tokens = tokens_ref[camera_rows(cam_is_odd(), rows), :]
    write_finished(0, pieces, tokens, out_weight_ref, info_ref, mixed_ref, payload_ref)


def time_kernel(frames, payload_ref, weight_ref, out_ref, query_ref, value_ref):
    rows = payload_ref.shape[0]
    places = rows // frames
    model = weight_ref.shape[1]
    normed = payload_ref[:, :model]
    keys = padded_keys(dot_nt(normed, weight_ref[INNER : 2 * INNER, :]))
    query_ref[...] = rounded(dot_nt(weight_ref[:INNER, :], normed))
    value_ref[...] = rounded(dot_nt(weight_ref[2 * INNER :, :], normed))
    lane = lax.broadcasted_iota(jnp.int32, (rows, LANES), 1)
    key = lax.broadcasted_iota(jnp.int32, (rows, LANES), 0)
    invalid = payload_ref[:, model:].astype(jnp.float32) < 0.5
    key_mask = jnp.where(
        lane < frames,
        jnp.where(jnp.logical_and(invalid, lane != key // places), -BIG, 0.0),
        jnp.where(lane - frames == key % places, 1.0, 0.0),
    ).astype(jnp.bfloat16)
    entry = lax.broadcasted_iota(jnp.int32, (LANES, rows), 0)
    query = lax.broadcasted_iota(jnp.int32, (LANES, rows), 1)
    query_mask = jnp.where(
        entry < frames,
        jnp.where(entry == query // places, 1.0, 0.0),
        jnp.where(jnp.logical_and(entry < frames + places, entry - frames != query % places), -BIG, 0.0),
    ).astype(jnp.bfloat16)
    zero_rows = jnp.zeros((LANES - HEAD, rows), jnp.float32)
    value_ones = one_then_zeros(8, rows)
    block = 256
    blocks = rows // block
    pieces = [[] for _ in range(blocks)]

    def score(item):
        h, b = item
        here = slice(b * block, (b + 1) * block)
        q = jnp.concatenate([head_rows(query_ref[:, here], h), zero_rows[:, here]], axis=0).astype(jnp.bfloat16)
        return dot_nn(
            jnp.concatenate([key_window(keys, h, None), key_mask], axis=1),
            jnp.concatenate([q, query_mask[:, here]], axis=0),
        )

    def rest(item, scores):
        h, b = item
        highest = jnp.max(scores, axis=0, keepdims=True)
        expo = jnp.exp2((scores - highest) * COEF).astype(jnp.bfloat16)
        v = jnp.concatenate([head_rows(value_ref[...], h), value_ones], axis=0).astype(jnp.bfloat16)
        summed = dot_nn(v, expo)
        pieces[b].append(summed[:HEAD] * (1.0 / summed[HEAD : HEAD + 1]))

    staggered([(h, b) for h in range(HEADS) for b in range(blocks)], score, rest, 3)
    for b in range(blocks):
        out_ref[b * block : (b + 1) * block, :] = jnp.concatenate(pieces[b], axis=0).T.astype(jnp.bfloat16)


def final_kernel(attended_ref, weight_ref, outer_ref, inner_ref, out_hbm, block_ref, sems):
    rows = outer_ref.shape[0]
    size = block_ref.shape[1]
    odd = cam_is_odd()
    copies = []
    for i, (cam, mixed_ref) in enumerate(((odd, outer_ref), (1 - odd, inner_ref))):
        for start in range(0, rows, size):
            slot = len(copies)
            result = dot_nn(attended_ref[i * rows + start : i * rows + start + size, :], weight_ref[...])
            result = result + mixed_ref[start : start + size, :].astype(jnp.float32)
            block_ref[slot] = result.astype(jnp.bfloat16)
            there = pl.ds(pl.multiple_of(cam * rows + start, size), size)
            copies.append(pltpu.make_async_copy(block_ref.at[slot], out_hbm.at[there], sems.at[slot]))
            copies[-1].start()
    for copy in copies:
        copy.wait()


SMEM = pl.BlockSpec(memory_space=pltpu.SMEM)
VMEM = pl.BlockSpec(memory_space=pltpu.VMEM)
ANY = pl.BlockSpec(memory_space=pl.ANY)


def kernel_call(body, ins, outs, scratch, mib, flops, nbytes, out_space=VMEM):
    return pl.pallas_call(
        body,
        out_shape=outs,
        in_specs=ins,
        out_specs=[out_space] * len(outs),
        scratch_shapes=scratch,
        compiler_params=pltpu.CompilerParams(vmem_limit_bytes=mib * MIB),
        cost_estimate=pl.CostEstimate(flops=flops, bytes_accessed=nbytes, transcendentals=0),
    )


def shards(tokens, counts, neighbours, side_keys, cross_qkv, cross_out, time_qkv, time_out):
    cam_here, frames_here, token_count, model = tokens.shape
    cameras = cam_here * lax.axis_size("cam")
    frames = lax.axis_size("frame")
    rows = cam_here * token_count
    bf16 = jnp.bfloat16
    spread = functools.partial(jax.ShapeDtypeStruct, dtype=bf16)

    flat = tokens.reshape(rows, model)
    own_counts = counts.reshape(1, cam_here)
    cross_t, time_t = cross_qkv.T, time_qkv.T
    inside_pairs, early_pairs, late_pairs = exchange_pairs(lax.axis_size("cam"))
    sent = token_count + 16

    outer, inner = kernel_call(
        norm_kernel, [SMEM, VMEM], [spread((sent, model))] * 2, [], 16, 6_000_000_000, 2_400_000
    )(own_counts, flat)
    early_far = lax.ppermute(outer, "cam", early_pairs)
    inner_far = lax.ppermute(inner, "cam", inside_pairs)

    query, part, info, mixed_inner, payload_inner = kernel_call(
        functools.partial(local_kernel, cameras),
        [SMEM, SMEM] + [VMEM] * 7,
        [
            jax.ShapeDtypeStruct((INNER, rows), jnp.float32),
            jax.ShapeDtypeStruct((HEADS, HEAD + 8, token_count), jnp.float32),
            jax.ShapeDtypeStruct((8, KEY_LANES), jnp.float32),
            spread((token_count, model)),
            spread((token_count, model + LANES)),
        ],
        [pltpu.VMEM((INNER, rows + token_count), jnp.float32)],
        36,
        8_000_000_000,
        20_000_000,
    )(own_counts, neighbours, outer, inner, inner_far, cross_t, side_keys, flat, cross_out)
    outer, payload_inner = lax.optimization_barrier((outer, payload_inner))
    late_far = lax.ppermute(outer, "cam", late_pairs)
    mixed_outer, payload = kernel_call(
        outer_kernel,
        [VMEM] * 9,
        [spread((token_count, model)), spread((rows, model + LANES))],
        [pltpu.VMEM((INNER, token_count), jnp.float32)],
        32,
        2_500_000_000,
        8_000_000,
    )(early_far, late_far, cross_t, info, query, part, flat, cross_out, payload_inner)

    chunk = rows // frames
    arrived = to_owners(payload.reshape(frames, chunk, model + LANES))
    (attended,) = kernel_call(
        functools.partial(time_kernel, frames),
        [VMEM] * 2,
        [spread((rows, INNER))],
        [pltpu.VMEM((INNER, rows), jnp.float32)] * 2,
        32,
        6_000_000_000,
        10_000_000,
    )(arrived.reshape(rows, model + LANES), time_t)
    returned = to_owners(attended.reshape(frames, chunk, INNER))
    (out,) = kernel_call(
        final_kernel,
        [VMEM] * 4,
        [spread((rows, model))],
        [pltpu.VMEM((4, rows // 4, model), bf16), pltpu.SemaphoreType.DMA((4,))],
        32,
        700_000_000,
        4_000_000,
        ANY,
    )(returned.reshape(rows, INNER), time_out, mixed_outer, mixed_inner)
    return out.reshape(tokens.shape)


def solution(mesh):
    return jax.shard_map(
        shards,
        mesh=mesh,
        in_specs=(
            P("cam", "frame", None, None),
            P("cam", "frame"),
            P("cam", None),
            P(),
            P(),
            P(),
            P(),
            P(),
        ),
        out_specs=P("cam", "frame", None, None),
        check_vma=False,
    )
```

time: 101 us -> 96.5 us (0.955)
  the two profiles are of different devices: /device:TPU:1 before, /device:TPU:22 now
where the time goes in v4:
time: 96.5 us; the launch traced here: 95 us
  blocking collectives  58.1 us (60%)
  Pallas kernels  19.5 us (20%)
  waiting for transfers between devices  12.3 us (13%)
  starting transfers between devices  2.9 us (3%)
  local copies, waits for them, and re-layouts  1.96 us (2%)
    all_to_all x2, blocking collectives, to_owners(): return lax.all_to_all(x, 'frame', split_axis=0, concat_axis=0, tiled=True)  58.1 us
    ppermute x1, waiting for transfers between devices, shards(): late_far = lax.ppermute(outer, 'cam', late_pairs)  11.1 us
    pallas_call x1, Pallas kernels, shards(): kernel_call(functools.partial(local_kernel, cameras), [SMEM, SMEM] + [VME...  8.11 us
    pallas_call x1, Pallas kernels, shards(): kernel_call(functools.partial(time_kernel, frames), [VMEM] * 2, [spread((...  5.21 us
    pallas_call x1, Pallas kernels, shards(): kernel_call(outer_kernel, [VMEM] * 9, [spread((token_count, model)), spre...  2.98 us
    ppermute x1, starting transfers between devices, shards(): late_far = lax.ppermute(outer, 'cam', late_pairs)  1.98 us
    unnamed x20, local copies, waits for them, and re-layouts  1.96 us
    pallas_call x1, Pallas kernels, shards(): kernel_call(final_kernel, [VMEM] * 4, [spread((rows, model))], [pltpu.VME...  1.94 us
  transfers between devices with their start and end apart: 3, of which 2 were waited for; matrix products, arithmetic and copies ran while one was open for 0% of the time, Pallas kernels for 9%

profile of v4, /device:TPU:22, one launch (start us, length us, event | category | flops | bytes accessed | tf_op | source)
XLA Modules:
  0.0 95.0 jit_solution(10396720592392863632)
XLA Ops:
  0.0 0.0 copy-start.3
  0.0 1.3 %copy-done.3 = bf16[2,1,256,1152]{3,2,1,0:T(8,128)(2,1)S(1)} copy-done((bf16[2,1,256,1152]{3,2,1,0:T(8,128)(2,1)S(1)}, bf16[2,1,256,1152]{3,2,1,0:T(8,128)(2,1)}, u32[]{:S(2)}) %copy-start.3) | copy-done | bytes 1179672
  1.3 0.0 copy-start.8
  1.3 0.7 copy-done.8
  1.9 0.0 copy-start
  1.9 0.0 copy-start.2
  1.9 0.0 copy-start.4
  1.9 0.0 copy-start.6
  1.9 0.0 copy-start.7
  1.9 0.0 copy-start.9
  2.0 1.2 %shard_map.82 = (bf16[272,1152]{1,0:T(8,128)(2,1)S(1)}, bf16[272,1152]{1,0:T(8,128)(2,1)S(1)}) custom-call(s32[1,2]{1,0:T(1,128)S(1)} %bitcast.21, bf16[512,1152]{1,0:T(8,128)(2,1)S(1)} %bitcast.16), custom_call_target="tpu_custom_call" | custom-call | flops 6000000000 | bytes 2400000 | tf_op jit(solution)/shard_map/pallas_call | solution.py:338
  3.2 0.1 collective-permute-start.1
  3.3 0.8 collective-permute-start
  4.2 1.2 %collective-permute-done.1.far_ref = bf16[272,1152]{1,0:T(8,128)(2,1)S(1)} collective-permute-done((bf16[272,1152]{1,0:T(8,128)(2,1)S(1)}, bf16[272,1152]{1,0:T(8,128)(2,1)S(1)}, u32[]{:S(2)}, u32[]{:S(2)}) %collective-permute-start.1) | collective-permute-done | bytes 626720 | tf_op jit(solution)/shard_map/ppermute | solution.py:342
  5.4 0.0 copy-done
  5.4 0.0 copy-done.2
  5.4 0.0 copy-done.4
  5.4 0.0 copy-done.6
  5.4 0.0 copy-done.7
  5.4 0.0 copy-done.9
  5.4 8.1 %shard_map.83 = (f32[576,512]{1,0:T(8,128)S(1)}, f32[8,80,256]{2,1,0:T(8,128)S(1)}, f32[8,640]{1,0:T(8,128)S(1)}, bf16[256,1152]{1,0:T(8,128)(2,1)S(1)}, bf16[256,1280]{1,0:T(8,128)(2,1)S(1)}) custom-call(s32[1,2]{1,0:T(1,128)S(1)} %bitcast.22, s32[2,2]{1,0:T(2,128)S(1)} %copy-done.7, bf16[272,1152]{1,0:T(8,128)(2,1)S(1)} %get-tuple-element.19.outer_ref, ...), custom_call_target="tpu_custom_call" | custom-call | flops 8000000000 | bytes 20000000 | tf_op jit(solution)/shard_map/pallas_call | solution.py:344
  13.5 2.0 %collective-permute-start.2 = (bf16[272,1152]{1,0:T(8,128)(2,1)S(1)}, bf16[272,1152]{1,0:T(8,128)(2,1)S(1)}, u32[]{:S(2)}, u32[]{:S(2)}) collective-permute-start(bf16[272,1152]{1,0:T(8,128)(2,1)S(1)} %get-tuple-element.19.outer_ref), channel_id=1, source_target_pairs={{64,128},{128,64},{65,129},{129,65},{66,130},{130,66},{67,131},{13... | collective-permute-start | bytes 1880072 | tf_op jit(solution)/shard_map/ppermute | solution.py:360
  15.5 0.0 collective-permute-done.early_ref
  15.5 11.1 %collective-permute-done.2.late_ref = bf16[272,1152]{1,0:T(8,128)(2,1)S(1)} collective-permute-done((bf16[272,1152]{1,0:T(8,128)(2,1)S(1)}, bf16[272,1152]{1,0:T(8,128)(2,1)S(1)}, u32[]{:S(2)}, u32[]{:S(2)}) %collective-permute-start.2) | collective-permute-done | bytes 626720 | tf_op jit(solution)/shard_map/ppermute | solution.py:360
  26.6 0.0 copy-start.5
  26.6 3.0 %shard_map.84 = (bf16[256,1152]{1,0:T(8,128)(2,1)S(1)}, bf16[512,1280]{1,0:T(8,128)(2,1)S(1)}) custom-call(bf16[272,1152]{1,0:T(8,128)(2,1)S(1)} %collective-permute-done.early_ref, bf16[272,1152]{1,0:T(8,128)(2,1)S(1)} %collective-permute-done.2.late_ref, bf16[1728,1152]{1,0:T(8,128)(2,1)S(1)} %bitcast.12, f32[8,640]{1,0:T(8,128)S(1)} %get-tuple-element.20.info_ref, ...), custom_call_target="tpu_custom_call" | custom-call | flops 2500000000 | bytes 8000000 | tf_op jit(solution)/shard_map/pallas_call | solution.py:361
  29.6 37.0 %all_to_all.10 = bf16[64,8,1280]{2,1,0:T(8,128)(2,1)S(1)} all-to-all(bf16[64,8,1280]{2,1,0:T(8,128)(2,1)S(1)} %bitcast.14), channel_id=1, replica_groups=mesh['cam'=4,'frame'=64] {'frame'}, dimensions={0} | all-to-all | bytes 2621440 | tf_op jit(solution)/shard_map/all_to_all | solution.py:24
  66.6 0.0 copy-done.5
  66.6 0.0 copy-start.1
  66.6 5.2 %shard_map.85 = bf16[512,576]{1,0:T(8,128)(2,1)S(1)} custom-call(bf16[512,1280]{1,0:T(8,128)(2,1)S(1)} %bitcast.15, bf16[1728,1152]{1,0:T(8,128)(2,1)S(1)} %bitcast.20), custom_call_target="tpu_custom_call" | custom-call | flops 6000000000 | bytes 10000000 | tf_op jit(solution)/shard_map/pallas_call | solution.py:373
  71.8 21.1 %all_to_all.11 = bf16[64,8,576]{2,1,0:T(8,128)(2,1)S(1)} all-to-all(bf16[64,8,576]{2,1,0:T(8,128)(2,1)S(1)} %bitcast.19), channel_id=1, replica_groups=mesh['cam'=4,'frame'=64] {'frame'}, dimensions={0} | all-to-all | bytes 1179648 | tf_op jit(solution)/shard_map/all_to_all | solution.py:24
  92.9 0.0 copy-done.1
  92.9 1.9 %shard_map.86 = bf16[512,1152]{1,0:T(8,128)(2,1)} custom-call(bf16[512,576]{1,0:T(8,128)(2,1)S(1)} %bitcast.13, bf16[576,1152]{1,0:T(8,128)(2,1)S(1)} %copy-done.1, bf16[256,1152]{1,0:T(8,128)(2,1)S(1)} %get-tuple-element.25.outer_ref, bf16[256,1152]{1,0:T(8,128)(2,1)S(1)} %get-tuple-element.26.inner_ref), custom_call_target="tpu_custom_call" | custom-call | flops 700000000 | bytes 4000000 | tf_op jit(solution)/shard_map/pallas_call | solution.py:383
Async XLA Ops:
  0.0 1.3 %copy-start.3 = (bf16[2,1,256,1152]{3,2,1,0:T(8,128)(2,1)S(1)}, bf16[2,1,256,1152]{3,2,1,0:T(8,128)(2,1)}, u32[]{:S(2)}) copy-start(bf16[2,1,256,1152]{3,2,1,0:T(8,128)(2,1)} %param.8) | copy-start | bytes 3538948
  1.3 0.7 copy-start.8
  1.9 3.4 %copy-start = (bf16[1152,1728]{0,1:T(8,128)(2,1)S(1)}, bf16[1152,1728]{0,1:T(8,128)(2,1)}, u32[]{:S(2)}) copy-start(bf16[1152,1728]{0,1:T(8,128)(2,1)} %param.12) | copy-start | bytes 11943940
  1.9 3.4 %copy-start.2 = (bf16[576,1152]{1,0:T(8,128)(2,1)S(1)}, bf16[576,1152]{1,0:T(8,128)(2,1)}, u32[]{:S(2)}) copy-start(bf16[576,1152]{1,0:T(8,128)(2,1)} %out_weight_ref.3) | copy-start | bytes 3981316
  1.9 3.4 %copy-start.4 = (bf16[2,1,256,1152]{3,2,1,0:T(8,128)(2,1)S(1)}, bf16[2,1,256,1152]{3,2,1,0:T(8,128)(2,1)}, u32[]{:S(2)}) copy-start(bf16[2,1,256,1152]{3,2,1,0:T(8,128)(2,1)} %param.8) | copy-start | bytes 3538948
  1.9 3.4 %copy-start.6 = (bf16[2,576]{1,0:T(2,128)(2,1)S(1)}, bf16[2,576]{1,0:T(2,128)(2,1)}, u32[]{:S(2)}) copy-start(bf16[2,576]{1,0:T(2,128)(2,1)} %side_ref.1) | copy-start | bytes 6916
  1.9 3.4 %copy-start.7 = (s32[2,2]{1,0:T(2,128)S(1)}, s32[2,2]{1,0:T(2,128)}, u32[]{:S(2)}) copy-start(s32[2,2]{1,0:T(2,128)} %neighbours_ref.1) | copy-start | bytes 52
  1.9 3.4 %copy-start.9 = (s32[2,1]{0,1:T(1,128)S(1)}, s32[2,1]{0,1:T(1,128)}, u32[]{:S(2)}) copy-start(s32[2,1]{0,1:T(1,128)} %param.9) | copy-start | bytes 28
  3.2 2.1 %collective-permute-start.1 = (bf16[272,1152]{1,0:T(8,128)(2,1)S(1)}, bf16[272,1152]{1,0:T(8,128)(2,1)S(1)}, u32[]{:S(2)}, u32[]{:S(2)}) collective-permute-start(bf16[272,1152]{1,0:T(8,128)(2,1)S(1)} %get-tuple-element.17.inner_ref), channel_id=1, source_target_pairs={{0,64},{64,0},{128,192},{192,128},{1,65},{65,1},{129,193},{193,129... | collective-permute-start | bytes 1880072 | tf_op jit(solution)/shard_map/ppermute | solution.py:342
  3.3 12.2 %collective-permute-start = (bf16[272,1152]{1,0:T(8,128)(2,1)S(1)}, bf16[272,1152]{1,0:T(8,128)(2,1)S(1)}, u32[]{:S(2)}, u32[]{:S(2)}) collective-permute-start(bf16[272,1152]{1,0:T(8,128)(2,1)S(1)} %get-tuple-element.19.outer_ref), channel_id=1, source_target_pairs={{192,0},{0,192},{193,1},{1,193},{194,2},{2,194},{195,3},{3,195},{1... | collective-permute-start | bytes 1880072 | tf_op jit(solution)/shard_map/ppermute | solution.py:341
  13.5 13.1 %collective-permute-start.2 = (bf16[272,1152]{1,0:T(8,128)(2,1)S(1)}, bf16[272,1152]{1,0:T(8,128)(2,1)S(1)}, u32[]{:S(2)}, u32[]{:S(2)}) collective-permute-start(bf16[272,1152]{1,0:T(8,128)(2,1)S(1)} %get-tuple-element.19.outer_ref), channel_id=1, source_target_pairs={{64,128},{128,64},{65,129},{129,65},{66,130},{130,66},{67,131},{13... | collective-permute-start | bytes 1880072 | tf_op jit(solution)/shard_map/ppermute | solution.py:360
  26.6 40.0 %copy-start.5 = (bf16[1152,1728]{0,1:T(8,128)(2,1)S(1)}, bf16[1152,1728]{0,1:T(8,128)(2,1)}, u32[]{:S(2)}) copy-start(bf16[1152,1728]{0,1:T(8,128)(2,1)} %param.14) | copy-start | bytes 11943940
  66.6 26.3 %copy-start.1 = (bf16[576,1152]{1,0:T(8,128)(2,1)S(1)}, bf16[576,1152]{1,0:T(8,128)(2,1)}, u32[]{:S(2)}) copy-start(bf16[576,1152]{1,0:T(8,128)(2,1)} %weight_ref.1) | copy-start | bytes 3981316

commit v5 on v4

--- a/solution.py
+++ b/solution.py
@@ -235,55 +235,62 @@
     write_finished(0, pieces, tokens, out_weight_ref, info_ref, mixed_ref, payload_ref)
 
 
+def swap_halves(first, second):
+    upper = lax.broadcasted_iota(jnp.int32, first.shape, 1) < 4
+    return jnp.where(upper, first, pltpu.roll(second, 4, 1)), jnp.where(upper, pltpu.roll(first, 4, 1), second)
+
+
 def time_kernel(frames, payload_ref, weight_ref, out_ref, query_ref, value_ref):
-    rows = payload_ref.shape[0]
-    places = rows // frames
+    rows, lanes = payload_ref.shape
     model = weight_ref.shape[1]
-    normed = payload_ref[:, :model]
+    half = rows // 2
+    places = half // frames
+    pairs = payload_ref[...].astype(jnp.float32).reshape(frames // 2, 2, 2 * places, lanes)
+    low, high = swap_halves(pairs[:, 0], pairs[:, 1])
+    payload = jnp.concatenate([low.reshape(half, lanes), high.reshape(half, lanes)], axis=0).astype(jnp.bfloat16)
+    normed = payload[:, :model]
     keys = padded_keys(dot_nt(normed, weight_ref[INNER : 2 * INNER, :]))
     query_ref[...] = rounded(dot_nt(weight_ref[:INNER, :], normed))
     value_ref[...] = rounded(dot_nt(weight_ref[2 * INNER :, :], normed))
     lane = lax.broadcasted_iota(jnp.int32, (rows, LANES), 1)
-    key = lax.broadcasted_iota(jnp.int32, (rows, LANES), 0)
-    invalid = payload_ref[:, model:].astype(jnp.float32) < 0.5
+    key = lax.rem(lax.broadcasted_iota(jnp.int32, (rows, LANES), 0), half)
+    invalid = payload[:, model:].astype(jnp.float32) < 0.5
     key_mask = jnp.where(
         lane < frames,
         jnp.where(jnp.logical_and(invalid, lane != key // places), -BIG, 0.0),
         jnp.where(lane - frames == key % places, 1.0, 0.0),
     ).astype(jnp.bfloat16)
-    entry = lax.broadcasted_iota(jnp.int32, (LANES, rows), 0)
-    query = lax.broadcasted_iota(jnp.int32, (LANES, rows), 1)
+    entry = lax.broadcasted_iota(jnp.int32, (LANES, half), 0)
+    query = lax.broadcasted_iota(jnp.int32, (LANES, half), 1)
     query_mask = jnp.where(
         entry < frames,
         jnp.where(entry == query // places, 1.0, 0.0),
         jnp.where(jnp.logical_and(entry < frames + places, entry - frames != query % places), -BIG, 0.0),
     ).astype(jnp.bfloat16)
-    zero_rows = jnp.zeros((LANES - HEAD, rows), jnp.float32)
-    value_ones = one_then_zeros(8, rows)
-    block = 256
-    blocks = rows // block
-    pieces = [[] for _ in range(blocks)]
+    zero_rows = jnp.zeros((LANES - HEAD, half), jnp.float32)
+    value_ones = one_then_zeros(8, half)
+    pieces = [[], []]
 
     def score(item):
         h, b = item
-        here = slice(b * block, (b + 1) * block)
-        q = jnp.concatenate([head_rows(query_ref[:, here], h), zero_rows[:, here]], axis=0).astype(jnp.bfloat16)
+        here = slice(b * half, (b + 1) * half)
+        q = jnp.concatenate([head_rows(query_ref[:, here], h), zero_rows], axis=0).astype(jnp.bfloat16)
         return dot_nn(
-            jnp.concatenate([key_window(keys, h, None), key_mask], axis=1),
-            jnp.concatenate([q, query_mask[:, here]], axis=0),
+            jnp.concatenate([key_window(keys[here], h, None), key_mask[here]], axis=1),
+            jnp.concatenate([q, query_mask], axis=0),
         )
 
     def rest(item, scores):
         h, b = item
         highest = jnp.max(scores, axis=0, keepdims=True)
         expo = jnp.exp2((scores - highest) * COEF).astype(jnp.bfloat16)
-        v = jnp.concatenate([head_rows(value_ref[...], h), value_ones], axis=0).astype(jnp.bfloat16)
-        summed = dot_nn(v, expo)
+        v = head_rows(value_ref[:, b * half : (b + 1) * half], h)
+        summed = dot_nn(jnp.concatenate([v, value_ones], axis=0).astype(jnp.bfloat16), expo)
         pieces[b].append(summed[:HEAD] * (1.0 / summed[HEAD : HEAD + 1]))
 
-    staggered([(h, b) for h in range(HEADS) for b in range(blocks)], score, rest, 3)
-    for b in range(blocks):
-        out_ref[b * block : (b + 1) * block, :] = jnp.concatenate(pieces[b], axis=0).T.astype(jnp.bfloat16)
+    staggered([(h, b) for h in range(HEADS) for b in range(2)], score, rest, 4)
+    blocks = [jnp.concatenate(piece, axis=0).T.reshape(frames // 2, 2 * places, INNER) for piece in pieces]
+    out_ref[...] = jnp.stack(swap_halves(*blocks), axis=1).reshape(rows, INNER).astype(jnp.bfloat16)
 
 
 def final_kernel(attended_ref, weight_ref, outer_ref, inner_ref, out_hbm, block_ref, sems):

time: 96.5 us -> 95.3 us (0.988)
  Pallas kernels: 19.5 us -> 18.3 us
    pallas_call x1, Pallas kernels: 5.21 us -> 4 us  [shards(): kernel_call(functools.partial(time_kernel, frames), [VMEM] * 2, [spread((...]
where the time goes in v5:
time: 95.3 us; the launch traced here: 93.8 us
  blocking collectives  58.1 us (61%)
  Pallas kernels  18.3 us (19%)
  waiting for transfers between devices  12.3 us (13%)
  starting transfers between devices  2.9 us (3%)
  local copies, waits for them, and re-layouts  1.96 us (2%)
    all_to_all x2, blocking collectives, to_owners(): return lax.all_to_all(x, 'frame', split_axis=0, concat_axis=0, tiled=True)  58.1 us
    ppermute x1, waiting for transfers between devices, shards(): late_far = lax.ppermute(outer, 'cam', late_pairs)  11.1 us
    pallas_call x1, Pallas kernels, shards(): kernel_call(functools.partial(local_kernel, cameras), [SMEM, SMEM] + [VME...  8.11 us
    pallas_call x1, Pallas kernels, shards(): kernel_call(functools.partial(time_kernel, frames), [VMEM] * 2, [spread((...  4 us
    pallas_call x1, Pallas kernels, shards(): kernel_call(outer_kernel, [VMEM] * 9, [spread((token_count, model)), spre...  2.98 us
    ppermute x1, starting transfers between devices, shards(): late_far = lax.ppermute(outer, 'cam', late_pairs)  1.98 us
    unnamed x20, local copies, waits for them, and re-layouts  1.96 us
    pallas_call x1, Pallas kernels, shards(): kernel_call(final_kernel, [VMEM] * 4, [spread((rows, model))], [pltpu.VME...  1.94 us
  transfers between devices with their start and end apart: 3, of which 2 were waited for; matrix products, arithmetic and copies ran while one was open for 0% of the time, Pallas kernels for 9%

profile of v5, /device:TPU:22, one launch (start us, length us, event | category | flops | bytes accessed | tf_op | source)
XLA Modules:
  0.0 93.8 jit_solution(389887489828653910)
XLA Ops:
  0.0 0.0 copy-start.3
  0.0 1.3 %copy-done.3 = bf16[2,1,256,1152]{3,2,1,0:T(8,128)(2,1)S(1)} copy-done((bf16[2,1,256,1152]{3,2,1,0:T(8,128)(2,1)S(1)}, bf16[2,1,256,1152]{3,2,1,0:T(8,128)(2,1)}, u32[]{:S(2)}) %copy-start.3) | copy-done | bytes 1179672
  1.3 0.0 copy-start.8
  1.3 0.7 copy-done.8
  1.9 0.0 copy-start
  1.9 0.0 copy-start.2
  1.9 0.0 copy-start.4
  1.9 0.0 copy-start.6
  1.9 0.0 copy-start.7
  1.9 0.0 copy-start.9
  2.0 1.2 %shard_map.82 = (bf16[272,1152]{1,0:T(8,128)(2,1)S(1)}, bf16[272,1152]{1,0:T(8,128)(2,1)S(1)}) custom-call(s32[1,2]{1,0:T(1,128)S(1)} %bitcast.21, bf16[512,1152]{1,0:T(8,128)(2,1)S(1)} %bitcast.16), custom_call_target="tpu_custom_call" | custom-call | flops 6000000000 | bytes 2400000 | tf_op jit(solution)/shard_map/pallas_call | solution.py:345
  3.2 0.1 collective-permute-start.1
  3.3 0.8 collective-permute-start
  4.2 1.2 %collective-permute-done.1.far_ref = bf16[272,1152]{1,0:T(8,128)(2,1)S(1)} collective-permute-done((bf16[272,1152]{1,0:T(8,128)(2,1)S(1)}, bf16[272,1152]{1,0:T(8,128)(2,1)S(1)}, u32[]{:S(2)}, u32[]{:S(2)}) %collective-permute-start.1) | collective-permute-done | bytes 626720 | tf_op jit(solution)/shard_map/ppermute | solution.py:349
  5.4 0.0 copy-done
  5.4 0.0 copy-done.2
  5.4 0.0 copy-done.4
  5.4 0.0 copy-done.6
  5.4 0.0 copy-done.7
  5.4 0.0 copy-done.9
  5.4 8.1 %shard_map.83 = (f32[576,512]{1,0:T(8,128)S(1)}, f32[8,80,256]{2,1,0:T(8,128)S(1)}, f32[8,640]{1,0:T(8,128)S(1)}, bf16[256,1152]{1,0:T(8,128)(2,1)S(1)}, bf16[256,1280]{1,0:T(8,128)(2,1)S(1)}) custom-call(s32[1,2]{1,0:T(1,128)S(1)} %bitcast.22, s32[2,2]{1,0:T(2,128)S(1)} %copy-done.7, bf16[272,1152]{1,0:T(8,128)(2,1)S(1)} %get-tuple-element.19.outer_ref, ...), custom_call_target="tpu_custom_call" | custom-call | flops 8000000000 | bytes 20000000 | tf_op jit(solution)/shard_map/pallas_call | solution.py:351
  13.5 2.0 %collective-permute-start.2 = (bf16[272,1152]{1,0:T(8,128)(2,1)S(1)}, bf16[272,1152]{1,0:T(8,128)(2,1)S(1)}, u32[]{:S(2)}, u32[]{:S(2)}) collective-permute-start(bf16[272,1152]{1,0:T(8,128)(2,1)S(1)} %get-tuple-element.19.outer_ref), channel_id=1, source_target_pairs={{64,128},{128,64},{65,129},{129,65},{66,130},{130,66},{67,131},{13... | collective-permute-start | bytes 1880072 | tf_op jit(solution)/shard_map/ppermute | solution.py:367
  15.5 0.0 collective-permute-done.early_ref
  15.5 11.1 %collective-permute-done.2.late_ref = bf16[272,1152]{1,0:T(8,128)(2,1)S(1)} collective-permute-done((bf16[272,1152]{1,0:T(8,128)(2,1)S(1)}, bf16[272,1152]{1,0:T(8,128)(2,1)S(1)}, u32[]{:S(2)}, u32[]{:S(2)}) %collective-permute-start.2) | collective-permute-done | bytes 626720 | tf_op jit(solution)/shard_map/ppermute | solution.py:367
  26.6 0.0 copy-start.5
  26.6 3.0 %shard_map.84 = (bf16[256,1152]{1,0:T(8,128)(2,1)S(1)}, bf16[512,1280]{1,0:T(8,128)(2,1)S(1)}) custom-call(bf16[272,1152]{1,0:T(8,128)(2,1)S(1)} %collective-permute-done.early_ref, bf16[272,1152]{1,0:T(8,128)(2,1)S(1)} %collective-permute-done.2.late_ref, bf16[1728,1152]{1,0:T(8,128)(2,1)S(1)} %bitcast.12, f32[8,640]{1,0:T(8,128)S(1)} %get-tuple-element.20.info_ref, ...), custom_call_target="tpu_custom_call" | custom-call | flops 2500000000 | bytes 8000000 | tf_op jit(solution)/shard_map/pallas_call | solution.py:368
  29.6 37.0 %all_to_all.10 = bf16[64,8,1280]{2,1,0:T(8,128)(2,1)S(1)} all-to-all(bf16[64,8,1280]{2,1,0:T(8,128)(2,1)S(1)} %bitcast.14), channel_id=1, replica_groups=mesh['cam'=4,'frame'=64] {'frame'}, dimensions={0} | all-to-all | bytes 2621440 | tf_op jit(solution)/shard_map/all_to_all | solution.py:24
  66.6 0.0 copy-done.5
  66.6 0.0 copy-start.1
  66.6 4.0 %shard_map.85 = bf16[512,576]{1,0:T(8,128)(2,1)S(1)} custom-call(bf16[512,1280]{1,0:T(8,128)(2,1)S(1)} %bitcast.15, bf16[1728,1152]{1,0:T(8,128)(2,1)S(1)} %bitcast.20), custom_call_target="tpu_custom_call" | custom-call | flops 6000000000 | bytes 10000000 | tf_op jit(solution)/shard_map/pallas_call | solution.py:380
  70.6 21.1 %all_to_all.11 = bf16[64,8,576]{2,1,0:T(8,128)(2,1)S(1)} all-to-all(bf16[64,8,576]{2,1,0:T(8,128)(2,1)S(1)} %bitcast.19), channel_id=1, replica_groups=mesh['cam'=4,'frame'=64] {'frame'}, dimensions={0} | all-to-all | bytes 1179648 | tf_op jit(solution)/shard_map/all_to_all | solution.py:24
  91.7 0.0 copy-done.1
  91.7 1.9 %shard_map.86 = bf16[512,1152]{1,0:T(8,128)(2,1)} custom-call(bf16[512,576]{1,0:T(8,128)(2,1)S(1)} %bitcast.13, bf16[576,1152]{1,0:T(8,128)(2,1)S(1)} %copy-done.1, bf16[256,1152]{1,0:T(8,128)(2,1)S(1)} %get-tuple-element.25.outer_ref, bf16[256,1152]{1,0:T(8,128)(2,1)S(1)} %get-tuple-element.26.inner_ref), custom_call_target="tpu_custom_call" | custom-call | flops 700000000 | bytes 4000000 | tf_op jit(solution)/shard_map/pallas_call | solution.py:390
Async XLA Ops:
  0.0 1.3 %copy-start.3 = (bf16[2,1,256,1152]{3,2,1,0:T(8,128)(2,1)S(1)}, bf16[2,1,256,1152]{3,2,1,0:T(8,128)(2,1)}, u32[]{:S(2)}) copy-start(bf16[2,1,256,1152]{3,2,1,0:T(8,128)(2,1)} %param.8) | copy-start | bytes 3538948
  1.3 0.7 copy-start.8
  1.9 3.4 %copy-start = (bf16[1152,1728]{0,1:T(8,128)(2,1)S(1)}, bf16[1152,1728]{0,1:T(8,128)(2,1)}, u32[]{:S(2)}) copy-start(bf16[1152,1728]{0,1:T(8,128)(2,1)} %param.12) | copy-start | bytes 11943940
  1.9 3.4 %copy-start.2 = (bf16[576,1152]{1,0:T(8,128)(2,1)S(1)}, bf16[576,1152]{1,0:T(8,128)(2,1)}, u32[]{:S(2)}) copy-start(bf16[576,1152]{1,0:T(8,128)(2,1)} %out_weight_ref.3) | copy-start | bytes 3981316
  1.9 3.4 %copy-start.4 = (bf16[2,1,256,1152]{3,2,1,0:T(8,128)(2,1)S(1)}, bf16[2,1,256,1152]{3,2,1,0:T(8,128)(2,1)}, u32[]{:S(2)}) copy-start(bf16[2,1,256,1152]{3,2,1,0:T(8,128)(2,1)} %param.8) | copy-start | bytes 3538948
  1.9 3.4 %copy-start.6 = (bf16[2,576]{1,0:T(2,128)(2,1)S(1)}, bf16[2,576]{1,0:T(2,128)(2,1)}, u32[]{:S(2)}) copy-start(bf16[2,576]{1,0:T(2,128)(2,1)} %side_ref.1) | copy-start | bytes 6916
  1.9 3.4 %copy-start.7 = (s32[2,2]{1,0:T(2,128)S(1)}, s32[2,2]{1,0:T(2,128)}, u32[]{:S(2)}) copy-start(s32[2,2]{1,0:T(2,128)} %neighbours_ref.1) | copy-start | bytes 52
  1.9 3.4 %copy-start.9 = (s32[2,1]{0,1:T(1,128)S(1)}, s32[2,1]{0,1:T(1,128)}, u32[]{:S(2)}) copy-start(s32[2,1]{0,1:T(1,128)} %param.9) | copy-start | bytes 28
  3.2 2.1 %collective-permute-start.1 = (bf16[272,1152]{1,0:T(8,128)(2,1)S(1)}, bf16[272,1152]{1,0:T(8,128)(2,1)S(1)}, u32[]{:S(2)}, u32[]{:S(2)}) collective-permute-start(bf16[272,1152]{1,0:T(8,128)(2,1)S(1)} %get-tuple-element.17.inner_ref), channel_id=1, source_target_pairs={{0,64},{64,0},{128,192},{192,128},{1,65},{65,1},{129,193},{193,129... | collective-permute-start | bytes 1880072 | tf_op jit(solution)/shard_map/ppermute | solution.py:349
  3.3 12.2 %collective-permute-start = (bf16[272,1152]{1,0:T(8,128)(2,1)S(1)}, bf16[272,1152]{1,0:T(8,128)(2,1)S(1)}, u32[]{:S(2)}, u32[]{:S(2)}) collective-permute-start(bf16[272,1152]{1,0:T(8,128)(2,1)S(1)} %get-tuple-element.19.outer_ref), channel_id=1, source_target_pairs={{192,0},{0,192},{193,1},{1,193},{194,2},{2,194},{195,3},{3,195},{1... | collective-permute-start | bytes 1880072 | tf_op jit(solution)/shard_map/ppermute | solution.py:348
  13.5 13.1 %collective-permute-start.2 = (bf16[272,1152]{1,0:T(8,128)(2,1)S(1)}, bf16[272,1152]{1,0:T(8,128)(2,1)S(1)}, u32[]{:S(2)}, u32[]{:S(2)}) collective-permute-start(bf16[272,1152]{1,0:T(8,128)(2,1)S(1)} %get-tuple-element.19.outer_ref), channel_id=1, source_target_pairs={{64,128},{128,64},{65,129},{129,65},{66,130},{130,66},{67,131},{13... | collective-permute-start | bytes 1880072 | tf_op jit(solution)/shard_map/ppermute | solution.py:367
  26.6 40.0 %copy-start.5 = (bf16[1152,1728]{0,1:T(8,128)(2,1)S(1)}, bf16[1152,1728]{0,1:T(8,128)(2,1)}, u32[]{:S(2)}) copy-start(bf16[1152,1728]{0,1:T(8,128)(2,1)} %param.14) | copy-start | bytes 11943940
  66.6 25.1 %copy-start.1 = (bf16[576,1152]{1,0:T(8,128)(2,1)S(1)}, bf16[576,1152]{1,0:T(8,128)(2,1)}, u32[]{:S(2)}) copy-start(bf16[576,1152]{1,0:T(8,128)(2,1)} %weight_ref.1) | copy-start | bytes 3981316

commit v6 on v5

--- a/solution.py
+++ b/solution.py
@@ -17,6 +17,8 @@
 COEF = HEAD ** (-0.5) * math.log2(math.e)
 LANES = 128
 KEY_LANES = 640
+PLACES = 2
+GROUPS = 4
 MIB = 1 << 20
 
 
@@ -124,10 +126,17 @@
     mixed = (dot_nn(attended, out_weight_ref[...]) + tokens.astype(jnp.float32)).astype(jnp.bfloat16)
     rows, width = mixed.shape
     mixed_ref[...] = mixed
-    payload_ref[:rows, :width] = normalize(mixed)
-    position = lax.broadcasted_iota(jnp.int32, (rows, LANES), 0).astype(jnp.float32)
-    valid = position < ROW_TOKENS * info_ref[2 + i : 3 + i, :LANES]
-    payload_ref[:rows, width:] = jnp.where(valid, 1.0, 0.0).astype(jnp.bfloat16)
+    normed = normalize(mixed)
+    size = rows // GROUPS
+    chunks = size // PLACES
+    for g in range(GROUPS):
+        block = normed[g * size : (g + 1) * size].reshape(chunks, PLACES, width)
+        payload_ref[:chunks, :, g * width : (g + 1) * width] = block
+    group = lax.broadcasted_iota(jnp.int32, (size, LANES), 1) // (LANES // GROUPS)
+    position = lax.broadcasted_iota(jnp.int32, (size, LANES), 0) + group * size
+    valid = position.astype(jnp.float32) < ROW_TOKENS * info_ref[2 + i : 3 + i, :LANES]
+    valid = jnp.where(valid, 1.0, 0.0).astype(jnp.bfloat16)
+    payload_ref[:chunks, :, GROUPS * width :] = valid.reshape(chunks, PLACES, LANES)
 
 
 def local_kernel(
@@ -211,7 +220,7 @@
     keys = padded_keys(dot_nt(far, weight_ref[INNER : 2 * INNER, :]))
     keys = with_side(keys, info_ref[0:1, :])
     value_ref[...] = rounded(dot_nt(weight_ref[2 * INNER :, :], far))
-    payload_ref[rows:, :] = inner_ref[...]
+    payload_ref[inner_ref.shape[0] :] = inner_ref[...]
     bias = keys_bias(rows, far_count.astype(jnp.float32)[:1])
     one_rows = one_then_zeros(LANES - HEAD, rows)
     value_ones = one_then_zeros(8, rows)
@@ -230,81 +239,87 @@
         summed = part * jnp.exp2((before - highest) * COEF) + dot_nn(v, expo)
         pieces.append(summed[:HEAD] * (1.0 / summed[HEAD : HEAD + 1]))
 
-    staggered(list(range(HEADS)), score, rest, 3)
+    staggered(list(range(HEADS)), score, rest, HEADS)
     tokens = tokens_ref[camera_rows(cam_is_odd(), rows), :]
     write_finished(0, pieces, tokens, out_weight_ref, info_ref, mixed_ref, payload_ref)
 
 
-def swap_halves(first, second):
-    upper = lax.broadcasted_iota(jnp.int32, first.shape, 1) < 4
-    return jnp.where(upper, first, pltpu.roll(second, 4, 1)), jnp.where(upper, pltpu.roll(first, 4, 1), second)
-
-
 def time_kernel(frames, payload_ref, weight_ref, out_ref, query_ref, value_ref):
-    rows, lanes = payload_ref.shape
+    size = frames * PLACES
+    rows = GROUPS * size
     model = weight_ref.shape[1]
-    half = rows // 2
-    places = half // frames
-    pairs = payload_ref[...].astype(jnp.float32).reshape(frames // 2, 2, 2 * places, lanes)
-    low, high = swap_halves(pairs[:, 0], pairs[:, 1])
-    payload = jnp.concatenate([low.reshape(half, lanes), high.reshape(half, lanes)], axis=0).astype(jnp.bfloat16)
-    normed = payload[:, :model]
+    normed = jnp.concatenate(
+        [payload_ref[:, :, g * model : (g + 1) * model].reshape(size, model) for g in range(GROUPS)], axis=0
+    )
     keys = padded_keys(dot_nt(normed, weight_ref[INNER : 2 * INNER, :]))
     query_ref[...] = rounded(dot_nt(weight_ref[:INNER, :], normed))
     value_ref[...] = rounded(dot_nt(weight_ref[2 * INNER :, :], normed))
-    lane = lax.broadcasted_iota(jnp.int32, (rows, LANES), 1)
-    key = lax.rem(lax.broadcasted_iota(jnp.int32, (rows, LANES), 0), half)
-    invalid = payload[:, model:].astype(jnp.float32) < 0.5
-    key_mask = jnp.where(
-        lane < frames,
-        jnp.where(jnp.logical_and(invalid, lane != key // places), -BIG, 0.0),
-        jnp.where(lane - frames == key % places, 1.0, 0.0),
-    ).astype(jnp.bfloat16)
-    entry = lax.broadcasted_iota(jnp.int32, (LANES, half), 0)
-    query = lax.broadcasted_iota(jnp.int32, (LANES, half), 1)
+    valid = payload_ref[:, :, GROUPS * model :].reshape(size, LANES).astype(jnp.float32)
+    lane = lax.broadcasted_iota(jnp.int32, (size, LANES), 1)
+    key = lax.broadcasted_iota(jnp.int32, (size, LANES), 0)
+    key_masks = []
+    for g in range(GROUPS):
+        first = g * (LANES // GROUPS)
+        invalid = valid[:, first : first + 1] < 0.5
+        key_mask = jnp.where(
+            lane < frames,
+            jnp.where(jnp.logical_and(invalid, lane != key // PLACES), -BIG, 0.0),
+            jnp.where(lane - frames == key % PLACES, 1.0, 0.0),
+        )
+        key_masks.append(key_mask.astype(jnp.bfloat16))
+    entry = lax.broadcasted_iota(jnp.int32, (LANES, size), 0)
+    query = lax.broadcasted_iota(jnp.int32, (LANES, size), 1)
     query_mask = jnp.where(
         entry < frames,
-        jnp.where(entry == query // places, 1.0, 0.0),
-        jnp.where(jnp.logical_and(entry < frames + places, entry - frames != query % places), -BIG, 0.0),
+        jnp.where(entry == query // PLACES, 1.0, 0.0),
+        jnp.where(jnp.logical_and(entry < frames + PLACES, entry - frames != query % PLACES), -BIG, 0.0),
     ).astype(jnp.bfloat16)
-    zero_rows = jnp.zeros((LANES - HEAD, half), jnp.float32)
-    value_ones = one_then_zeros(8, half)
-    pieces = [[], []]
+    zero_rows = jnp.zeros((LANES - HEAD, size), jnp.float32)
+    value_ones = one_then_zeros(8, size)
+    pieces = [[] for _ in range(GROUPS)]
 
     def score(item):
-        h, b = item
-        here = slice(b * half, (b + 1) * half)
+        h, g = item
+        here = slice(g * size, (g + 1) * size)
         q = jnp.concatenate([head_rows(query_ref[:, here], h), zero_rows], axis=0).astype(jnp.bfloat16)
         return dot_nn(
-            jnp.concatenate([key_window(keys[here], h, None), key_mask[here]], axis=1),
+            jnp.concatenate([key_window(keys[here], h, None), key_masks[g]], axis=1),
             jnp.concatenate([q, query_mask], axis=0),
         )
 
     def rest(item, scores):
-        h, b = item
+        h, g = item
         highest = jnp.max(scores, axis=0, keepdims=True)
         expo = jnp.exp2((scores - highest) * COEF).astype(jnp.bfloat16)
-        v = head_rows(value_ref[:, b * half : (b + 1) * half], h)
+        v = head_rows(value_ref[:, g * size : (g + 1) * size], h)
         summed = dot_nn(jnp.concatenate([v, value_ones], axis=0).astype(jnp.bfloat16), expo)
-        pieces[b].append(summed[:HEAD] * (1.0 / summed[HEAD : HEAD + 1]))
-
-    staggered([(h, b) for h in range(HEADS) for b in range(2)], score, rest, 4)
-    blocks = [jnp.concatenate(piece, axis=0).T.reshape(frames // 2, 2 * places, INNER) for piece in pieces]
-    out_ref[...] = jnp.stack(swap_halves(*blocks), axis=1).reshape(rows, INNER).astype(jnp.bfloat16)
+        pieces[g].append(summed[:HEAD] * (1.0 / summed[HEAD : HEAD + 1]))
+
+    staggered([(h, g) for h in range(HEADS) for g in range(GROUPS)], score, rest, 6)
+    attended = jnp.concatenate(sum(pieces, []), axis=0).T.astype(jnp.bfloat16)
+    out_ref[...] = attended.reshape(frames, PLACES, GROUPS * INNER)
 
 
 def final_kernel(attended_ref, weight_ref, outer_ref, inner_ref, out_hbm, block_ref, sems):
     rows = outer_ref.shape[0]
-    size = block_ref.shape[1]
+    size = rows // GROUPS
+    chunks = size // PLACES
+    half = GROUPS // 2
     odd = cam_is_odd()
     copies = []
     for i, (cam, mixed_ref) in enumerate(((odd, outer_ref), (1 - odd, inner_ref))):
-        for start in range(0, rows, size):
+        here = slice(i * chunks, (i + 1) * chunks)
+        blocks = [
+            attended_ref[here, :, g * INNER : (g + 1) * INNER].reshape(size, INNER) for g in range(GROUPS)
+        ]
+        for part in range(2):
             slot = len(copies)
-            result = dot_nn(attended_ref[i * rows + start : i * rows + start + size, :], weight_ref[...])
-            result = result + mixed_ref[start : start + size, :].astype(jnp.float32)
+            start = part * half * size
+            attended = jnp.concatenate(blocks[part * half : (part + 1) * half], axis=0)
+            result = dot_nn(attended, weight_ref[...])
+            result = result + mixed_ref[start : start + half * size, :].astype(jnp.float32)
             block_ref[slot] = result.astype(jnp.bfloat16)
-            there = pl.ds(pl.multiple_of(cam * rows + start, size), size)
+            there = pl.ds(pl.multiple_of(cam * rows + start, half * size), half * size)
             copies.append(pltpu.make_async_copy(block_ref.at[slot], out_hbm.at[there], sems.at[slot]))
             copies[-1].start()
     for copy in copies:
@@ -337,6 +352,7 @@
     spread = functools.partial(jax.ShapeDtypeStruct, dtype=bf16)
 
     flat = tokens.reshape(rows, model)
+    payload_lanes = GROUPS * model + LANES
     own_counts = counts.reshape(1, cam_here)
     cross_t, time_t = cross_qkv.T, time_qkv.T
     inside_pairs, early_pairs, late_pairs = exchange_pairs(lax.axis_size("cam"))
@@ -356,7 +372,7 @@
             jax.ShapeDtypeStruct((HEADS, HEAD + 8, token_count), jnp.float32),
             jax.ShapeDtypeStruct((8, KEY_LANES), jnp.float32),
             spread((token_count, model)),
-            spread((token_count, model + LANES)),
+            spread((frames // 2, PLACES, payload_lanes)),
         ],
         [pltpu.VMEM((INNER, rows + token_count), jnp.float32)],
         36,
@@ -368,25 +384,24 @@
     mixed_outer, payload = kernel_call(
         outer_kernel,
         [VMEM] * 9,
-        [spread((token_count, model)), spread((rows, model + LANES))],
+        [spread((token_count, model)), spread((frames, PLACES, payload_lanes))],
         [pltpu.VMEM((INNER, token_count), jnp.float32)],
         32,
         2_500_000_000,
         8_000_000,
     )(early_far, late_far, cross_t, info, query, part, flat, cross_out, payload_inner)
 
-    chunk = rows // frames
-    arrived = to_owners(payload.reshape(frames, chunk, model + LANES))
+    arrived = to_owners(payload)
     (attended,) = kernel_call(
         functools.partial(time_kernel, frames),
         [VMEM] * 2,
-        [spread((rows, INNER))],
+        [spread((frames, PLACES, GROUPS * INNER))],
         [pltpu.VMEM((INNER, rows), jnp.float32)] * 2,
         32,
         6_000_000_000,
         10_000_000,
-    )(arrived.reshape(rows, model + LANES), time_t)
-    returned = to_owners(attended.reshape(frames, chunk, INNER))
+    )(arrived, time_t)
+    returned = to_owners(attended)
     (out,) = kernel_call(
         final_kernel,
         [VMEM] * 4,
@@ -396,7 +411,7 @@
         700_000_000,
         4_000_000,
         ANY,
-    )(returned.reshape(rows, INNER), time_out, mixed_outer, mixed_inner)
+    )(returned, time_out, mixed_outer, mixed_inner)
     return out.reshape(tokens.shape)
 
 

time: 95.3 us -> 91.8 us (0.963)
  blocking collectives: 58.1 us -> 55.3 us
    all_to_all x2, blocking collectives: 58.1 us -> 55.3 us  [to_owners(): return lax.all_to_all(x, 'frame', split_axis=0, concat_axis=0, tiled=True)]
where the time goes in v6:
time: 91.8 us; the launch traced here: 91 us
  blocking collectives  55.3 us (60%)
  Pallas kernels  18.2 us (20%)
  waiting for transfers between devices  12.3 us (13%)
  starting transfers between devices  2.9 us (3%)
  local copies, waits for them, and re-layouts  1.96 us (2%)
    all_to_all x2, blocking collectives, to_owners(): return lax.all_to_all(x, 'frame', split_axis=0, concat_axis=0, tiled=True)  55.3 us
    ppermute x1, waiting for transfers between devices, shards(): late_far = lax.ppermute(outer, 'cam', late_pairs)  11.1 us
    pallas_call x1, Pallas kernels, shards(): kernel_call(functools.partial(local_kernel, cameras), [SMEM, SMEM] + [VME...  8.17 us
    pallas_call x1, Pallas kernels, shards(): kernel_call(functools.partial(time_kernel, frames), [VMEM] * 2, [spread((...  4.05 us
    pallas_call x1, Pallas kernels, shards(): kernel_call(outer_kernel, [VMEM] * 9, [spread((token_count, model)), spre...  2.76 us
    pallas_call x1, Pallas kernels, shards(): kernel_call(final_kernel, [VMEM] * 4, [spread((rows, model))], [pltpu.VME...  2 us
    ppermute x1, starting transfers between devices, shards(): late_far = lax.ppermute(outer, 'cam', late_pairs)  1.98 us
    unnamed x20, local copies, waits for them, and re-layouts  1.96 us
  transfers between devices with their start and end apart: 3, of which 2 were waited for; matrix products, arithmetic and copies ran while one was open for 0% of the time, Pallas kernels for 9%

profile of v6, /device:TPU:22, one launch (start us, length us, event | category | flops | bytes accessed | tf_op | source)
XLA Modules:
  0.0 91.0 jit_solution(4675891351927118238)
XLA Ops:
  0.0 0.0 copy-start.3
  0.0 1.3 %copy-done.3 = bf16[2,1,256,1152]{3,2,1,0:T(8,128)(2,1)S(1)} copy-done((bf16[2,1,256,1152]{3,2,1,0:T(8,128)(2,1)S(1)}, bf16[2,1,256,1152]{3,2,1,0:T(8,128)(2,1)}, u32[]{:S(2)}) %copy-start.3) | copy-done | bytes 1179672
  1.3 0.0 copy-start.8
  1.3 0.7 copy-done.8
  1.9 0.0 copy-start
  1.9 0.0 copy-start.2
  1.9 0.0 copy-start.4
  1.9 0.0 copy-start.6
  1.9 0.0 copy-start.7
  1.9 0.0 copy-start.9
  2.0 1.2 %shard_map.82 = (bf16[272,1152]{1,0:T(8,128)(2,1)S(1)}, bf16[272,1152]{1,0:T(8,128)(2,1)S(1)}) custom-call(s32[1,2]{1,0:T(1,128)S(1)} %bitcast.13, bf16[512,1152]{1,0:T(8,128)(2,1)S(1)} %bitcast.9), custom_call_target="tpu_custom_call" | custom-call | flops 6000000000 | bytes 2400000 | tf_op jit(solution)/shard_map/pallas_call | solution.py:361
  3.2 0.1 collective-permute-start.1
  3.3 0.8 collective-permute-start
  4.2 1.2 %collective-permute-done.1.far_ref = bf16[272,1152]{1,0:T(8,128)(2,1)S(1)} collective-permute-done((bf16[272,1152]{1,0:T(8,128)(2,1)S(1)}, bf16[272,1152]{1,0:T(8,128)(2,1)S(1)}, u32[]{:S(2)}, u32[]{:S(2)}) %collective-permute-start.1) | collective-permute-done | bytes 626720 | tf_op jit(solution)/shard_map/ppermute | solution.py:365
  5.4 0.0 copy-done
  5.4 0.0 copy-done.2
  5.4 0.0 copy-done.4
  5.4 0.0 copy-done.6
  5.4 0.0 copy-done.7
  5.4 0.0 copy-done.9
  5.4 8.2 %shard_map.83 = (f32[576,512]{1,0:T(8,128)S(1)}, f32[8,80,256]{2,1,0:T(8,128)S(1)}, f32[8,640]{1,0:T(8,128)S(1)}, bf16[256,1152]{1,0:T(8,128)(2,1)S(1)}, bf16[32,2,4736]{2,1,0:T(2,128)(2,1)S(1)}) custom-call(s32[1,2]{1,0:T(1,128)S(1)} %bitcast.14, s32[2,2]{1,0:T(2,128)S(1)} %copy-done.7, bf16[272,1152]{1,0:T(8,128)(2,1)S(1)} %get-tuple-element.19.outer_ref, ...), custom_call_target="tpu_custom_call" | custom-call | flops 8000000000 | bytes 20000000 | tf_op jit(solution)/shard_map/pallas_call | solution.py:367
  13.6 2.0 %collective-permute-start.2 = (bf16[272,1152]{1,0:T(8,128)(2,1)S(1)}, bf16[272,1152]{1,0:T(8,128)(2,1)S(1)}, u32[]{:S(2)}, u32[]{:S(2)}) collective-permute-start(bf16[272,1152]{1,0:T(8,128)(2,1)S(1)} %get-tuple-element.19.outer_ref), channel_id=1, source_target_pairs={{64,128},{128,64},{65,129},{129,65},{66,130},{130,66},{67,131},{13... | collective-permute-start | bytes 1880072 | tf_op jit(solution)/shard_map/ppermute | solution.py:383
  15.6 0.0 collective-permute-done.early_ref
  15.6 11.1 %collective-permute-done.2.late_ref = bf16[272,1152]{1,0:T(8,128)(2,1)S(1)} collective-permute-done((bf16[272,1152]{1,0:T(8,128)(2,1)S(1)}, bf16[272,1152]{1,0:T(8,128)(2,1)S(1)}, u32[]{:S(2)}, u32[]{:S(2)}) %collective-permute-start.2) | collective-permute-done | bytes 626720 | tf_op jit(solution)/shard_map/ppermute | solution.py:383
  26.7 0.0 copy-start.5
  26.7 2.8 %shard_map.84 = (bf16[256,1152]{1,0:T(8,128)(2,1)S(1)}, bf16[64,2,4736]{2,1,0:T(2,128)(2,1)S(1)}) custom-call(bf16[272,1152]{1,0:T(8,128)(2,1)S(1)} %collective-permute-done.early_ref, bf16[272,1152]{1,0:T(8,128)(2,1)S(1)} %collective-permute-done.2.late_ref, bf16[1728,1152]{1,0:T(8,128)(2,1)S(1)} %bitcast.8, f32[8,640]{1,0:T(8,128)S(1)} %get-tuple-element.20.info_ref, ...), custom_call_target="tpu_custom_call" | custom-call | flops 2500000000 | bytes 8000000 | tf_op jit(solution)/shard_map/pallas_call | solution.py:384
  29.4 34.9 %all_to_all.10.payload_ref = bf16[64,2,4736]{2,1,0:T(2,128)(2,1)S(1)} all-to-all(bf16[64,2,4736]{2,1,0:T(2,128)(2,1)S(1)} %get-tuple-element.24), channel_id=1, replica_groups=mesh['cam'=4,'frame'=64] {'frame'}, dimensions={0} | all-to-all | bytes 2424832 | tf_op jit(solution)/shard_map/all_to_all | solution.py:26
  64.4 0.0 copy-done.5
  64.4 0.0 copy-start.1
  64.4 4.1 %shard_map.85 = bf16[64,2,2304]{2,1,0:T(2,128)(2,1)S(1)} custom-call(bf16[64,2,4736]{2,1,0:T(2,128)(2,1)S(1)} %all_to_all.10.payload_ref, bf16[1728,1152]{1,0:T(8,128)(2,1)S(1)} %bitcast.12), custom_call_target="tpu_custom_call" | custom-call | flops 6000000000 | bytes 10000000 | tf_op jit(solution)/shard_map/pallas_call | solution.py:395
  68.4 20.4 %all_to_all.11.attended_ref = bf16[64,2,2304]{2,1,0:T(2,128)(2,1)S(1)} all-to-all(bf16[64,2,2304]{2,1,0:T(2,128)(2,1)S(1)} %shard_map.85), channel_id=1, replica_groups=mesh['cam'=4,'frame'=64] {'frame'}, dimensions={0} | all-to-all | bytes 1179648 | tf_op jit(solution)/shard_map/all_to_all | solution.py:26
  88.8 0.0 copy-done.1
  88.8 2.0 %shard_map.86 = bf16[512,1152]{1,0:T(8,128)(2,1)} custom-call(bf16[64,2,2304]{2,1,0:T(2,128)(2,1)S(1)} %all_to_all.11.attended_ref, bf16[576,1152]{1,0:T(8,128)(2,1)S(1)} %copy-done.1, bf16[256,1152]{1,0:T(8,128)(2,1)S(1)} %get-tuple-element.25.outer_ref, bf16[256,1152]{1,0:T(8,128)(2,1)S(1)} %get-tuple-element.26.inner_ref), custom_call_target="tpu_custom_call" | custom-call | flops 700000000 | bytes 4000000 | tf_op jit(solution)/shard_map/pallas_call | solution.py:405
Async XLA Ops:
  0.0 1.3 %copy-start.3 = (bf16[2,1,256,1152]{3,2,1,0:T(8,128)(2,1)S(1)}, bf16[2,1,256,1152]{3,2,1,0:T(8,128)(2,1)}, u32[]{:S(2)}) copy-start(bf16[2,1,256,1152]{3,2,1,0:T(8,128)(2,1)} %param.8) | copy-start | bytes 3538948
  1.3 0.7 copy-start.8
  1.9 3.4 %copy-start = (bf16[1152,1728]{0,1:T(8,128)(2,1)S(1)}, bf16[1152,1728]{0,1:T(8,128)(2,1)}, u32[]{:S(2)}) copy-start(bf16[1152,1728]{0,1:T(8,128)(2,1)} %param.12) | copy-start | bytes 11943940
  1.9 3.4 %copy-start.2 = (bf16[576,1152]{1,0:T(8,128)(2,1)S(1)}, bf16[576,1152]{1,0:T(8,128)(2,1)}, u32[]{:S(2)}) copy-start(bf16[576,1152]{1,0:T(8,128)(2,1)} %out_weight_ref.3) | copy-start | bytes 3981316
  1.9 3.4 %copy-start.4 = (bf16[2,1,256,1152]{3,2,1,0:T(8,128)(2,1)S(1)}, bf16[2,1,256,1152]{3,2,1,0:T(8,128)(2,1)}, u32[]{:S(2)}) copy-start(bf16[2,1,256,1152]{3,2,1,0:T(8,128)(2,1)} %param.8) | copy-start | bytes 3538948
  1.9 3.4 %copy-start.6 = (bf16[2,576]{1,0:T(2,128)(2,1)S(1)}, bf16[2,576]{1,0:T(2,128)(2,1)}, u32[]{:S(2)}) copy-start(bf16[2,576]{1,0:T(2,128)(2,1)} %side_ref.1) | copy-start | bytes 6916
  1.9 3.4 %copy-start.7 = (s32[2,2]{1,0:T(2,128)S(1)}, s32[2,2]{1,0:T(2,128)}, u32[]{:S(2)}) copy-start(s32[2,2]{1,0:T(2,128)} %neighbours_ref.1) | copy-start | bytes 52
  1.9 3.4 %copy-start.9 = (s32[2,1]{0,1:T(1,128)S(1)}, s32[2,1]{0,1:T(1,128)}, u32[]{:S(2)}) copy-start(s32[2,1]{0,1:T(1,128)} %param.9) | copy-start | bytes 28
  3.2 2.1 %collective-permute-start.1 = (bf16[272,1152]{1,0:T(8,128)(2,1)S(1)}, bf16[272,1152]{1,0:T(8,128)(2,1)S(1)}, u32[]{:S(2)}, u32[]{:S(2)}) collective-permute-start(bf16[272,1152]{1,0:T(8,128)(2,1)S(1)} %get-tuple-element.17.inner_ref), channel_id=1, source_target_pairs={{0,64},{64,0},{128,192},{192,128},{1,65},{65,1},{129,193},{193,129... | collective-permute-start | bytes 1880072 | tf_op jit(solution)/shard_map/ppermute | solution.py:365
  3.3 12.3 %collective-permute-start = (bf16[272,1152]{1,0:T(8,128)(2,1)S(1)}, bf16[272,1152]{1,0:T(8,128)(2,1)S(1)}, u32[]{:S(2)}, u32[]{:S(2)}) collective-permute-start(bf16[272,1152]{1,0:T(8,128)(2,1)S(1)} %get-tuple-element.19.outer_ref), channel_id=1, source_target_pairs={{192,0},{0,192},{193,1},{1,193},{194,2},{2,194},{195,3},{3,195},{1... | collective-permute-start | bytes 1880072 | tf_op jit(solution)/shard_map/ppermute | solution.py:364
  13.6 13.1 %collective-permute-start.2 = (bf16[272,1152]{1,0:T(8,128)(2,1)S(1)}, bf16[272,1152]{1,0:T(8,128)(2,1)S(1)}, u32[]{:S(2)}, u32[]{:S(2)}) collective-permute-start(bf16[272,1152]{1,0:T(8,128)(2,1)S(1)} %get-tuple-element.19.outer_ref), channel_id=1, source_target_pairs={{64,128},{128,64},{65,129},{129,65},{66,130},{130,66},{67,131},{13... | collective-permute-start | bytes 1880072 | tf_op jit(solution)/shard_map/ppermute | solution.py:383
  26.7 37.7 %copy-start.5 = (bf16[1152,1728]{0,1:T(8,128)(2,1)S(1)}, bf16[1152,1728]{0,1:T(8,128)(2,1)}, u32[]{:S(2)}) copy-start(bf16[1152,1728]{0,1:T(8,128)(2,1)} %param.14) | copy-start | bytes 11943940
  64.4 24.4 %copy-start.1 = (bf16[576,1152]{1,0:T(8,128)(2,1)S(1)}, bf16[576,1152]{1,0:T(8,128)(2,1)}, u32[]{:S(2)}) copy-start(bf16[576,1152]{1,0:T(8,128)(2,1)} %weight_ref.1) | copy-start | bytes 3981316

commit v7 on v6

--- a/solution.py
+++ b/solution.py
@@ -116,9 +116,20 @@
     rows = tokens_ref.shape[0] // 2
     odd = cam_is_odd()
     for cam, out_ref in ((odd, outer_ref), (1 - odd, inner_ref)):
-        out_ref[:rows, :] = normalize(tokens_ref[camera_rows(cam, rows), :])
+        last, *block = out_ref.shape
+        last -= 1
+        out_ref[:last] = normalize(tokens_ref[camera_rows(cam, rows), :]).reshape(last, *block)
         count = counts_ref[0, cam].astype(jnp.float32)
-        out_ref[rows:, :] = jnp.full((out_ref.shape[0] - rows, out_ref.shape[1]), count, jnp.float32).astype(jnp.bfloat16)
+        out_ref[last:] = jnp.full((1, *block), count, jnp.float32).astype(jnp.bfloat16)
+
+
+def sent_rows(ref):
+    blocks, size, width = ref.shape
+    return ref[: blocks - 1].reshape((blocks - 1) * size, width)
+
+
+def sent_count(ref):
+    return ref[ref.shape[0] - 1, :, :LANES].astype(jnp.float32)[:1]
 
 
 def write_finished(i, pieces, tokens, out_weight_ref, info_ref, mixed_ref, payload_ref):
@@ -146,7 +157,7 @@
     rows = mixed_ref.shape[0]
     odd = cam_is_odd()
     cams = (odd, 1 - odd)
-    normed = jnp.concatenate([outer_ref[:rows, :], inner_ref[:rows, :], far_ref[:rows, :]], axis=0)
+    normed = jnp.concatenate([sent_rows(ref) for ref in (outer_ref, inner_ref, far_ref)], axis=0)
     keys = padded_keys(dot_nt(normed, weight_ref[INNER : 2 * INNER, :]))
     query_ref[...] = rounded(dot_nt(weight_ref[:INNER, :], normed[: 2 * rows]))
     value_ref[...] = rounded(dot_nt(weight_ref[2 * INNER :, :], normed))
@@ -162,7 +173,7 @@
         info_ref[2 + i : 3 + i, :] = jnp.full((1, KEY_LANES), counts[i], jnp.float32)
     info_ref[4:, :] = jnp.zeros((info_ref.shape[0] - 4, KEY_LANES), jnp.float32)
     biases = [keys_bias(rows, count) for count in counts]
-    far_bias = keys_bias(rows, far_ref[rows : rows + 16, :LANES].astype(jnp.float32)[:1])
+    far_bias = keys_bias(rows, sent_count(far_ref))
     one_rows = one_then_zeros(LANES - HEAD, rows)
     value_ones = one_then_zeros(8, 3 * rows)
     outer, inner, far = (slice(i * rows, (i + 1) * rows) for i in range(3))
@@ -204,7 +215,7 @@
         else:
             pieces.append(summed[:HEAD] * (1.0 / summed[HEAD : HEAD + 1]))
 
-    staggered([(i, h) for i in (1, 0) for h in range(HEADS)], score, rest, 3)
+    staggered([(i, h) for i in (1, 0) for h in range(HEADS)], score, rest, 8)
     tokens = tokens_ref[camera_rows(1 - odd, rows), :]
     write_finished(1, pieces, tokens, out_weight_ref, info_ref, mixed_ref, payload_ref)
 
@@ -215,13 +226,13 @@
 ):
     rows = mixed_ref.shape[0]
     early = is_early()
-    far = jnp.where(early, early_ref[:rows, :], late_ref[:rows, :])
-    far_count = jnp.where(early, early_ref[rows : rows + 16, :LANES], late_ref[rows : rows + 16, :LANES])
+    far = jnp.where(early, sent_rows(early_ref), sent_rows(late_ref))
+    far_count = jnp.where(early, sent_count(early_ref), sent_count(late_ref))
     keys = padded_keys(dot_nt(far, weight_ref[INNER : 2 * INNER, :]))
     keys = with_side(keys, info_ref[0:1, :])
     value_ref[...] = rounded(dot_nt(weight_ref[2 * INNER :, :], far))
     payload_ref[inner_ref.shape[0] :] = inner_ref[...]
-    bias = keys_bias(rows, far_count.astype(jnp.float32)[:1])
+    bias = keys_bias(rows, far_count)
     one_rows = one_then_zeros(LANES - HEAD, rows)
     value_ones = one_then_zeros(8, rows)
     pieces = []
@@ -295,7 +306,7 @@
         summed = dot_nn(jnp.concatenate([v, value_ones], axis=0).astype(jnp.bfloat16), expo)
         pieces[g].append(summed[:HEAD] * (1.0 / summed[HEAD : HEAD + 1]))
 
-    staggered([(h, g) for h in range(HEADS) for g in range(GROUPS)], score, rest, 6)
+    staggered([(h, g) for g in range(GROUPS) for h in range(HEADS)], score, rest, 10)
     attended = jnp.concatenate(sum(pieces, []), axis=0).T.astype(jnp.bfloat16)
     out_ref[...] = attended.reshape(frames, PLACES, GROUPS * INNER)
 
@@ -356,10 +367,10 @@
     own_counts = counts.reshape(1, cam_here)
     cross_t, time_t = cross_qkv.T, time_qkv.T
     inside_pairs, early_pairs, late_pairs = exchange_pairs(lax.axis_size("cam"))
-    sent = token_count + 16
+    sent = (token_count // 4 + 1, 4, model)
 
     outer, inner = kernel_call(
-        norm_kernel, [SMEM, VMEM], [spread((sent, model))] * 2, [], 16, 6_000_000_000, 2_400_000
+        norm_kernel, [SMEM, VMEM], [spread(sent)] * 2, [], 16, 6_000_000_000, 2_400_000
     )(own_counts, flat)
     early_far = lax.ppermute(outer, "cam", early_pairs)
     inner_far = lax.ppermute(inner, "cam", inside_pairs)

time: 91.8 us -> 91.6 us (level)
  no operation moved by 1% of the time
where the time goes in v7:
time: 91.6 us; the launch traced here: 90.6 us
  blocking collectives  55.4 us (60%)
  Pallas kernels  18 us (20%)
  waiting for transfers between devices  12 us (13%)
  starting transfers between devices  2.9 us (3%)
  local copies, waits for them, and re-layouts  1.96 us (2%)
    all_to_all x2, blocking collectives, to_owners(): return lax.all_to_all(x, 'frame', split_axis=0, concat_axis=0, tiled=True)  55.4 us
    ppermute x1, waiting for transfers between devices, shards(): late_far = lax.ppermute(outer, 'cam', late_pairs)  10.8 us
    pallas_call x1, Pallas kernels, shards(): kernel_call(functools.partial(local_kernel, cameras), [SMEM, SMEM] + [VME...  8.07 us
    pallas_call x1, Pallas kernels, shards(): kernel_call(functools.partial(time_kernel, frames), [VMEM] * 2, [spread((...  3.9 us
    pallas_call x1, Pallas kernels, shards(): kernel_call(outer_kernel, [VMEM] * 9, [spread((token_count, model)), spre...  2.75 us
    pallas_call x1, Pallas kernels, shards(): kernel_call(final_kernel, [VMEM] * 4, [spread((rows, model))], [pltpu.VME...  1.99 us
    ppermute x1, starting transfers between devices, shards(): late_far = lax.ppermute(outer, 'cam', late_pairs)  1.98 us
    unnamed x20, local copies, waits for them, and re-layouts  1.96 us
  transfers between devices with their start and end apart: 3, of which 2 were waited for; matrix products, arithmetic and copies ran while one was open for 0% of the time, Pallas kernels for 9%

profile of v7, /device:TPU:22, one launch (start us, length us, event | category | flops | bytes accessed | tf_op | source)
XLA Modules:
  0.0 90.6 jit_solution(3054603306390432004)
XLA Ops:
  0.0 0.0 copy-start.3
  0.0 1.3 %copy-done.3 = bf16[2,1,256,1152]{3,2,1,0:T(8,128)(2,1)S(1)} copy-done((bf16[2,1,256,1152]{3,2,1,0:T(8,128)(2,1)S(1)}, bf16[2,1,256,1152]{3,2,1,0:T(8,128)(2,1)}, u32[]{:S(2)}) %copy-start.3) | copy-done | bytes 1179672
  1.3 0.0 copy-start.8
  1.3 0.7 copy-done.8
  1.9 0.0 copy-start
  1.9 0.0 copy-start.1
  1.9 0.0 copy-start.4
  1.9 0.0 copy-start.6
  1.9 0.0 copy-start.7
  1.9 0.0 copy-start.9
  2.0 1.3 %shard_map.82 = (bf16[65,4,1152]{2,1,0:T(4,128)(2,1)S(1)}, bf16[65,4,1152]{2,1,0:T(4,128)(2,1)S(1)}) custom-call(s32[1,2]{1,0:T(1,128)S(1)} %bitcast.13, bf16[512,1152]{1,0:T(8,128)(2,1)S(1)} %bitcast.9), custom_call_target="tpu_custom_call" | custom-call | flops 6000000000 | bytes 2400000 | tf_op jit(solution)/shard_map/pallas_call | solution.py:372
  3.3 0.1 collective-permute-start.1
  3.4 0.8 collective-permute-start
  4.2 1.2 %collective-permute-done.1.far_ref = bf16[65,4,1152]{2,1,0:T(4,128)(2,1)S(1)} collective-permute-done((bf16[65,4,1152]{2,1,0:T(4,128)(2,1)S(1)}, bf16[65,4,1152]{2,1,0:T(4,128)(2,1)S(1)}, u32[]{:S(2)}, u32[]{:S(2)}) %collective-permute-start.1) | collective-permute-done | bytes 599072 | tf_op jit(solution)/shard_map/ppermute | solution.py:376
  5.4 0.0 copy-done
  5.4 0.0 copy-done.1
  5.4 0.0 copy-done.4
  5.4 0.0 copy-done.6
  5.4 0.0 copy-done.7
  5.4 0.0 copy-done.9
  5.4 8.1 %shard_map.83 = (f32[576,512]{1,0:T(8,128)S(1)}, f32[8,80,256]{2,1,0:T(8,128)S(1)}, f32[8,640]{1,0:T(8,128)S(1)}, bf16[256,1152]{1,0:T(8,128)(2,1)S(1)}, bf16[32,2,4736]{2,1,0:T(2,128)(2,1)S(1)}) custom-call(s32[1,2]{1,0:T(1,128)S(1)} %bitcast.14, s32[2,2]{1,0:T(2,128)S(1)} %copy-done.7, bf16[65,4,1152]{2,1,0:T(4,128)(2,1)S(1)} %get-tuple-element.19.outer_ref, ...), custom_call_target="tpu_custom_call" | custom-call | flops 8000000000 | bytes 20000000 | tf_op jit(solution)/shard_map/pallas_call | solution.py:378
  13.5 2.0 %collective-permute-start.2 = (bf16[65,4,1152]{2,1,0:T(4,128)(2,1)S(1)}, bf16[65,4,1152]{2,1,0:T(4,128)(2,1)S(1)}, u32[]{:S(2)}, u32[]{:S(2)}) collective-permute-start(bf16[65,4,1152]{2,1,0:T(4,128)(2,1)S(1)} %get-tuple-element.19.outer_ref), channel_id=1, source_target_pairs={{64,128},{128,64},{65,129},{129,65},{66,130},{130,66},{67,131},{13... | collective-permute-start | bytes 1797128 | tf_op jit(solution)/shard_map/ppermute | solution.py:394
  15.5 0.0 collective-permute-done.early_ref
  15.5 10.8 %collective-permute-done.2.late_ref = bf16[65,4,1152]{2,1,0:T(4,128)(2,1)S(1)} collective-permute-done((bf16[65,4,1152]{2,1,0:T(4,128)(2,1)S(1)}, bf16[65,4,1152]{2,1,0:T(4,128)(2,1)S(1)}, u32[]{:S(2)}, u32[]{:S(2)}) %collective-permute-start.2) | collective-permute-done | bytes 599072 | tf_op jit(solution)/shard_map/ppermute | solution.py:394
  26.3 0.0 copy-start.5
  26.3 2.8 %shard_map.84 = (bf16[256,1152]{1,0:T(8,128)(2,1)S(1)}, bf16[64,2,4736]{2,1,0:T(2,128)(2,1)S(1)}) custom-call(bf16[65,4,1152]{2,1,0:T(4,128)(2,1)S(1)} %collective-permute-done.early_ref, bf16[65,4,1152]{2,1,0:T(4,128)(2,1)S(1)} %collective-permute-done.2.late_ref, bf16[1728,1152]{1,0:T(8,128)(2,1)S(1)} %bitcast.8, f32[8,640]{1,0:T(8,128)S(1)} %get-tuple-element.20.info_ref, ...), custom_call_target="tpu_custom_call" | custom-call | flops 2500000000 | bytes 8000000 | tf_op jit(solution)/shard_map/pallas_call | solution.py:395
  29.1 35.1 %all_to_all.10.payload_ref = bf16[64,2,4736]{2,1,0:T(2,128)(2,1)S(1)} all-to-all(bf16[64,2,4736]{2,1,0:T(2,128)(2,1)S(1)} %get-tuple-element.24), channel_id=1, replica_groups=mesh['cam'=4,'frame'=64] {'frame'}, dimensions={0} | all-to-all | bytes 2424832 | tf_op jit(solution)/shard_map/all_to_all | solution.py:26
  64.1 0.0 copy-done.5
  64.2 0.0 copy-start.2
  64.2 3.9 %shard_map.85 = bf16[64,2,2304]{2,1,0:T(2,128)(2,1)S(1)} custom-call(bf16[64,2,4736]{2,1,0:T(2,128)(2,1)S(1)} %all_to_all.10.payload_ref, bf16[1728,1152]{1,0:T(8,128)(2,1)S(1)} %bitcast.12), custom_call_target="tpu_custom_call" | custom-call | flops 6000000000 | bytes 10000000 | tf_op jit(solution)/shard_map/pallas_call | solution.py:406
  68.1 20.4 %all_to_all.11.attended_ref = bf16[64,2,2304]{2,1,0:T(2,128)(2,1)S(1)} all-to-all(bf16[64,2,2304]{2,1,0:T(2,128)(2,1)S(1)} %shard_map.85), channel_id=1, replica_groups=mesh['cam'=4,'frame'=64] {'frame'}, dimensions={0} | all-to-all | bytes 1179648 | tf_op jit(solution)/shard_map/all_to_all | solution.py:26
  88.4 0.0 copy-done.2
  88.4 2.0 %shard_map.86 = bf16[512,1152]{1,0:T(8,128)(2,1)} custom-call(bf16[64,2,2304]{2,1,0:T(2,128)(2,1)S(1)} %all_to_all.11.attended_ref, bf16[576,1152]{1,0:T(8,128)(2,1)S(1)} %copy-done.2, bf16[256,1152]{1,0:T(8,128)(2,1)S(1)} %get-tuple-element.25.outer_ref, bf16[256,1152]{1,0:T(8,128)(2,1)S(1)} %get-tuple-element.26.inner_ref), custom_call_target="tpu_custom_call" | custom-call | flops 700000000 | bytes 4000000 | tf_op jit(solution)/shard_map/pallas_call | solution.py:416
Async XLA Ops:
  0.0 1.3 %copy-start.3 = (bf16[2,1,256,1152]{3,2,1,0:T(8,128)(2,1)S(1)}, bf16[2,1,256,1152]{3,2,1,0:T(8,128)(2,1)}, u32[]{:S(2)}) copy-start(bf16[2,1,256,1152]{3,2,1,0:T(8,128)(2,1)} %param.8) | copy-start | bytes 3538948
  1.3 0.7 copy-start.8
  1.9 3.5 %copy-start = (bf16[1152,1728]{0,1:T(8,128)(2,1)S(1)}, bf16[1152,1728]{0,1:T(8,128)(2,1)}, u32[]{:S(2)}) copy-start(bf16[1152,1728]{0,1:T(8,128)(2,1)} %param.12) | copy-start | bytes 11943940
  1.9 3.5 %copy-start.1 = (bf16[576,1152]{1,0:T(8,128)(2,1)S(1)}, bf16[576,1152]{1,0:T(8,128)(2,1)}, u32[]{:S(2)}) copy-start(bf16[576,1152]{1,0:T(8,128)(2,1)} %out_weight_ref.3) | copy-start | bytes 3981316
  1.9 3.5 %copy-start.4 = (bf16[2,1,256,1152]{3,2,1,0:T(8,128)(2,1)S(1)}, bf16[2,1,256,1152]{3,2,1,0:T(8,128)(2,1)}, u32[]{:S(2)}) copy-start(bf16[2,1,256,1152]{3,2,1,0:T(8,128)(2,1)} %param.8) | copy-start | bytes 3538948
  1.9 3.5 %copy-start.6 = (bf16[2,576]{1,0:T(2,128)(2,1)S(1)}, bf16[2,576]{1,0:T(2,128)(2,1)}, u32[]{:S(2)}) copy-start(bf16[2,576]{1,0:T(2,128)(2,1)} %side_ref.1) | copy-start | bytes 6916
  1.9 3.5 %copy-start.7 = (s32[2,2]{1,0:T(2,128)S(1)}, s32[2,2]{1,0:T(2,128)}, u32[]{:S(2)}) copy-start(s32[2,2]{1,0:T(2,128)} %neighbours_ref.1) | copy-start | bytes 52
  1.9 3.5 %copy-start.9 = (s32[2,1]{0,1:T(1,128)S(1)}, s32[2,1]{0,1:T(1,128)}, u32[]{:S(2)}) copy-start(s32[2,1]{0,1:T(1,128)} %param.9) | copy-start | bytes 28
  3.3 2.1 %collective-permute-start.1 = (bf16[65,4,1152]{2,1,0:T(4,128)(2,1)S(1)}, bf16[65,4,1152]{2,1,0:T(4,128)(2,1)S(1)}, u32[]{:S(2)}, u32[]{:S(2)}) collective-permute-start(bf16[65,4,1152]{2,1,0:T(4,128)(2,1)S(1)} %get-tuple-element.17.inner_ref), channel_id=1, source_target_pairs={{0,64},{64,0},{128,192},{192,128},{1,65},{65,1},{129,193},{193,129... | collective-permute-start | bytes 1797128 | tf_op jit(solution)/shard_map/ppermute | solution.py:376
  3.4 12.1 %collective-permute-start = (bf16[65,4,1152]{2,1,0:T(4,128)(2,1)S(1)}, bf16[65,4,1152]{2,1,0:T(4,128)(2,1)S(1)}, u32[]{:S(2)}, u32[]{:S(2)}) collective-permute-start(bf16[65,4,1152]{2,1,0:T(4,128)(2,1)S(1)} %get-tuple-element.19.outer_ref), channel_id=1, source_target_pairs={{192,0},{0,192},{193,1},{1,193},{194,2},{2,194},{195,3},{3,195},{1... | collective-permute-start | bytes 1797128 | tf_op jit(solution)/shard_map/ppermute | solution.py:375
  13.5 12.8 %collective-permute-start.2 = (bf16[65,4,1152]{2,1,0:T(4,128)(2,1)S(1)}, bf16[65,4,1152]{2,1,0:T(4,128)(2,1)S(1)}, u32[]{:S(2)}, u32[]{:S(2)}) collective-permute-start(bf16[65,4,1152]{2,1,0:T(4,128)(2,1)S(1)} %get-tuple-element.19.outer_ref), channel_id=1, source_target_pairs={{64,128},{128,64},{65,129},{129,65},{66,130},{130,66},{67,131},{13... | collective-permute-start | bytes 1797128 | tf_op jit(solution)/shard_map/ppermute | solution.py:394
  26.3 37.8 %copy-start.5 = (bf16[1152,1728]{0,1:T(8,128)(2,1)S(1)}, bf16[1152,1728]{0,1:T(8,128)(2,1)}, u32[]{:S(2)}) copy-start(bf16[1152,1728]{0,1:T(8,128)(2,1)} %param.14) | copy-start | bytes 11943940
  64.2 24.3 %copy-start.2 = (bf16[576,1152]{1,0:T(8,128)(2,1)S(1)}, bf16[576,1152]{1,0:T(8,128)(2,1)}, u32[]{:S(2)}) copy-start(bf16[576,1152]{1,0:T(8,128)(2,1)} %weight_ref.1) | copy-start | bytes 3981316

commit v8 on v7

--- a/solution.py
+++ b/solution.py
@@ -35,13 +35,13 @@
     for i in range(0, peers, 2):
         inside += [(i, i + 1), (i + 1, i)]
         last = (i + peers - 1) % peers
-        (late if (i // 2) % 2 else early).extend([(last, i), (i, last)])
+        (early if (i // 2) % 2 else late).extend([(last, i), (i, last)])
     return inside, early, late
 
 
 def is_early():
     peers = lax.axis_size("cam")
-    return lax.rem(lax.rem(lax.axis_index("cam") + 1, peers) // 2, 2) == 0
+    return lax.rem(lax.rem(lax.axis_index("cam") + 1, peers) // 2, 2) == 1
 
 
 def dot_nt(a, b):

time: 91.6 us -> 91.1 us (level)
  the two profiles are of different devices: /device:TPU:22 before, /device:TPU:6 now
where the time goes in v8:
time: 91.1 us; the launch traced here: 90.9 us
  blocking collectives  55.8 us (61%)
  Pallas kernels  18 us (20%)
  waiting for transfers between devices  9.12 us (10%)
  starting transfers between devices  5.76 us (6%)
  local copies, waits for them, and re-layouts  1.96 us (2%)
    all_to_all x2, blocking collectives, to_owners(): return lax.all_to_all(x, 'frame', split_axis=0, concat_axis=0, tiled=True)  55.8 us
    pallas_call x1, Pallas kernels, shards(): kernel_call(functools.partial(local_kernel, cameras), [SMEM, SMEM] + [VME...  8.07 us
    ppermute x1, waiting for transfers between devices, shards(): late_far = lax.ppermute(outer, 'cam', late_pairs)  7.95 us
    ppermute x1, starting transfers between devices, shards(): late_far = lax.ppermute(outer, 'cam', late_pairs)  4.84 us
    pallas_call x1, Pallas kernels, shards(): kernel_call(functools.partial(time_kernel, frames), [VMEM] * 2, [spread((...  3.89 us
    pallas_call x1, Pallas kernels, shards(): kernel_call(outer_kernel, [VMEM] * 9, [spread((token_count, model)), spre...  2.75 us
    pallas_call x1, Pallas kernels, shards(): kernel_call(final_kernel, [VMEM] * 4, [spread((rows, model))], [pltpu.VME...  1.99 us
    unnamed x20, local copies, waits for them, and re-layouts  1.96 us
  transfers between devices with their start and end apart: 3, of which 2 were waited for; matrix products, arithmetic and copies ran while one was open for 0% of the time, Pallas kernels for 9%

profile of v8, /device:TPU:6, one launch (start us, length us, event | category | flops | bytes accessed | tf_op | source)
XLA Modules:
  0.0 90.9 jit_solution(18412991916908384948)
XLA Ops:
  0.0 0.0 copy-start.3
  0.0 1.3 %copy-done.3 = bf16[2,1,256,1152]{3,2,1,0:T(8,128)(2,1)S(1)} copy-done((bf16[2,1,256,1152]{3,2,1,0:T(8,128)(2,1)S(1)}, bf16[2,1,256,1152]{3,2,1,0:T(8,128)(2,1)}, u32[]{:S(2)}) %copy-start.3) | copy-done | bytes 1179672
  1.3 0.0 copy-start.8
  1.3 0.7 copy-done.8
  1.9 0.0 copy-start
  1.9 0.0 copy-start.1
  1.9 0.0 copy-start.4
  1.9 0.0 copy-start.6
  1.9 0.0 copy-start.7
  1.9 0.0 copy-start.9
  2.0 1.3 %shard_map.82 = (bf16[65,4,1152]{2,1,0:T(4,128)(2,1)S(1)}, bf16[65,4,1152]{2,1,0:T(4,128)(2,1)S(1)}) custom-call(s32[1,2]{1,0:T(1,128)S(1)} %bitcast.13, bf16[512,1152]{1,0:T(8,128)(2,1)S(1)} %bitcast.9), custom_call_target="tpu_custom_call" | custom-call | flops 6000000000 | bytes 2400000 | tf_op jit(solution)/shard_map/pallas_call | solution.py:372
  3.3 0.1 collective-permute-start.1
  3.4 0.8 collective-permute-start
  4.2 1.2 %collective-permute-done.1.far_ref = bf16[65,4,1152]{2,1,0:T(4,128)(2,1)S(1)} collective-permute-done((bf16[65,4,1152]{2,1,0:T(4,128)(2,1)S(1)}, bf16[65,4,1152]{2,1,0:T(4,128)(2,1)S(1)}, u32[]{:S(2)}, u32[]{:S(2)}) %collective-permute-start.1) | collective-permute-done | bytes 599072 | tf_op jit(solution)/shard_map/ppermute | solution.py:376
  5.4 0.0 copy-done
  5.4 0.0 copy-done.1
  5.4 0.0 copy-done.4
  5.4 0.0 copy-done.6
  5.4 0.0 copy-done.7
  5.4 0.0 copy-done.9
  5.4 8.1 %shard_map.83 = (f32[576,512]{1,0:T(8,128)S(1)}, f32[8,80,256]{2,1,0:T(8,128)S(1)}, f32[8,640]{1,0:T(8,128)S(1)}, bf16[256,1152]{1,0:T(8,128)(2,1)S(1)}, bf16[32,2,4736]{2,1,0:T(2,128)(2,1)S(1)}) custom-call(s32[1,2]{1,0:T(1,128)S(1)} %bitcast.14, s32[2,2]{1,0:T(2,128)S(1)} %copy-done.7, bf16[65,4,1152]{2,1,0:T(4,128)(2,1)S(1)} %get-tuple-element.19.outer_ref, ...), custom_call_target="tpu_custom_call" | custom-call | flops 8000000000 | bytes 20000000 | tf_op jit(solution)/shard_map/pallas_call | solution.py:378
  13.5 4.8 %collective-permute-start.2 = (bf16[65,4,1152]{2,1,0:T(4,128)(2,1)S(1)}, bf16[65,4,1152]{2,1,0:T(4,128)(2,1)S(1)}, u32[]{:S(2)}, u32[]{:S(2)}) collective-permute-start(bf16[65,4,1152]{2,1,0:T(4,128)(2,1)S(1)} %get-tuple-element.19.outer_ref), channel_id=1, source_target_pairs={{192,0},{0,192},{193,1},{1,193},{194,2},{2,194},{195,3},{3,195},{1... | collective-permute-start | bytes 1797128 | tf_op jit(solution)/shard_map/ppermute | solution.py:394
  18.4 0.0 collective-permute-done.early_ref
  18.4 7.9 %collective-permute-done.2.late_ref = bf16[65,4,1152]{2,1,0:T(4,128)(2,1)S(1)} collective-permute-done((bf16[65,4,1152]{2,1,0:T(4,128)(2,1)S(1)}, bf16[65,4,1152]{2,1,0:T(4,128)(2,1)S(1)}, u32[]{:S(2)}, u32[]{:S(2)}) %collective-permute-start.2) | collective-permute-done | bytes 599072 | tf_op jit(solution)/shard_map/ppermute | solution.py:394
  26.3 0.0 copy-start.5
  26.3 2.7 %shard_map.84 = (bf16[256,1152]{1,0:T(8,128)(2,1)S(1)}, bf16[64,2,4736]{2,1,0:T(2,128)(2,1)S(1)}) custom-call(bf16[65,4,1152]{2,1,0:T(4,128)(2,1)S(1)} %collective-permute-done.early_ref, bf16[65,4,1152]{2,1,0:T(4,128)(2,1)S(1)} %collective-permute-done.2.late_ref, bf16[1728,1152]{1,0:T(8,128)(2,1)S(1)} %bitcast.8, f32[8,640]{1,0:T(8,128)S(1)} %get-tuple-element.20.info_ref, ...), custom_call_target="tpu_custom_call" | custom-call | flops 2500000000 | bytes 8000000 | tf_op jit(solution)/shard_map/pallas_call | solution.py:395
  29.1 35.4 %all_to_all.10.payload_ref = bf16[64,2,4736]{2,1,0:T(2,128)(2,1)S(1)} all-to-all(bf16[64,2,4736]{2,1,0:T(2,128)(2,1)S(1)} %get-tuple-element.24), channel_id=1, replica_groups=mesh['cam'=4,'frame'=64] {'frame'}, dimensions={0} | all-to-all | bytes 2424832 | tf_op jit(solution)/shard_map/all_to_all | solution.py:26
  64.5 0.0 copy-done.5
  64.5 0.0 copy-start.2
  64.5 3.9 %shard_map.85 = bf16[64,2,2304]{2,1,0:T(2,128)(2,1)S(1)} custom-call(bf16[64,2,4736]{2,1,0:T(2,128)(2,1)S(1)} %all_to_all.10.payload_ref, bf16[1728,1152]{1,0:T(8,128)(2,1)S(1)} %bitcast.12), custom_call_target="tpu_custom_call" | custom-call | flops 6000000000 | bytes 10000000 | tf_op jit(solution)/shard_map/pallas_call | solution.py:406
  68.4 20.4 %all_to_all.11.attended_ref = bf16[64,2,2304]{2,1,0:T(2,128)(2,1)S(1)} all-to-all(bf16[64,2,2304]{2,1,0:T(2,128)(2,1)S(1)} %shard_map.85), channel_id=1, replica_groups=mesh['cam'=4,'frame'=64] {'frame'}, dimensions={0} | all-to-all | bytes 1179648 | tf_op jit(solution)/shard_map/all_to_all | solution.py:26
  88.8 0.0 copy-done.2
  88.8 2.0 %shard_map.86 = bf16[512,1152]{1,0:T(8,128)(2,1)} custom-call(bf16[64,2,2304]{2,1,0:T(2,128)(2,1)S(1)} %all_to_all.11.attended_ref, bf16[576,1152]{1,0:T(8,128)(2,1)S(1)} %copy-done.2, bf16[256,1152]{1,0:T(8,128)(2,1)S(1)} %get-tuple-element.25.outer_ref, bf16[256,1152]{1,0:T(8,128)(2,1)S(1)} %get-tuple-element.26.inner_ref), custom_call_target="tpu_custom_call" | custom-call | flops 700000000 | bytes 4000000 | tf_op jit(solution)/shard_map/pallas_call | solution.py:416
Async XLA Ops:
  0.0 1.3 %copy-start.3 = (bf16[2,1,256,1152]{3,2,1,0:T(8,128)(2,1)S(1)}, bf16[2,1,256,1152]{3,2,1,0:T(8,128)(2,1)}, u32[]{:S(2)}) copy-start(bf16[2,1,256,1152]{3,2,1,0:T(8,128)(2,1)} %param.8) | copy-start | bytes 3538948
  1.3 0.7 copy-start.8
  1.9 3.5 %copy-start = (bf16[1152,1728]{0,1:T(8,128)(2,1)S(1)}, bf16[1152,1728]{0,1:T(8,128)(2,1)}, u32[]{:S(2)}) copy-start(bf16[1152,1728]{0,1:T(8,128)(2,1)} %param.12) | copy-start | bytes 11943940
  1.9 3.5 %copy-start.1 = (bf16[576,1152]{1,0:T(8,128)(2,1)S(1)}, bf16[576,1152]{1,0:T(8,128)(2,1)}, u32[]{:S(2)}) copy-start(bf16[576,1152]{1,0:T(8,128)(2,1)} %out_weight_ref.3) | copy-start | bytes 3981316
  1.9 3.5 %copy-start.4 = (bf16[2,1,256,1152]{3,2,1,0:T(8,128)(2,1)S(1)}, bf16[2,1,256,1152]{3,2,1,0:T(8,128)(2,1)}, u32[]{:S(2)}) copy-start(bf16[2,1,256,1152]{3,2,1,0:T(8,128)(2,1)} %param.8) | copy-start | bytes 3538948
  1.9 3.5 %copy-start.6 = (bf16[2,576]{1,0:T(2,128)(2,1)S(1)}, bf16[2,576]{1,0:T(2,128)(2,1)}, u32[]{:S(2)}) copy-start(bf16[2,576]{1,0:T(2,128)(2,1)} %side_ref.1) | copy-start | bytes 6916
  1.9 3.5 %copy-start.7 = (s32[2,2]{1,0:T(2,128)S(1)}, s32[2,2]{1,0:T(2,128)}, u32[]{:S(2)}) copy-start(s32[2,2]{1,0:T(2,128)} %neighbours_ref.1) | copy-start | bytes 52
  1.9 3.5 %copy-start.9 = (s32[2,1]{0,1:T(1,128)S(1)}, s32[2,1]{0,1:T(1,128)}, u32[]{:S(2)}) copy-start(s32[2,1]{0,1:T(1,128)} %param.9) | copy-start | bytes 28
  3.3 2.1 %collective-permute-start.1 = (bf16[65,4,1152]{2,1,0:T(4,128)(2,1)S(1)}, bf16[65,4,1152]{2,1,0:T(4,128)(2,1)S(1)}, u32[]{:S(2)}, u32[]{:S(2)}) collective-permute-start(bf16[65,4,1152]{2,1,0:T(4,128)(2,1)S(1)} %get-tuple-element.17.inner_ref), channel_id=1, source_target_pairs={{0,64},{64,0},{128,192},{192,128},{1,65},{65,1},{129,193},{193,129... | collective-permute-start | bytes 1797128 | tf_op jit(solution)/shard_map/ppermute | solution.py:376
  3.4 15.0 %collective-permute-start = (bf16[65,4,1152]{2,1,0:T(4,128)(2,1)S(1)}, bf16[65,4,1152]{2,1,0:T(4,128)(2,1)S(1)}, u32[]{:S(2)}, u32[]{:S(2)}) collective-permute-start(bf16[65,4,1152]{2,1,0:T(4,128)(2,1)S(1)} %get-tuple-element.19.outer_ref), channel_id=1, source_target_pairs={{64,128},{128,64},{65,129},{129,65},{66,130},{130,66},{67,131},{13... | collective-permute-start | bytes 1797128 | tf_op jit(solution)/shard_map/ppermute | solution.py:375
  13.5 12.8 %collective-permute-start.2 = (bf16[65,4,1152]{2,1,0:T(4,128)(2,1)S(1)}, bf16[65,4,1152]{2,1,0:T(4,128)(2,1)S(1)}, u32[]{:S(2)}, u32[]{:S(2)}) collective-permute-start(bf16[65,4,1152]{2,1,0:T(4,128)(2,1)S(1)} %get-tuple-element.19.outer_ref), channel_id=1, source_target_pairs={{192,0},{0,192},{193,1},{1,193},{194,2},{2,194},{195,3},{3,195},{1... | collective-permute-start | bytes 1797128 | tf_op jit(solution)/shard_map/ppermute | solution.py:394
  26.3 38.2 %copy-start.5 = (bf16[1152,1728]{0,1:T(8,128)(2,1)S(1)}, bf16[1152,1728]{0,1:T(8,128)(2,1)}, u32[]{:S(2)}) copy-start(bf16[1152,1728]{0,1:T(8,128)(2,1)} %param.14) | copy-start | bytes 11943940
  64.5 24.3 %copy-start.2 = (bf16[576,1152]{1,0:T(8,128)(2,1)S(1)}, bf16[576,1152]{1,0:T(8,128)(2,1)}, u32[]{:S(2)}) copy-start(bf16[576,1152]{1,0:T(8,128)(2,1)} %weight_ref.1) | copy-start | bytes 3981316

commit v9 on v8

--- a/solution.py
+++ b/solution.py
@@ -214,10 +214,11 @@
             part_ref[h] = jnp.where(row == HEAD + 1, highest, summed)
         else:
             pieces.append(summed[:HEAD] * (1.0 / summed[HEAD : HEAD + 1]))
+            if h == HEADS - 1:
+                tokens = tokens_ref[camera_rows(1 - odd, rows), :]
+                write_finished(1, pieces, tokens, out_weight_ref, info_ref, mixed_ref, payload_ref)
 
     staggered([(i, h) for i in (1, 0) for h in range(HEADS)], score, rest, 8)
-    tokens = tokens_ref[camera_rows(1 - odd, rows), :]
-    write_finished(1, pieces, tokens, out_weight_ref, info_ref, mixed_ref, payload_ref)
 
 
 def outer_kernel(

time: 91.1 us -> 91.1 us (level)
  no operation moved by 1% of the time
where the time goes in v9:
time: 91.1 us; the launch traced here: 90.9 us
  blocking collectives  55.8 us (61%)
  Pallas kernels  18 us (20%)
  waiting for transfers between devices  9.12 us (10%)
  starting transfers between devices  5.76 us (6%)
  local copies, waits for them, and re-layouts  1.96 us (2%)
    all_to_all x2, blocking collectives, to_owners(): return lax.all_to_all(x, 'frame', split_axis=0, concat_axis=0, tiled=True)  55.8 us
    pallas_call x1, Pallas kernels, shards(): kernel_call(functools.partial(local_kernel, cameras), [SMEM, SMEM] + [VME...  8.04 us
    ppermute x1, waiting for transfers between devices, shards(): late_far = lax.ppermute(outer, 'cam', late_pairs)  7.95 us
    ppermute x1, starting transfers between devices, shards(): late_far = lax.ppermute(outer, 'cam', late_pairs)  4.84 us
    pallas_call x1, Pallas kernels, shards(): kernel_call(functools.partial(time_kernel, frames), [VMEM] * 2, [spread((...  3.9 us
    pallas_call x1, Pallas kernels, shards(): kernel_call(outer_kernel, [VMEM] * 9, [spread((token_count, model)), spre...  2.76 us
    pallas_call x1, Pallas kernels, shards(): kernel_call(final_kernel, [VMEM] * 4, [spread((rows, model))], [pltpu.VME...  1.99 us
    unnamed x20, local copies, waits for them, and re-layouts  1.96 us
  transfers between devices with their start and end apart: 3, of which 2 were waited for; matrix products, arithmetic and copies ran while one was open for 0% of the time, Pallas kernels for 9%

profile of v9, /device:TPU:6, one launch (start us, length us, event | category | flops | bytes accessed | tf_op | source)
XLA Modules:
  0.0 90.9 jit_solution(3074397715859448016)
XLA Ops:
  0.0 0.0 copy-start.3
  0.0 1.3 %copy-done.3 = bf16[2,1,256,1152]{3,2,1,0:T(8,128)(2,1)S(1)} copy-done((bf16[2,1,256,1152]{3,2,1,0:T(8,128)(2,1)S(1)}, bf16[2,1,256,1152]{3,2,1,0:T(8,128)(2,1)}, u32[]{:S(2)}) %copy-start.3) | copy-done | bytes 1179672
  1.3 0.0 copy-start.8
  1.3 0.7 copy-done.8
  1.9 0.0 copy-start
  1.9 0.0 copy-start.1
  1.9 0.0 copy-start.4
  1.9 0.0 copy-start.6
  1.9 0.0 copy-start.7
  1.9 0.0 copy-start.9
  2.0 1.3 %shard_map.82 = (bf16[65,4,1152]{2,1,0:T(4,128)(2,1)S(1)}, bf16[65,4,1152]{2,1,0:T(4,128)(2,1)S(1)}) custom-call(s32[1,2]{1,0:T(1,128)S(1)} %bitcast.13, bf16[512,1152]{1,0:T(8,128)(2,1)S(1)} %bitcast.9), custom_call_target="tpu_custom_call" | custom-call | flops 6000000000 | bytes 2400000 | tf_op jit(solution)/shard_map/pallas_call | solution.py:373
  3.3 0.1 collective-permute-start.1
  3.4 0.8 collective-permute-start
  4.2 1.2 %collective-permute-done.1.far_ref = bf16[65,4,1152]{2,1,0:T(4,128)(2,1)S(1)} collective-permute-done((bf16[65,4,1152]{2,1,0:T(4,128)(2,1)S(1)}, bf16[65,4,1152]{2,1,0:T(4,128)(2,1)S(1)}, u32[]{:S(2)}, u32[]{:S(2)}) %collective-permute-start.1) | collective-permute-done | bytes 599072 | tf_op jit(solution)/shard_map/ppermute | solution.py:377
  5.4 0.0 copy-done
  5.4 0.0 copy-done.1
  5.4 0.0 copy-done.4
  5.4 0.0 copy-done.6
  5.4 0.0 copy-done.7
  5.4 0.0 copy-done.9
  5.4 8.0 %shard_map.83 = (f32[576,512]{1,0:T(8,128)S(1)}, f32[8,80,256]{2,1,0:T(8,128)S(1)}, f32[8,640]{1,0:T(8,128)S(1)}, bf16[256,1152]{1,0:T(8,128)(2,1)S(1)}, bf16[32,2,4736]{2,1,0:T(2,128)(2,1)S(1)}) custom-call(s32[1,2]{1,0:T(1,128)S(1)} %bitcast.14, s32[2,2]{1,0:T(2,128)S(1)} %copy-done.7, bf16[65,4,1152]{2,1,0:T(4,128)(2,1)S(1)} %get-tuple-element.19.outer_ref, ...), custom_call_target="tpu_custom_call" | custom-call | flops 8000000000 | bytes 20000000 | tf_op jit(solution)/shard_map/pallas_call | solution.py:379
  13.5 4.8 %collective-permute-start.2 = (bf16[65,4,1152]{2,1,0:T(4,128)(2,1)S(1)}, bf16[65,4,1152]{2,1,0:T(4,128)(2,1)S(1)}, u32[]{:S(2)}, u32[]{:S(2)}) collective-permute-start(bf16[65,4,1152]{2,1,0:T(4,128)(2,1)S(1)} %get-tuple-element.19.outer_ref), channel_id=1, source_target_pairs={{192,0},{0,192},{193,1},{1,193},{194,2},{2,194},{195,3},{3,195},{1... | collective-permute-start | bytes 1797128 | tf_op jit(solution)/shard_map/ppermute | solution.py:395
  18.3 0.0 collective-permute-done.early_ref
  18.3 7.9 %collective-permute-done.2.late_ref = bf16[65,4,1152]{2,1,0:T(4,128)(2,1)S(1)} collective-permute-done((bf16[65,4,1152]{2,1,0:T(4,128)(2,1)S(1)}, bf16[65,4,1152]{2,1,0:T(4,128)(2,1)S(1)}, u32[]{:S(2)}, u32[]{:S(2)}) %collective-permute-start.2) | collective-permute-done | bytes 599072 | tf_op jit(solution)/shard_map/ppermute | solution.py:395
  26.3 0.0 copy-start.5
  26.3 2.8 %shard_map.84 = (bf16[256,1152]{1,0:T(8,128)(2,1)S(1)}, bf16[64,2,4736]{2,1,0:T(2,128)(2,1)S(1)}) custom-call(bf16[65,4,1152]{2,1,0:T(4,128)(2,1)S(1)} %collective-permute-done.early_ref, bf16[65,4,1152]{2,1,0:T(4,128)(2,1)S(1)} %collective-permute-done.2.late_ref, bf16[1728,1152]{1,0:T(8,128)(2,1)S(1)} %bitcast.8, f32[8,640]{1,0:T(8,128)S(1)} %get-tuple-element.20.info_ref, ...), custom_call_target="tpu_custom_call" | custom-call | flops 2500000000 | bytes 8000000 | tf_op jit(solution)/shard_map/pallas_call | solution.py:396
  29.1 35.4 %all_to_all.10.payload_ref = bf16[64,2,4736]{2,1,0:T(2,128)(2,1)S(1)} all-to-all(bf16[64,2,4736]{2,1,0:T(2,128)(2,1)S(1)} %get-tuple-element.24), channel_id=1, replica_groups=mesh['cam'=4,'frame'=64] {'frame'}, dimensions={0} | all-to-all | bytes 2424832 | tf_op jit(solution)/shard_map/all_to_all | solution.py:26
  64.5 0.0 copy-done.5
  64.5 0.0 copy-start.2
  64.5 3.9 %shard_map.85 = bf16[64,2,2304]{2,1,0:T(2,128)(2,1)S(1)} custom-call(bf16[64,2,4736]{2,1,0:T(2,128)(2,1)S(1)} %all_to_all.10.payload_ref, bf16[1728,1152]{1,0:T(8,128)(2,1)S(1)} %bitcast.12), custom_call_target="tpu_custom_call" | custom-call | flops 6000000000 | bytes 10000000 | tf_op jit(solution)/shard_map/pallas_call | solution.py:407
  68.4 20.4 %all_to_all.11.attended_ref = bf16[64,2,2304]{2,1,0:T(2,128)(2,1)S(1)} all-to-all(bf16[64,2,2304]{2,1,0:T(2,128)(2,1)S(1)} %shard_map.85), channel_id=1, replica_groups=mesh['cam'=4,'frame'=64] {'frame'}, dimensions={0} | all-to-all | bytes 1179648 | tf_op jit(solution)/shard_map/all_to_all | solution.py:26
  88.7 0.0 copy-done.2
  88.7 2.0 %shard_map.86 = bf16[512,1152]{1,0:T(8,128)(2,1)} custom-call(bf16[64,2,2304]{2,1,0:T(2,128)(2,1)S(1)} %all_to_all.11.attended_ref, bf16[576,1152]{1,0:T(8,128)(2,1)S(1)} %copy-done.2, bf16[256,1152]{1,0:T(8,128)(2,1)S(1)} %get-tuple-element.25.outer_ref, bf16[256,1152]{1,0:T(8,128)(2,1)S(1)} %get-tuple-element.26.inner_ref), custom_call_target="tpu_custom_call" | custom-call | flops 700000000 | bytes 4000000 | tf_op jit(solution)/shard_map/pallas_call | solution.py:417
Async XLA Ops:
  0.0 1.3 %copy-start.3 = (bf16[2,1,256,1152]{3,2,1,0:T(8,128)(2,1)S(1)}, bf16[2,1,256,1152]{3,2,1,0:T(8,128)(2,1)}, u32[]{:S(2)}) copy-start(bf16[2,1,256,1152]{3,2,1,0:T(8,128)(2,1)} %param.8) | copy-start | bytes 3538948
  1.3 0.7 copy-start.8
  1.9 3.5 %copy-start = (bf16[1152,1728]{0,1:T(8,128)(2,1)S(1)}, bf16[1152,1728]{0,1:T(8,128)(2,1)}, u32[]{:S(2)}) copy-start(bf16[1152,1728]{0,1:T(8,128)(2,1)} %param.12) | copy-start | bytes 11943940
  1.9 3.5 %copy-start.1 = (bf16[576,1152]{1,0:T(8,128)(2,1)S(1)}, bf16[576,1152]{1,0:T(8,128)(2,1)}, u32[]{:S(2)}) copy-start(bf16[576,1152]{1,0:T(8,128)(2,1)} %out_weight_ref.3) | copy-start | bytes 3981316
  1.9 3.5 %copy-start.4 = (bf16[2,1,256,1152]{3,2,1,0:T(8,128)(2,1)S(1)}, bf16[2,1,256,1152]{3,2,1,0:T(8,128)(2,1)}, u32[]{:S(2)}) copy-start(bf16[2,1,256,1152]{3,2,1,0:T(8,128)(2,1)} %param.8) | copy-start | bytes 3538948
  1.9 3.5 %copy-start.6 = (bf16[2,576]{1,0:T(2,128)(2,1)S(1)}, bf16[2,576]{1,0:T(2,128)(2,1)}, u32[]{:S(2)}) copy-start(bf16[2,576]{1,0:T(2,128)(2,1)} %side_ref.1) | copy-start | bytes 6916
  1.9 3.5 %copy-start.7 = (s32[2,2]{1,0:T(2,128)S(1)}, s32[2,2]{1,0:T(2,128)}, u32[]{:S(2)}) copy-start(s32[2,2]{1,0:T(2,128)} %neighbours_ref.1) | copy-start | bytes 52
  1.9 3.5 %copy-start.9 = (s32[2,1]{0,1:T(1,128)S(1)}, s32[2,1]{0,1:T(1,128)}, u32[]{:S(2)}) copy-start(s32[2,1]{0,1:T(1,128)} %param.9) | copy-start | bytes 28
  3.3 2.1 %collective-permute-start.1 = (bf16[65,4,1152]{2,1,0:T(4,128)(2,1)S(1)}, bf16[65,4,1152]{2,1,0:T(4,128)(2,1)S(1)}, u32[]{:S(2)}, u32[]{:S(2)}) collective-permute-start(bf16[65,4,1152]{2,1,0:T(4,128)(2,1)S(1)} %get-tuple-element.17.inner_ref), channel_id=1, source_target_pairs={{0,64},{64,0},{128,192},{192,128},{1,65},{65,1},{129,193},{193,129... | collective-permute-start | bytes 1797128 | tf_op jit(solution)/shard_map/ppermute | solution.py:377
  3.4 14.9 %collective-permute-start = (bf16[65,4,1152]{2,1,0:T(4,128)(2,1)S(1)}, bf16[65,4,1152]{2,1,0:T(4,128)(2,1)S(1)}, u32[]{:S(2)}, u32[]{:S(2)}) collective-permute-start(bf16[65,4,1152]{2,1,0:T(4,128)(2,1)S(1)} %get-tuple-element.19.outer_ref), channel_id=1, source_target_pairs={{64,128},{128,64},{65,129},{129,65},{66,130},{130,66},{67,131},{13... | collective-permute-start | bytes 1797128 | tf_op jit(solution)/shard_map/ppermute | solution.py:376
  13.5 12.8 %collective-permute-start.2 = (bf16[65,4,1152]{2,1,0:T(4,128)(2,1)S(1)}, bf16[65,4,1152]{2,1,0:T(4,128)(2,1)S(1)}, u32[]{:S(2)}, u32[]{:S(2)}) collective-permute-start(bf16[65,4,1152]{2,1,0:T(4,128)(2,1)S(1)} %get-tuple-element.19.outer_ref), channel_id=1, source_target_pairs={{192,0},{0,192},{193,1},{1,193},{194,2},{2,194},{195,3},{3,195},{1... | collective-permute-start | bytes 1797128 | tf_op jit(solution)/shard_map/ppermute | solution.py:395
  26.3 38.2 %copy-start.5 = (bf16[1152,1728]{0,1:T(8,128)(2,1)S(1)}, bf16[1152,1728]{0,1:T(8,128)(2,1)}, u32[]{:S(2)}) copy-start(bf16[1152,1728]{0,1:T(8,128)(2,1)} %param.14) | copy-start | bytes 11943940
  64.5 24.3 %copy-start.2 = (bf16[576,1152]{1,0:T(8,128)(2,1)S(1)}, bf16[576,1152]{1,0:T(8,128)(2,1)}, u32[]{:S(2)}) copy-start(bf16[576,1152]{1,0:T(8,128)(2,1)} %weight_ref.1) | copy-start | bytes 3981316
